TPU v7x, 128 devices: a whole 4x4x4 slice. The times are simulated.
128 devices in a mesh: tok: 4 (over y_hi, core), wt: 32 (over x, z, y_lo).
Axes of the slice: x: 4, y: 4 (y_hi: 2, y_lo: 2; y = y_hi * 2 + y_lo), z: 4, core: 2. Of those that a mesh axis runs over, the one named last changes fastest.
Arguments:
- activations: bfloat16 [1536, 8192], P('tok', 'wt'), may hold values from -6 to 6
- gate_pre: bfloat16 [1536, 16384], P('tok', 'wt'), may hold values from -6 to 6
- up_pre: bfloat16 [1536, 16384], P('tok', 'wt'), may hold values from -6 to 6
- hidden_grad: bfloat16 [1536, 16384], P('tok', 'wt'), may hold values from -0.59765625 to 0.59765625
- gate_blocks: bfloat16 [4096, 128, 128], P('wt'), may hold values from -0.125 to 0.125
- up_blocks: bfloat16 [4096, 128, 128], P('wt'), may hold values from -0.125 to 0.125
- block_rows: int32 [4096], P('wt'), may hold values from 0 to 127, as said below
- block_cols: int32 [4096], P('wt'), may hold values from 0 to 63, as said below
- block_count: int32 [32], P('wt'), may hold values from 32 to 128, as said below
Outputs:
- input_grad: bfloat16 [1536, 8192], P('tok', 'wt')
- gate_weight_grad: bfloat16 [4096, 128, 128], P('wt')
- up_weight_grad: bfloat16 [4096, 128, 128], P('wt')
Inputs may be any that keep to these rules, and one draw needn't show every extreme that they name: `block_rows`: slots of wt index w are w * 128 to (w + 1) * 128 - 1; their block rows lie in w * 4 to (w + 1) * 4 - 1; slots past the count repeat the owner's first slot. `block_cols`: the live slots of one owner name distinct blocks. `block_count`: one owner holds exactly 128 kept blocks.
All inputs are finite; a program needn't handle non-finite values.
Results may differ from a plain program's by a relative error of at most 0.025.
Values may be sent and summed in bfloat16 or wider, within the bound.
No kernel may reach another device: no remote copies, remote signals or barrier semaphores. Data moves between devices by JAX's collectives and lax.ppermute only.
A program may use at most 192 MiB of HBM per device.

v0:
```python
import functools

import jax
import jax.numpy as jnp
from jax import lax
from jax.experimental import pallas as pl
from jax.experimental.pallas import tpu as pltpu
from jax.sharding import Mesh
from jax.sharding import PartitionSpec as P

BF = jnp.bfloat16
F32 = jnp.float32
AXES = {"x": ("c", "x"), "z": ("c", "z"), "y": ("yh", "c", "yl")}
SIZES = {"yh": 2, "c": 2, "x": 4, "z": 4, "yl": 2}
TOK = 384
SLOTS = 128
PAIRS = 82


def shift(value, axis, step):
    pairs = []
    if axis in ("yh", "c", "yl"):
        return lax.ppermute(value, axis, [(0, 1), (1, 0)])
    if axis == "y":
        for yh in range(2):
            for c in range(2):
                for yl in range(2):
                    y = (yh * 2 + yl + (step if c == 0 else -step)) % 4
                    pairs.append(((yh * 2 + c) * 2 + yl, ((y // 2) * 2 + c) * 2 + y % 2))
    else:
        for c in range(2):
            for a in range(4):
                b = (a + (step if c == 0 else -step)) % 4
                pairs.append((c * 4 + a, c * 4 + b))
    return lax.ppermute(value, AXES[axis], pairs)


def add(a, b):
    return (a.astype(F32) + b.astype(F32)).astype(BF)


def sum_of(a, b, c):
    return (a.astype(F32) + b.astype(F32) + c.astype(F32)).astype(BF)


def gates_kernel(gate_ref, up_ref, hid_ref, gu, gut):
    g = gate_ref[...].astype(F32)
    u = up_ref[...].astype(F32)
    h = hid_ref[...].astype(F32)
    sig = 1.0 / (1.0 + jnp.exp(-g))
    gg = h * u * sig * (1.0 + g * (1.0 - sig))
    ug = h * g * sig
    gu[:, :128] = gg.astype(BF)
    gu[:, 128:] = ug.astype(BF)
    gut[:128, :] = gg.T.astype(BF)
    gut[128:, :] = ug.T.astype(BF)


def chunk_kernel(k, tab, order, gu, wg, wu, out):
    @pl.loop(0, 8)
    def _(j):
        base = order[k * 8 + j]
        total = jnp.zeros((TOK, 256), F32)
        for r in range(4):
            sides = []
            for side in range(2):
                slot = tab[r * 64 + base + side]
                index = jnp.minimum(slot, SLOTS - 1)
                block = jnp.concatenate([wg[index], wu[index]], axis=0)
                sides.append(jnp.where(slot < SLOTS, block, jnp.zeros_like(block)))
            both = jnp.concatenate(sides, axis=1)
            total += jnp.dot(gu[:, r * 256 : (r + 1) * 256], both, preferred_element_type=F32)
        out[j] = total.astype(BF)


PIECE = jax.ShapeDtypeStruct((8, TOK, 256), BF)
VM = pl.BlockSpec(memory_space=pltpu.VMEM)
SM = pl.BlockSpec(memory_space=pltpu.SMEM)
ANY = pl.BlockSpec(memory_space=pl.ANY)


def gates(gate_pre, up_pre, hidden):
    return pl.pallas_call(
        gates_kernel,
        out_shape=[jax.ShapeDtypeStruct((TOK, 1024), BF), jax.ShapeDtypeStruct((1024, TOK), BF)],
        grid=(4,),
        in_specs=[pl.BlockSpec((TOK, 128), lambda r: (0, r))] * 3,
        out_specs=[pl.BlockSpec((TOK, 256), lambda r: (0, r)), pl.BlockSpec((256, TOK), lambda r: (r, 0))],
        compiler_params=pltpu.CompilerParams(vmem_limit_bytes=16 * 1024 * 1024),
        cost_estimate=pl.CostEstimate(flops=1, bytes_accessed=1, transcendentals=0),
        name="gates",
    )(gate_pre, up_pre, hidden)


def terms(k, tab, order, gu, wg, wu):
    return pl.pallas_call(
        functools.partial(chunk_kernel, k),
        out_shape=PIECE,
        in_specs=[SM] * 2 + [VM] * 3,
        out_specs=VM,
        compiler_params=pltpu.CompilerParams(vmem_limit_bytes=8 * 1024 * 1024),
        cost_estimate=pl.CostEstimate(flops=1, bytes_accessed=1, transcendentals=0),
        name="terms",
    )(tab, order, gu, wg, wu)


def put(block, grads, slot, sem):
    pltpu.make_async_copy(block, grads.at[slot], sem).start()


def finish(copies, zero, grads, sem):
    @pl.loop(0, copies)
    def _(_):
        pltpu.make_async_copy(zero, grads.at[0], sem).wait()


def same_row_pairs(kind, origin, refs, groups, lrow, lslot, ltile, meta, gt, gate, up, gbuf, ubuf, sem):
    @pl.loop(meta[kind], meta[kind + 1])
    def _(step):
        for pair in range(2):
            pos = step * 4 + pair * 2
            rows = pl.ds(pl.multiple_of(lrow[pos] * 256, 256), 256)
            left = jnp.concatenate([gt[g, rows, :] for g in groups], axis=1)
            sides = []
            for side in range(2):
                tiles = [ref[ltile[(pos + side) * 4 + n]] for n, ref in enumerate(refs)]
                sides.append(jnp.concatenate(tiles, axis=0))
            total = jnp.dot(left, jnp.concatenate(sides, axis=1), preferred_element_type=F32).astype(BF)
            for side in range(2):
                gbuf[pos + side - origin] = total[:128, side * 128 : side * 128 + 128]
                ubuf[pos + side - origin] = total[128:, side * 128 : side * 128 + 128]
        for n in range(4):
            pos = step * 4 + n

            @pl.when(lslot[pos] < SLOTS)
            def _():
                put(gbuf.at[pos - origin], gate, lslot[pos], sem)
                put(ubuf.at[pos - origin], up, lslot[pos], sem)


def kinds_kernel(kinds, held, lrow, lslot, ltile, meta, gt, *rest):
    pieces, (gate, up, gbuf, ubuf, zero, sem) = rest[: len(rest) - 6 - held], rest[-6:]
    origin = meta[kinds[0][0]] * 4
    if not held:
        zero[...] = jnp.zeros((128, 128), BF)

        @pl.loop(meta[8], SLOTS)
        def _(s):
            put(zero, gate, s, sem)
            put(zero, up, s, sem)

        finish(2 * (SLOTS - meta[8]), zero, gate, sem)
    for kind, picks in kinds:
        refs = [pieces[n] for n in picks]
        flip = meta[7]
        groups = (flip, 1 - flip, 3 - flip, 2 + flip) if kind == 3 else (0, 1, 2, 3)
        same_row_pairs(kind, origin, refs, groups, lrow, lslot, ltile, meta, gt, gate, up, gbuf, ubuf, sem)
    finish(2 * (meta[9 + kinds[-1][0] + 1] - meta[9 + kinds[0][0]]), zero, gate, sem)


def weight_grads(name, kinds, room, lists, gt, pieces, held=()):
    grads = jax.ShapeDtypeStruct((SLOTS, 128, 128), BF)
    first = 5 + len(pieces)
    return pl.pallas_call(
        functools.partial(kinds_kernel, kinds, len(held)),
        out_shape=[grads] * 2,
        in_specs=[SM] * 4 + [VM] * (1 + len(pieces)) + [ANY] * len(held),
        out_specs=[ANY] * 2,
        scratch_shapes=[
            pltpu.VMEM((room, 128, 128), BF),
            pltpu.VMEM((room, 128, 128), BF),
            pltpu.VMEM((128, 128), BF),
            pltpu.SemaphoreType.DMA,
        ],
        input_output_aliases={first + n: n for n in range(len(held))},
        compiler_params=pltpu.CompilerParams(vmem_limit_bytes=25 * 1024 * 1024),
        cost_estimate=pl.CostEstimate(flops=1, bytes_accessed=1, transcendentals=0),
        name=name,
    )(*lists, gt, *pieces, *held)


def block_table(block_rows, block_cols, block_count):
    i32 = jnp.int32
    x, z, yl = lax.axis_index("x"), lax.axis_index("z"), lax.axis_index("yl")
    sign = 1 - 2 * lax.axis_index("c")
    slots = jnp.arange(SLOTS, dtype=i32)
    key = jnp.where(slots < block_count[0], block_rows % 4 * 64 + block_cols, -1)
    hit = key[None, :] == jnp.arange(256, dtype=i32)[:, None]
    tab = jnp.min(jnp.where(hit, slots[None, :], SLOTS), axis=1)
    k = jnp.arange(4, dtype=i32)
    xs = (x - sign * k) % 4
    zs = (z - sign * k) % 4
    ys = yl ^ jnp.arange(2, dtype=i32)
    order = (((xs[:, None, None] * 4 + zs[None, :, None]) * 2 + ys[None, None, :]) * 2).reshape(32)
    return tab, order


def slot_lists(block_rows, block_cols, block_count):
    i32 = jnp.int32
    x, z = lax.axis_index("x"), lax.axis_index("z")
    yh, yl = lax.axis_index("yh"), lax.axis_index("yl")
    sign = 1 - 2 * lax.axis_index("c")
    slots = jnp.arange(SLOTS, dtype=i32)
    live = slots < block_count[0]
    row = block_rows % 4
    col = block_cols
    near = (sign * (z - (col >> 2))) % 4
    odd_kind = jnp.where(near == 0, 0, jnp.where(near == 3, 1, jnp.where(near == 1, 2, 5)))
    even_kind = jnp.where(((col >> 1) & 1) == yl, 4, 3)
    kind = jnp.where((col & 1) == 0, even_kind, odd_kind)
    group = kind * 4 + row
    same = (group[:, None] == group[None, :]) & live[None, :]
    rank = jnp.sum(jnp.where(same & (slots[None, :] < slots[:, None]), 1, 0), axis=1)
    groups = jnp.arange(24, dtype=i32)
    count = jnp.sum(jnp.where((group[None, :] == groups[:, None]) & live[None, :], 1, 0), axis=1)
    npair = (count + 1) // 2
    kinds = jnp.arange(6, dtype=i32)
    steps = (jnp.sum(npair.reshape(6, 4), axis=1) + 1) // 2
    edges = jnp.arange(7, dtype=i32)
    before = kinds[None, :] < edges[:, None]
    bounds = jnp.sum(jnp.where(before, steps[None, :], 0), axis=1)
    lives = jnp.sum(jnp.where(before, jnp.sum(count.reshape(6, 4), axis=1)[None, :], 0), axis=1)
    start = jnp.sum(jnp.where(kinds[None, :] < kind[:, None], 2 * steps[None, :], 0), axis=1) + jnp.sum(
        jnp.where((groups[None, :] < group[:, None]) & (groups[None, :] // 4 == kind[:, None]), npair[None, :], 0),
        axis=1,
    )
    place = jnp.where(live, start * 2 + rank, -1)
    at = place[None, :] == jnp.arange(2 * PAIRS, dtype=i32)[:, None]
    lslot = jnp.min(jnp.where(at, slots[None, :], SLOTS), axis=1)
    lrow = jnp.sum(jnp.where(at, row[None, :], 0), axis=1)
    lcol = jnp.sum(jnp.where(at, col[None, :], 0), axis=1)
    cx, cz, cy, par = lcol >> 4, (lcol >> 2) & 3, (lcol >> 1) & 1, lcol & 1
    tiles = []
    for way in (sign, -sign):
        kx = (way * (x - cx)) % 4
        kz = (way * (z - cz)) % 4
        for j in range(2):
            ky = (way * ((yh * 2 + yl) - ((yh ^ j) * 2 + cy))) % 4
            tiles.append(jnp.where(par == 0, kz, ky) * 4 + kx)
    ltile = jnp.stack(tiles, axis=1).reshape(-1)
    flip = jnp.where((yl == 1) == (sign == 1), 0, 1).astype(i32)
    meta = jnp.concatenate([bounds, flip[None], block_count, lives]).astype(i32)
    return lrow, lslot, ltile, meta


def after(value, *others):
    return lax.optimization_barrier((value, *others))[0]


def body(
    activations, gate_pre, up_pre, hidden_grad, gate_blocks, up_blocks, block_rows, block_cols, block_count,
):
    tab, order = block_table(block_rows, block_cols, block_count)
    blocks = (gate_blocks, up_blocks)
    gu, gut = gates(gate_pre, up_pre, hidden_grad)
    other = shift(gut, "yh", 1)
    both = after(jnp.stack([activations[:, :128], activations[:, 128:]]), gut)
    near = [both] + [shift(both, "x", k) for k in (1, 2, 3)]
    t2 = terms(2, tab, order, gu, *blocks)
    ahead = shift(t2, "x", 1)
    even = after(jnp.stack([v[0] for v in near]), t2)
    odd = after(jnp.stack([v[1] for v in near]), t2, other)
    evens, odds = [even], [odd]
    evens.append(shift(even, "z", 1))
    odds.append(shift(odd, "y", 1))
    t1 = terms(1, tab, order, after(gu, even, odd), *blocks)
    back = shift(t1, "x", -1)
    evens.append(shift(after(evens[1], t1), "z", 1))
    odds.append(shift(after(odds[1], t1), "y", 1))
    t3 = terms(3, tab, order, after(gu, evens[1], odds[1]), *blocks)
    evens.append(shift(after(evens[2], t3), "z", 1))
    odds.append(shift(after(odds[2], t3), "y", 1))
    t0 = terms(0, tab, order, after(gu, evens[2], odds[2]), *blocks)
    moving = add(ahead, t3)
    even_0 = after(jnp.concatenate(evens), t0, moving)
    odd_0 = after(jnp.concatenate(odds), t0, moving)
    even_1, even_3 = shift(even_0, "y", 1), shift(even_0, "y", -1)
    odd_1, odd_3 = shift(odd_0, "z", 1), shift(odd_0, "z", -1)
    ahead = shift(moving, "x", 1)
    rows_late, cols_late, count_late = (after(v, even_0, odd_0) for v in (block_rows, block_cols, block_count))
    lrow, lslot, ltile, meta = slot_lists(rows_late, cols_late, count_late)
    mine = sum_of(t0, ahead, back).reshape(4, 2, TOK, 256)
    own = after(jnp.stack([gut, other]), mine)
    gt = jnp.concatenate([own, shift(own, "c", 1)])
    odd_0c = shift(after(odd_0, mine), "c", 1)

    def grads_of(name, kinds, room, pieces, held=(), wait=()):
        return weight_grads(name, kinds, room, (lrow, lslot, ltile, after(meta, *wait)), gt, pieces, held)

    even_2 = shift(after(even_1, even_3), "y", 1)
    odd_2 = shift(after(odd_1, odd_3), "z", 1)
    odd_1c, odd_3c = shift(odd_1, "c", 1), shift(odd_3, "c", 1)
    even_1c, even_3c = shift(after(even_1, odd_1c), "c", 1), shift(after(even_3, odd_1c), "c", 1)
    grads = grads_of(
        "grads_0_1_2",
        ((0, (0, 0, 1, 1)), (1, (3, 3, 4, 4)), (2, (2, 2, 5, 5))),
        116,
        (odd_0, odd_0c, odd_1, odd_3, odd_1c, odd_3c),
    )
    even_0c = shift(after(even_0, grads[0]), "c", 1)
    ahead = shift(after(mine[2], grads[0]), "z", 1)
    back = shift(after(mine[1], grads[0]), "z", -1)
    ahead = add(ahead, mine[3])
    grads = grads_of(
        "grads_3", ((3, (0, 1, 2, 3)),), 72, (even_1, even_3, even_1c, even_3c), grads, (even_2, odd_2, ahead)
    )
    even_2c, odd_2c = shift(even_2, "c", 1), shift(odd_2, "c", 1)
    ahead = shift(ahead, "z", 1)
    send = sum_of(mine[0, 1], ahead[1], back[1])
    keep = mine[0, 0].astype(F32) + ahead[0].astype(F32) + back[0].astype(F32)
    gate_grad, up_grad = grads_of(
        "grads_4_5",
        ((4, (0, 1, 2, 3)), (5, (4, 4, 5, 5))),
        108,
        (even_0, even_2, even_0c, even_2c, odd_2, odd_2c),
        grads,
        (send,),
    )
    input_grad = (keep + after(shift(send, "yl", 1), gate_grad).astype(F32)).astype(BF)
    return input_grad, gate_grad, up_grad


def solution(mesh):
    fine = Mesh(mesh.devices.reshape(2, 2, 4, 4, 2), ("yh", "c", "x", "z", "yl"))
    tok, wt = ("yh", "c"), ("x", "z", "yl")
    in_specs = (P(tok, wt),) * 4 + (P(wt, None, None),) * 2 + (P(wt),) * 3
    out_specs = (P(tok, wt), P(wt, None, None), P(wt, None, None))
    return jax.shard_map(body, mesh=fine, in_specs=in_specs, out_specs=out_specs, check_vma=False)
```

profile of v0, /device:TPU:0, one launch (start us, length us, event | category | flops | bytes accessed | tf_op | source)
XLA Modules:
  0.0 167.2 jit_solution(12999541165306062569)
XLA Ops:
  7.4 2.7 %collective-permute-start.1 = (bf16[2,384,128]{2,1,0:T(8,128)(2,1)S(1)}, bf16[2,384,128]{2,1,0:T(8,128)(2,1)S(1)}, u32[]{:S(2)}, u32[]{:S(2)}) collective-permute-start(bf16[2,384,128]{2,1,0:T(8,128)(2,1)S(1)} %pad_maximum_fusion.5), channel_id=1, source_target_pairs={{0,16},{8,24},{16,0},{24,8},{32,48},{40,56},{48,32},{56,40},{1,17}... | collective-permute-start | bytes 589832 | tf_op jit(solution)/shard_map/ppermute | solution.py:35
  11.6 3.2 %collective-permute-start.4 = (bf16[1024,384]{1,0:T(8,128)(2,1)S(1)}, bf16[1024,384]{1,0:T(8,128)(2,1)S(1)}, u32[]{:S(2)}, u32[]{:S(2)}) collective-permute-start(bf16[1024,384]{1,0:T(8,128)(2,1)S(1)} %get-tuple-element.39), channel_id=1, source_target_pairs={{0,64},{64,0},{1,65},{65,1},{2,66},{66,2},{3,67},{67,3},{4,68},{68... | collective-permute-start | bytes 2359304 | tf_op jit(solution)/shard_map/ppermute | solution.py:23
  18.1 2.2 %copy-done.4 = bf16[128,128,128]{2,1,0:T(8,128)(2,1)S(1)} copy-done((bf16[128,128,128]{2,1,0:T(8,128)(2,1)S(1)}, bf16[128,128,128]{2,1,0:T(8,128)(2,1)}, u32[]{:S(2)}) %copy-start.4) | copy-done | bytes 4194328
  20.3 4.8 %terms.4 = bf16[8,384,256]{2,1,0:T(8,128)(2,1)} custom-call(s32[256]{0:T(256)S(1)} %select_reduce_fusion.tab, s32[32]{0:T(128)S(1)} %mul.262.order, bf16[384,1024]{1,0:T(8,128)(2,1)S(1)} %get-tuple-element.46.gu, bf16[128,128,128]{2,1,0:T(8,128)(2,1)S(1)} %copy-done, bf16[128,128,128]{2,1,0:T(8,128)(2,1)S(1)} %copy-done.4), custom_call_target="tpu_custom_call" | custom-call | flops 1 | bytes 1 | tf_op jit(solution)/shard_map/terms/pallas_call | solution.py:96
  27.9 2.5 %collective-permute-done.4 = bf16[1024,384]{1,0:T(8,128)(2,1)S(1)} collective-permute-done((bf16[1024,384]{1,0:T(8,128)(2,1)S(1)}, bf16[1024,384]{1,0:T(8,128)(2,1)S(1)}, u32[]{:S(2)}, u32[]{:S(2)}) %collective-permute-start.4) | collective-permute-done | bytes 786464 | tf_op jit(solution)/shard_map/ppermute | solution.py:23
  31.9 4.8 %terms.5 = bf16[8,384,256]{2,1,0:T(8,128)(2,1)} custom-call(s32[256]{0:T(256)S(1)} %select_reduce_fusion.tab, s32[32]{0:T(128)S(1)} %mul.262.order, bf16[384,1024]{1,0:T(8,128)(2,1)S(1)} %get-tuple-element.46.gu, bf16[128,128,128]{2,1,0:T(8,128)(2,1)S(1)} %copy-done.1, bf16[128,128,128]{2,1,0:T(8,128)(2,1)S(1)} %copy-done.4), custom_call_target="tpu_custom_call" | custom-call | flops 1 | bytes 1 | tf_op jit(solution)/shard_map/terms/pallas_call | solution.py:96
  40.9 2.3 %collective-permute-start.10 = (bf16[8,384,256]{2,1,0:T(8,128)(2,1)}, bf16[8,384,256]{2,1,0:T(8,128)(2,1)}, u32[]{:S(2)}, u32[]{:S(2)}) collective-permute-start(bf16[8,384,256]{2,1,0:T(8,128)(2,1)} %terms.5), channel_id=1, source_target_pairs={{0,24},{8,0},{16,8},{24,16},{32,40},{40,48},{48,56},{56,32},{1,25}... | collective-permute-start | bytes 4718600 | tf_op jit(solution)/shard_map/ppermute | solution.py:35
  43.2 2.2 %copy-done.2 = bf16[128,128,128]{2,1,0:T(8,128)(2,1)S(1)} copy-done((bf16[128,128,128]{2,1,0:T(8,128)(2,1)S(1)}, bf16[128,128,128]{2,1,0:T(8,128)(2,1)}, u32[]{:S(2)}) %copy-start.2) | copy-done | bytes 4194328
  45.4 2.2 %copy-done.5 = bf16[128,128,128]{2,1,0:T(8,128)(2,1)S(1)} copy-done((bf16[128,128,128]{2,1,0:T(8,128)(2,1)S(1)}, bf16[128,128,128]{2,1,0:T(8,128)(2,1)}, u32[]{:S(2)}) %copy-start.5) | copy-done | bytes 4194328
  47.6 3.7 %terms.7 = bf16[8,384,256]{2,1,0:T(8,128)(2,1)S(1)} custom-call(s32[256]{0:T(256)S(1)} %select_reduce_fusion.tab, s32[32]{0:T(128)S(1)} %mul.262.order, bf16[384,1024]{1,0:T(8,128)(2,1)S(1)} %get-tuple-element.46.gu, bf16[128,128,128]{2,1,0:T(8,128)(2,1)S(1)} %copy-done.2, bf16[128,128,128]{2,1,0:T(8,128)(2,1)S(1)} %copy-done.5), custom_call_target="tpu_custom_call" | custom-call | flops 1 | bytes 1 | tf_op jit(solution)/shard_map/terms/pallas_call | solution.py:96
  55.9 3.6 %terms.6 = bf16[8,384,256]{2,1,0:T(8,128)(2,1)S(1)} custom-call(s32[256]{0:T(256)S(1)} %select_reduce_fusion.tab, s32[32]{0:T(128)S(1)} %mul.262.order, bf16[384,1024]{1,0:T(8,128)(2,1)S(1)} %get-tuple-element.46.gu, bf16[128,128,128]{2,1,0:T(8,128)(2,1)S(1)} %copy-done.3, bf16[128,128,128]{2,1,0:T(8,128)(2,1)S(1)} %copy-done.6), custom_call_target="tpu_custom_call" | custom-call | flops 1 | bytes 1 | tf_op jit(solution)/shard_map/terms/pallas_call | solution.py:96
  59.5 3.0 %add_convert_fusion.1 = bf16[8,384,256]{2,1,0:T(8,128)(2,1)} fusion(bf16[8,384,256]{2,1,0:T(8,128)(2,1)S(1)} %terms.7, bf16[8,384,256]{2,1,0:T(8,128)(2,1)} %collective-permute-done.8), kind=kLoop, calls=%fused_computation.1 | loop fusion | flops 3145728 | bytes 4718592 | tf_op jit(solution)/shard_map/convert_element_type | solution.py:39
  63.1 2.4 %pad_maximum_fusion.rest_0_ = bf16[16,384,128]{2,1,0:T(8,128)(2,1)} fusion(bf16[4,384,128]{2,1,0:T(8,128)(2,1)S(1)} %collective-permute-done.11, bf16[4,384,128]{2,1,0:T(8,128)(2,1)} %collective-permute-done.5, bf16[4,384,128]{2,1,0:T(8,128)(2,1)S(1)} %copy-done.14, bf16[4,384,128]{2,1,0:T(8,128)(2,1)S(1)} %pad_maximum_fusion.3), kind=kLoop, calls=%fused_computation.2 | loop fusion | flops 2359296 | bytes 3145728 | tf_op jit(solution)/shard_map/concatenate | solution.py:275
  72.7 2.2 %collective-permute-start.24 = (bf16[16,384,128]{2,1,0:T(8,128)(2,1)}, bf16[16,384,128]{2,1,0:T(8,128)(2,1)}, u32[]{:S(2)}, u32[]{:S(2)}) collective-permute-start(bf16[16,384,128]{2,1,0:T(8,128)(2,1)} %pad_maximum_fusion.rest_0_), channel_id=1, source_target_pairs={{0,65},{1,0},{32,33},{33,96},{64,1},{65,64},{96,97},{97,32},{2,67}... | collective-permute-start | bytes 4718600 | tf_op jit(solution)/shard_map/ppermute | solution.py:35
  74.9 9.6 %collective-permute-done.9 = bf16[8,384,256]{2,1,0:T(8,128)(2,1)} collective-permute-done((bf16[8,384,256]{2,1,0:T(8,128)(2,1)}, bf16[8,384,256]{2,1,0:T(8,128)(2,1)}, u32[]{:S(2)}, u32[]{:S(2)}) %collective-permute-start.9) | collective-permute-done | bytes 1572896 | tf_op jit(solution)/shard_map/ppermute | solution.py:35
  84.5 3.6 %add_convert_fusion = bf16[8,384,256]{2,1,0:T(8,128)(2,1)} fusion(bf16[8,384,256]{2,1,0:T(8,128)(2,1)} %collective-permute-done.10, bf16[8,384,256]{2,1,0:T(8,128)(2,1)} %collective-permute-done.9, bf16[8,384,256]{2,1,0:T(8,128)(2,1)S(1)} %terms.6), kind=kLoop, calls=%fused_computation | loop fusion | flops 4718592 | bytes 6291456 | tf_op jit(solution)/shard_map/convert_element_type | solution.py:43
  88.4 12.4 %collective-permute-done.23.rest_0_ = bf16[16,384,128]{2,1,0:T(8,128)(2,1)} collective-permute-done((bf16[16,384,128]{2,1,0:T(8,128)(2,1)}, bf16[16,384,128]{2,1,0:T(8,128)(2,1)}, u32[]{:S(2)}, u32[]{:S(2)}) %collective-permute-start.23) | collective-permute-done | bytes 1572896 | tf_op jit(solution)/shard_map/ppermute | solution.py:35
  100.9 3.6 %collective-permute-done.15.rest_2_ = bf16[16,384,128]{2,1,0:T(8,128)(2,1)} collective-permute-done((bf16[16,384,128]{2,1,0:T(8,128)(2,1)S(1)}, bf16[16,384,128]{2,1,0:T(8,128)(2,1)}, u32[]{:S(2)}, u32[]{:S(2)}) %collective-permute-start.15) | collective-permute-done | bytes 1572896 | tf_op jit(solution)/shard_map/ppermute | solution.py:35
  111.2 12.4 %grads_0_1_2.1 = (bf16[128,128,128]{2,1,0:T(8,128)(2,1)}, bf16[128,128,128]{2,1,0:T(8,128)(2,1)}) custom-call(s32[164]{0:T(256)S(1)} %get-tuple-element.77.lrow, s32[164]{0:T(256)S(1)} %get-tuple-element.76.lslot, s32[656]{0:T(1024)S(1)} %reshape.625.ltile, s32[16]{0:T(128)S(1)} %pad_add_fusion.1.meta, ...), custom_call_target="tpu_custom_call" | custom-call | flops 1 | bytes 1 | tf_op jit(solution)/shard_map/grads_0_1_2/pallas_call | solution.py:164
  123.7 3.2 %collective-permute-start.21 = (bf16[2,384,256]{2,1,0:T(8,128)(2,1)S(1)}, bf16[2,384,256]{2,1,0:T(8,128)(2,1)S(1)}, u32[]{:S(2)}, u32[]{:S(2)}) collective-permute-start(bf16[2,384,256]{2,1,0:T(8,128)(2,1)S(1)} %get-tuple-element.59), channel_id=1, source_target_pairs={{0,6},{2,0},{4,2},{6,4},{32,34},{34,36},{36,38},{38,32},{1,7},{3,1... | collective-permute-start | bytes 1179656 | tf_op jit(solution)/shard_map/ppermute | solution.py:35
  126.9 10.8 %collective-permute-done.19 = bf16[2,384,256]{2,1,0:T(8,128)(2,1)S(1)} collective-permute-done((bf16[2,384,256]{2,1,0:T(8,128)(2,1)S(1)}, bf16[2,384,256]{2,1,0:T(8,128)(2,1)S(1)}, u32[]{:S(2)}, u32[]{:S(2)}) %collective-permute-start.19) | collective-permute-done | bytes 393248 | tf_op jit(solution)/shard_map/ppermute | solution.py:35
  138.9 7.9 %collective-permute-done.20 = bf16[2,384,256]{2,1,0:T(8,128)(2,1)S(1)} collective-permute-done((bf16[2,384,256]{2,1,0:T(8,128)(2,1)S(1)}, bf16[2,384,256]{2,1,0:T(8,128)(2,1)S(1)}, u32[]{:S(2)}, u32[]{:S(2)}) %collective-permute-start.20) | collective-permute-done | bytes 393248 | tf_op jit(solution)/shard_map/ppermute | solution.py:35
  148.7 7.9 %grads_3.1 = (bf16[128,128,128]{2,1,0:T(8,128)(2,1)}, bf16[128,128,128]{2,1,0:T(8,128)(2,1)}) custom-call(s32[164]{0:T(256)S(1)} %get-tuple-element.77.lrow, s32[164]{0:T(256)S(1)} %get-tuple-element.76.lslot, s32[656]{0:T(1024)S(1)} %reshape.625.ltile, s32[16]{0:T(128)S(1)} %pad_add_fusion.1.meta, ...), custom_call_target="tpu_custom_call", output_to_operand_aliasing={{0}: (9, {}), {1}: (10, {})} | custom-call | flops 1 | bytes 1 | tf_op jit(solution)/shard_map/grads_3/pallas_call | solution.py:164
  156.7 9.8 %grads_4_5.1 = (bf16[128,128,128]{2,1,0:T(8,128)(2,1)}, bf16[128,128,128]{2,1,0:T(8,128)(2,1)}) custom-call(s32[164]{0:T(256)S(1)} %get-tuple-element.77.lrow, s32[164]{0:T(256)S(1)} %get-tuple-element.76.lslot, s32[656]{0:T(1024)S(1)} %reshape.625.ltile, s32[16]{0:T(128)S(1)} %pad_add_fusion.1.meta, ...), custom_call_target="tpu_custom_call", output_to_operand_aliasing={{0}: (11, {}), {1}: (12, {})} | custom-call | flops 1 | bytes 1 | tf_op jit(solution)/shard_map/grads_4_5/pallas_call | solution.py:164
  (136 shorter events, 42.5 us)
Async XLA Ops:
  5.8 19.9 %collective-permute-start = (bf16[2,384,128]{2,1,0:T(8,128)(2,1)S(1)}, bf16[2,384,128]{2,1,0:T(8,128)(2,1)S(1)}, u32[]{:S(2)}, u32[]{:S(2)}) collective-permute-start(bf16[2,384,128]{2,1,0:T(8,128)(2,1)S(1)} %pad_maximum_fusion.5), channel_id=1, source_target_pairs={{0,8},{8,16},{16,24},{24,0},{32,56},{40,32},{48,40},{56,48},{1,9},... | collective-permute-start | bytes 589832 | tf_op jit(solution)/shard_map/ppermute | solution.py:35
  7.4 18.2 %collective-permute-start.1 = (bf16[2,384,128]{2,1,0:T(8,128)(2,1)S(1)}, bf16[2,384,128]{2,1,0:T(8,128)(2,1)S(1)}, u32[]{:S(2)}, u32[]{:S(2)}) collective-permute-start(bf16[2,384,128]{2,1,0:T(8,128)(2,1)S(1)} %pad_maximum_fusion.5), channel_id=1, source_target_pairs={{0,16},{8,24},{16,0},{24,8},{32,48},{40,56},{48,32},{56,40},{1,17}... | collective-permute-start | bytes 589832 | tf_op jit(solution)/shard_map/ppermute | solution.py:35
  10.2 15.5 %collective-permute-start.2 = (bf16[2,384,128]{2,1,0:T(8,128)(2,1)S(1)}, bf16[2,384,128]{2,1,0:T(8,128)(2,1)S(1)}, u32[]{:S(2)}, u32[]{:S(2)}) collective-permute-start(bf16[2,384,128]{2,1,0:T(8,128)(2,1)S(1)} %pad_maximum_fusion.5), channel_id=1, source_target_pairs={{0,24},{8,0},{16,8},{24,16},{32,40},{40,48},{48,56},{56,32},{1,25}... | collective-permute-start | bytes 589832 | tf_op jit(solution)/shard_map/ppermute | solution.py:35
  11.6 18.7 %collective-permute-start.4 = (bf16[1024,384]{1,0:T(8,128)(2,1)S(1)}, bf16[1024,384]{1,0:T(8,128)(2,1)S(1)}, u32[]{:S(2)}, u32[]{:S(2)}) collective-permute-start(bf16[1024,384]{1,0:T(8,128)(2,1)S(1)} %get-tuple-element.39), channel_id=1, source_target_pairs={{0,64},{64,0},{1,65},{65,1},{2,66},{66,2},{3,67},{67,3},{4,68},{68... | collective-permute-start | bytes 2359304 | tf_op jit(solution)/shard_map/ppermute | solution.py:23
  25.1 34.5 %collective-permute-start.8 = (bf16[8,384,256]{2,1,0:T(8,128)(2,1)}, bf16[8,384,256]{2,1,0:T(8,128)(2,1)}, u32[]{:S(2)}, u32[]{:S(2)}) collective-permute-start(bf16[8,384,256]{2,1,0:T(8,128)(2,1)} %terms.4), channel_id=1, source_target_pairs={{0,8},{8,16},{16,24},{24,0},{32,56},{40,32},{48,40},{56,48},{1,9},... | collective-permute-start | bytes 4718600 | tf_op jit(solution)/shard_map/ppermute | solution.py:35
  25.8 10.9 %collective-permute-start.3 = (bf16[4,384,128]{2,1,0:T(8,128)(2,1)S(1)}, bf16[4,384,128]{2,1,0:T(8,128)(2,1)S(1)}, u32[]{:S(2)}, u32[]{:S(2)}) collective-permute-start(bf16[4,384,128]{2,1,0:T(8,128)(2,1)S(1)} %pad_maximum_fusion.3), channel_id=1, source_target_pairs={{0,2},{2,4},{4,6},{6,0},{32,38},{34,32},{36,34},{38,36},{1,3},{3,5... | collective-permute-start | bytes 1179656 | tf_op jit(solution)/shard_map/ppermute | solution.py:35
  36.7 14.6 %collective-permute-start.5 = (bf16[4,384,128]{2,1,0:T(8,128)(2,1)S(1)}, bf16[4,384,128]{2,1,0:T(8,128)(2,1)}, u32[]{:S(2)}, u32[]{:S(2)}) collective-permute-start(bf16[4,384,128]{2,1,0:T(8,128)(2,1)S(1)} %collective-permute-done.3), channel_id=1, source_target_pairs={{0,2},{2,4},{4,6},{6,0},{32,38},{34,32},{36,34},{38,36},{1,3},{3,5... | collective-permute-start | bytes 1179656 | tf_op jit(solution)/shard_map/ppermute | solution.py:35
  39.4 15.2 %collective-permute-start.7 = (bf16[4,384,128]{2,1,0:T(8,128)(2,1)}, bf16[4,384,128]{2,1,0:T(8,128)(2,1)}, u32[]{:S(2)}, u32[]{:S(2)}) collective-permute-start(bf16[4,384,128]{2,1,0:T(8,128)(2,1)} %collective-permute-done.6), channel_id=1, source_target_pairs={{0,1},{1,64},{32,97},{33,32},{64,65},{65,0},{96,33},{97,96},{2,3},... | collective-permute-start | bytes 1179656 | tf_op jit(solution)/shard_map/ppermute | solution.py:35
  40.9 31.8 %collective-permute-start.10 = (bf16[8,384,256]{2,1,0:T(8,128)(2,1)}, bf16[8,384,256]{2,1,0:T(8,128)(2,1)}, u32[]{:S(2)}, u32[]{:S(2)}) collective-permute-start(bf16[8,384,256]{2,1,0:T(8,128)(2,1)} %terms.5), channel_id=1, source_target_pairs={{0,24},{8,0},{16,8},{24,16},{32,40},{40,48},{48,56},{56,32},{1,25}... | collective-permute-start | bytes 4718600 | tf_op jit(solution)/shard_map/ppermute | solution.py:35
  51.3 11.8 %collective-permute-start.11 = (bf16[4,384,128]{2,1,0:T(8,128)(2,1)}, bf16[4,384,128]{2,1,0:T(8,128)(2,1)S(1)}, u32[]{:S(2)}, u32[]{:S(2)}) collective-permute-start(bf16[4,384,128]{2,1,0:T(8,128)(2,1)} %collective-permute-done.5), channel_id=1, source_target_pairs={{0,2},{2,4},{4,6},{6,0},{32,38},{34,32},{36,34},{38,36},{1,3},{3,5... | collective-permute-start | bytes 1179656 | tf_op jit(solution)/shard_map/ppermute | solution.py:35
  54.6 12.0 %collective-permute-start.12 = (bf16[4,384,128]{2,1,0:T(8,128)(2,1)}, bf16[4,384,128]{2,1,0:T(8,128)(2,1)S(1)}, u32[]{:S(2)}, u32[]{:S(2)}) collective-permute-start(bf16[4,384,128]{2,1,0:T(8,128)(2,1)} %collective-permute-done.7), channel_id=1, source_target_pairs={{0,1},{1,64},{32,97},{33,32},{64,65},{65,0},{96,33},{97,96},{2,3},... | collective-permute-start | bytes 1179656 | tf_op jit(solution)/shard_map/ppermute | solution.py:35
  62.6 21.9 %collective-permute-start.9 = (bf16[8,384,256]{2,1,0:T(8,128)(2,1)}, bf16[8,384,256]{2,1,0:T(8,128)(2,1)}, u32[]{:S(2)}, u32[]{:S(2)}) collective-permute-start(bf16[8,384,256]{2,1,0:T(8,128)(2,1)} %add_convert_fusion.1), channel_id=1, source_target_pairs={{0,8},{8,16},{16,24},{24,0},{32,56},{40,32},{48,40},{56,48},{1,9},... | collective-permute-start | bytes 4718600 | tf_op jit(solution)/shard_map/ppermute | solution.py:35
  65.5 35.4 %collective-permute-start.23 = (bf16[16,384,128]{2,1,0:T(8,128)(2,1)}, bf16[16,384,128]{2,1,0:T(8,128)(2,1)}, u32[]{:S(2)}, u32[]{:S(2)}) collective-permute-start(bf16[16,384,128]{2,1,0:T(8,128)(2,1)} %pad_maximum_fusion.rest_0_), channel_id=1, source_target_pairs={{0,1},{1,64},{32,97},{33,32},{64,65},{65,0},{96,33},{97,96},{2,3},... | collective-permute-start | bytes 4718600 | tf_op jit(solution)/shard_map/ppermute | solution.py:35
  67.9 36.6 %collective-permute-start.15 = (bf16[16,384,128]{2,1,0:T(8,128)(2,1)S(1)}, bf16[16,384,128]{2,1,0:T(8,128)(2,1)}, u32[]{:S(2)}, u32[]{:S(2)}) collective-permute-start(bf16[16,384,128]{2,1,0:T(8,128)(2,1)S(1)} %pad_maximum_fusion.1.rest_0_), channel_id=1, source_target_pairs={{0,2},{2,4},{4,6},{6,0},{32,38},{34,32},{36,34},{38,36},{1,3},{3,5... | collective-permute-start | bytes 4718600 | tf_op jit(solution)/shard_map/ppermute | solution.py:35
  69.9 34.6 %collective-permute-start.16 = (bf16[16,384,128]{2,1,0:T(8,128)(2,1)S(1)}, bf16[16,384,128]{2,1,0:T(8,128)(2,1)}, u32[]{:S(2)}, u32[]{:S(2)}) collective-permute-start(bf16[16,384,128]{2,1,0:T(8,128)(2,1)S(1)} %pad_maximum_fusion.1.rest_0_), channel_id=1, source_target_pairs={{0,6},{2,0},{4,2},{6,4},{32,34},{34,36},{36,38},{38,32},{1,7},{3,1... | collective-permute-start | bytes 4718600 | tf_op jit(solution)/shard_map/ppermute | solution.py:35
  72.7 32.7 %collective-permute-start.24 = (bf16[16,384,128]{2,1,0:T(8,128)(2,1)}, bf16[16,384,128]{2,1,0:T(8,128)(2,1)}, u32[]{:S(2)}, u32[]{:S(2)}) collective-permute-start(bf16[16,384,128]{2,1,0:T(8,128)(2,1)} %pad_maximum_fusion.rest_0_), channel_id=1, source_target_pairs={{0,65},{1,0},{32,33},{33,96},{64,1},{65,64},{96,97},{97,32},{2,67}... | collective-permute-start | bytes 4718600 | tf_op jit(solution)/shard_map/ppermute | solution.py:35
  88.1 19.2 %collective-permute-start.13 = (bf16[2,1024,384]{2,1,0:T(8,128)(2,1)}, bf16[2,1024,384]{2,1,0:T(8,128)(2,1)}, u32[]{:S(2)}, u32[]{:S(2)}) collective-permute-start(bf16[2,1024,384]{2,1,0:T(8,128)(2,1)} %pad_maximum_fusion.2), channel_id=1, source_target_pairs={{0,32},{32,0},{1,33},{33,1},{2,34},{34,2},{3,35},{35,3},{4,36},{36... | collective-permute-start | bytes 4718600 | tf_op jit(solution)/shard_map/ppermute | solution.py:23
  105.4 32.5 %collective-permute-start.25 = (bf16[16,384,128]{2,1,0:T(8,128)(2,1)}, bf16[16,384,128]{2,1,0:T(8,128)(2,1)S(1)}, u32[]{:S(2)}, u32[]{:S(2)}) collective-permute-start(bf16[16,384,128]{2,1,0:T(8,128)(2,1)} %collective-permute-done.23.rest_0_), channel_id=1, source_target_pairs={{0,1},{1,64},{32,97},{33,32},{64,65},{65,0},{96,33},{97,96},{2,3},... | collective-permute-start | bytes 4718600 | tf_op jit(solution)/shard_map/ppermute | solution.py:35
  107.4 31.0 %collective-permute-start.28 = (bf16[16,384,128]{2,1,0:T(8,128)(2,1)}, bf16[16,384,128]{2,1,0:T(8,128)(2,1)S(1)}, u32[]{:S(2)}, u32[]{:S(2)}) collective-permute-start(bf16[16,384,128]{2,1,0:T(8,128)(2,1)} %collective-permute-done.15.rest_2_), channel_id=1, source_target_pairs={{0,2},{2,4},{4,6},{6,0},{32,38},{34,32},{36,34},{38,36},{1,3},{3,5... | collective-permute-start | bytes 4718600 | tf_op jit(solution)/shard_map/ppermute | solution.py:35
  123.6 14.1 %collective-permute-start.19 = (bf16[2,384,256]{2,1,0:T(8,128)(2,1)S(1)}, bf16[2,384,256]{2,1,0:T(8,128)(2,1)S(1)}, u32[]{:S(2)}, u32[]{:S(2)}) collective-permute-start(bf16[2,384,256]{2,1,0:T(8,128)(2,1)S(1)} %get-tuple-element.58), channel_id=1, source_target_pairs={{0,2},{2,4},{4,6},{6,0},{32,38},{34,32},{36,34},{38,36},{1,3},{3,5... | collective-permute-start | bytes 1179656 | tf_op jit(solution)/shard_map/ppermute | solution.py:35
  123.7 14.9 %collective-permute-start.21 = (bf16[2,384,256]{2,1,0:T(8,128)(2,1)S(1)}, bf16[2,384,256]{2,1,0:T(8,128)(2,1)S(1)}, u32[]{:S(2)}, u32[]{:S(2)}) collective-permute-start(bf16[2,384,256]{2,1,0:T(8,128)(2,1)S(1)} %get-tuple-element.59), channel_id=1, source_target_pairs={{0,6},{2,0},{4,2},{6,4},{32,34},{34,36},{36,38},{38,32},{1,7},{3,1... | collective-permute-start | bytes 1179656 | tf_op jit(solution)/shard_map/ppermute | solution.py:35
  138.4 18.2 %collective-permute-start.27 = (bf16[16,384,128]{2,1,0:T(8,128)(2,1)S(1)}, bf16[16,384,128]{2,1,0:T(8,128)(2,1)S(1)}, u32[]{:S(2)}, u32[]{:S(2)}) collective-permute-start(bf16[16,384,128]{2,1,0:T(8,128)(2,1)S(1)} %collective-permute-done.25.rest_1_), channel_id=1, source_target_pairs={{0,32},{32,0},{1,33},{33,1},{2,34},{34,2},{3,35},{35,3},{4,36},{36... | collective-permute-start | bytes 4718600 | tf_op jit(solution)/shard_map/ppermute | solution.py:23
  138.5 18.1 %collective-permute-start.26 = (bf16[16,384,128]{2,1,0:T(8,128)(2,1)}, bf16[16,384,128]{2,1,0:T(8,128)(2,1)S(1)}, u32[]{:S(2)}, u32[]{:S(2)}) collective-permute-start(bf16[16,384,128]{2,1,0:T(8,128)(2,1)} %pad_maximum_fusion.rest_0_), channel_id=1, source_target_pairs={{0,32},{32,0},{1,33},{33,1},{2,34},{34,2},{3,35},{35,3},{4,36},{36... | collective-permute-start | bytes 4718600 | tf_op jit(solution)/shard_map/ppermute | solution.py:23
  146.9 19.6 %collective-permute-start.22 = (bf16[384,256]{1,0:T(8,128)(2,1)S(1)}, bf16[384,256]{1,0:T(8,128)(2,1)S(1)}, u32[]{:S(2)}, u32[]{:S(2)}) collective-permute-start(bf16[384,256]{1,0:T(8,128)(2,1)S(1)} %fusion), channel_id=1, source_target_pairs={{0,1},{1,0},{2,3},{3,2},{4,5},{5,4},{6,7},{7,6},{8,9},{9,8},{10,11... | collective-permute-start | bytes 589832 | tf_op jit(solution)/shard_map/ppermute | solution.py:23
  (27 other events, 214.1 us)
where the time goes:
time: 167 us
  Pallas kernels  48.1 us (29%)
  waiting for transfers between devices  47.4 us (28%)
  starting transfers between devices  37.9 us (23%)
  local copies, waits for them, and re-layouts  16.5 us (10%)
  other arithmetic  15.5 us (9%)
  between operations  1.79 us (1%)
    ppermute x21, waiting for transfers between devices, shift(): return lax.ppermute(value, AXES[axis], pairs)  44.9 us
    ppermute x21, starting transfers between devices, shift(): return lax.ppermute(value, AXES[axis], pairs)  31.3 us
    pallas_call x3, Pallas kernels, weight_grads(): pl.pallas_call(functools.partial(kinds_kernel, kinds, len(held)), out_sha...  30.1 us
    pallas_call x4, Pallas kernels, terms(): pl.pallas_call(functools.partial(chunk_kernel, k), out_shape=PIECE, in_sp...  16.9 us
    unnamed x39, local copies, waits for them, and re-layouts  13.3 us
    ppermute x11, starting transfers between devices, shift(): return lax.ppermute(value, axis, [(0, 1), (1, 0)])  6.61 us
    convert_element_type x2, other arithmetic, sum_of(): return (a.astype(F32) + b.astype(F32) + c.astype(F32)).astype(BF)  3.68 us
  transfers between devices with their start and end apart: 32, of which 7 were waited for; matrix products, arithmetic and copies ran while one was open for 11% of the time, Pallas kernels for 28%

commit v1 on v0

--- a/solution.py
+++ b/solution.py
@@ -271,7 +271,7 @@
     evens.append(shift(after(evens[2], t3), "z", 1))
     odds.append(shift(after(odds[2], t3), "y", 1))
     t0 = terms(0, tab, order, after(gu, evens[2], odds[2]), *blocks)
-    moving = add(ahead, t3)
+    moving = add(after(ahead, evens[2], odds[2]), t3)
     even_0 = after(jnp.concatenate(evens), t0, moving)
     odd_0 = after(jnp.concatenate(odds), t0, moving)
     even_1, even_3 = shift(even_0, "y", 1), shift(even_0, "y", -1)
@@ -290,7 +290,7 @@
     even_2 = shift(after(even_1, even_3), "y", 1)
     odd_2 = shift(after(odd_1, odd_3), "z", 1)
     odd_1c, odd_3c = shift(odd_1, "c", 1), shift(odd_3, "c", 1)
-    even_1c, even_3c = shift(after(even_1, odd_1c), "c", 1), shift(after(even_3, odd_1c), "c", 1)
+    even_1c, even_3c = (shift(after(v, odd_1c, odd_3c, odd_0c), "c", 1) for v in (even_1, even_3))
     grads = grads_of(
         "grads_0_1_2",
         ((0, (0, 0, 1, 1)), (1, (3, 3, 4, 4)), (2, (2, 2, 5, 5))),
@@ -298,24 +298,20 @@
         (odd_0, odd_0c, odd_1, odd_3, odd_1c, odd_3c),
     )
     even_0c = shift(after(even_0, grads[0]), "c", 1)
+    even_2 = after(even_2, grads[0])
     ahead = shift(after(mine[2], grads[0]), "z", 1)
     back = shift(after(mine[1], grads[0]), "z", -1)
-    ahead = add(ahead, mine[3])
+    grads = grads_of("grads_3", ((3, (0, 1, 2, 3)),), 72, (even_1, even_3, even_1c, even_3c), grads, (even_2,))
+    even_2c = shift(even_2, "c", 1)
+    odd_2c = shift(odd_2, "c", 1)
+    ahead = add(after(ahead, grads[0]), mine[3])
     grads = grads_of(
-        "grads_3", ((3, (0, 1, 2, 3)),), 72, (even_1, even_3, even_1c, even_3c), grads, (even_2, odd_2, ahead)
+        "grads_4", ((4, (0, 1, 2, 3)),), 72, (even_0, even_2, even_0c, even_2c), grads, (ahead, odd_2)
     )
-    even_2c, odd_2c = shift(even_2, "c", 1), shift(odd_2, "c", 1)
-    ahead = shift(ahead, "z", 1)
+    ahead = after(shift(ahead, "z", 1), grads[0])
     send = sum_of(mine[0, 1], ahead[1], back[1])
     keep = mine[0, 0].astype(F32) + ahead[0].astype(F32) + back[0].astype(F32)
-    gate_grad, up_grad = grads_of(
-        "grads_4_5",
-        ((4, (0, 1, 2, 3)), (5, (4, 4, 5, 5))),
-        108,
-        (even_0, even_2, even_0c, even_2c, odd_2, odd_2c),
-        grads,
-        (send,),
-    )
+    gate_grad, up_grad = grads_of("grads_5", ((5, (0, 0, 1, 1)),), 40, (odd_2, odd_2c), grads, (send,))
     input_grad = (keep + after(shift(send, "yl", 1), gate_grad).astype(F32)).astype(BF)
     return input_grad, gate_grad, up_grad
 

time: 167 us -> 163 us (0.976)
  local copies, waits for them, and re-layouts: 16.5 us -> 22.8 us
  waiting for transfers between devices: 47.4 us -> 41.4 us
  Pallas kernels: 48.1 us -> 43.2 us
  other arithmetic: 15.5 us -> 12.2 us
  starting transfers between devices: 37.9 us -> 41.1 us
    ppermute x21, waiting for transfers between devices: 44.9 us -> 36.2 us  [shift(): return lax.ppermute(value, AXES[axis], pairs)]
    unnamed x39 -> x57, local copies, waits for them, and re-layouts: 13.3 us -> 18.5 us
    pallas_call x3 -> x4, Pallas kernels: 30.1 us -> 26.3 us  [weight_grads(): pl.pallas_call(functools.partial(kinds_kernel, kinds, len(held)), out_sha...]
    ppermute x11, starting transfers between devices: 6.61 us -> 10.2 us  [shift(): return lax.ppermute(value, axis, [(0, 1), (1, 0)])]
    ppermute x11, waiting for transfers between devices: 2.51 us -> 5.23 us  [shift(): return lax.ppermute(value, axis, [(0, 1), (1, 0)])]
  transfers between devices with their start and end apart: 32 -> 32, of which waited for: 7 -> 12; matrix products, arithmetic and copies ran while one was open for 11% -> 10% of each run, Pallas kernels for 28% -> 26%
where the time goes in v1:
time: 163 us
  Pallas kernels  43.2 us (27%)
  waiting for transfers between devices  41.4 us (25%)
  starting transfers between devices  41.1 us (25%)
  local copies, waits for them, and re-layouts  22.8 us (14%)
  other arithmetic  12.2 us (7%)
  between operations  1.79 us (1%)
    ppermute x21, waiting for transfers between devices, shift(): return lax.ppermute(value, AXES[axis], pairs)  36.2 us
    ppermute x21, starting transfers between devices, shift(): return lax.ppermute(value, AXES[axis], pairs)  31 us
    pallas_call x4, Pallas kernels, weight_grads(): pl.pallas_call(functools.partial(kinds_kernel, kinds, len(held)), out_sha...  26.3 us
    unnamed x57, local copies, waits for them, and re-layouts  18.5 us
    pallas_call x4, Pallas kernels, terms(): pl.pallas_call(functools.partial(chunk_kernel, k), out_shape=PIECE, in_sp...  15.8 us
    ppermute x11, starting transfers between devices, shift(): return lax.ppermute(value, axis, [(0, 1), (1, 0)])  10.2 us
    ppermute x11, waiting for transfers between devices, shift(): return lax.ppermute(value, axis, [(0, 1), (1, 0)])  5.23 us
    convert_element_type x2, other arithmetic, sum_of(): return (a.astype(F32) + b.astype(F32) + c.astype(F32)).astype(BF)  4.23 us
  transfers between devices with their start and end apart: 32, of which 12 were waited for; matrix products, arithmetic and copies ran while one was open for 10% of the time, Pallas kernels for 26%

profile of v1, /device:TPU:0, one launch (start us, length us, event | category | flops | bytes accessed | tf_op | source)
XLA Modules:
  0.0 162.5 jit_solution(7440350711662741660)
XLA Ops:
  7.4 2.7 %collective-permute-start.1 = (bf16[2,384,128]{2,1,0:T(8,128)(2,1)S(1)}, bf16[2,384,128]{2,1,0:T(8,128)(2,1)S(1)}, u32[]{:S(2)}, u32[]{:S(2)}) collective-permute-start(bf16[2,384,128]{2,1,0:T(8,128)(2,1)S(1)} %pad_maximum_fusion.5), channel_id=1, source_target_pairs={{0,16},{8,24},{16,0},{24,8},{32,48},{40,56},{48,32},{56,40},{1,17}... | collective-permute-start | bytes 589832 | tf_op jit(solution)/shard_map/ppermute | solution.py:35
  11.6 3.2 %collective-permute-start.4 = (bf16[1024,384]{1,0:T(8,128)(2,1)S(1)}, bf16[1024,384]{1,0:T(8,128)(2,1)S(1)}, u32[]{:S(2)}, u32[]{:S(2)}) collective-permute-start(bf16[1024,384]{1,0:T(8,128)(2,1)S(1)} %get-tuple-element.46), channel_id=1, source_target_pairs={{0,64},{64,0},{1,65},{65,1},{2,66},{66,2},{3,67},{67,3},{4,68},{68... | collective-permute-start | bytes 2359304 | tf_op jit(solution)/shard_map/ppermute | solution.py:23
  18.1 2.2 %copy-done.3 = bf16[128,128,128]{2,1,0:T(8,128)(2,1)S(1)} copy-done((bf16[128,128,128]{2,1,0:T(8,128)(2,1)S(1)}, bf16[128,128,128]{2,1,0:T(8,128)(2,1)}, u32[]{:S(2)}) %copy-start.3) | copy-done | bytes 4194328
  20.3 3.7 %terms.4 = bf16[8,384,256]{2,1,0:T(8,128)(2,1)S(1)} custom-call(s32[256]{0:T(256)S(1)} %select_reduce_fusion.tab, s32[32]{0:T(128)S(1)} %mul.262.order, bf16[384,1024]{1,0:T(8,128)(2,1)S(1)} %get-tuple-element.53.gu, bf16[128,128,128]{2,1,0:T(8,128)(2,1)S(1)} %copy-done, bf16[128,128,128]{2,1,0:T(8,128)(2,1)S(1)} %copy-done.3), custom_call_target="tpu_custom_call" | custom-call | flops 1 | bytes 1 | tf_op jit(solution)/shard_map/terms/pallas_call | solution.py:96
  27.7 2.6 %collective-permute-done.4 = bf16[1024,384]{1,0:T(8,128)(2,1)S(1)} collective-permute-done((bf16[1024,384]{1,0:T(8,128)(2,1)S(1)}, bf16[1024,384]{1,0:T(8,128)(2,1)S(1)}, u32[]{:S(2)}, u32[]{:S(2)}) %collective-permute-start.4) | collective-permute-done | bytes 786464 | tf_op jit(solution)/shard_map/ppermute | solution.py:23
  31.9 4.8 %terms.5 = bf16[8,384,256]{2,1,0:T(8,128)(2,1)} custom-call(s32[256]{0:T(256)S(1)} %select_reduce_fusion.tab, s32[32]{0:T(128)S(1)} %mul.262.order, bf16[384,1024]{1,0:T(8,128)(2,1)S(1)} %get-tuple-element.53.gu, bf16[128,128,128]{2,1,0:T(8,128)(2,1)S(1)} %copy-done.1, bf16[128,128,128]{2,1,0:T(8,128)(2,1)S(1)} %copy-done.3), custom_call_target="tpu_custom_call" | custom-call | flops 1 | bytes 1 | tf_op jit(solution)/shard_map/terms/pallas_call | solution.py:96
  40.3 2.4 %collective-permute-start.10 = (bf16[8,384,256]{2,1,0:T(8,128)(2,1)}, bf16[8,384,256]{2,1,0:T(8,128)(2,1)}, u32[]{:S(2)}, u32[]{:S(2)}) collective-permute-start(bf16[8,384,256]{2,1,0:T(8,128)(2,1)} %terms.5), channel_id=1, source_target_pairs={{0,24},{8,0},{16,8},{24,16},{32,40},{40,48},{48,56},{56,32},{1,25}... | collective-permute-start | bytes 4718600 | tf_op jit(solution)/shard_map/ppermute | solution.py:35
  42.7 3.7 %terms.7 = bf16[8,384,256]{2,1,0:T(8,128)(2,1)S(1)} custom-call(s32[256]{0:T(256)S(1)} %select_reduce_fusion.tab, s32[32]{0:T(128)S(1)} %mul.262.order, bf16[384,1024]{1,0:T(8,128)(2,1)S(1)} %get-tuple-element.53.gu, bf16[128,128,128]{2,1,0:T(8,128)(2,1)S(1)} %copy-done.1, bf16[128,128,128]{2,1,0:T(8,128)(2,1)S(1)} %copy-done.3), custom_call_target="tpu_custom_call" | custom-call | flops 1 | bytes 1 | tf_op jit(solution)/shard_map/terms/pallas_call | solution.py:96
  53.7 2.2 %copy-done.2 = bf16[128,128,128]{2,1,0:T(8,128)(2,1)S(1)} copy-done((bf16[128,128,128]{2,1,0:T(8,128)(2,1)S(1)}, bf16[128,128,128]{2,1,0:T(8,128)(2,1)}, u32[]{:S(2)}) %copy-start.2) | copy-done | bytes 4194328
  58.1 3.6 %terms.6 = bf16[8,384,256]{2,1,0:T(8,128)(2,1)S(1)} custom-call(s32[256]{0:T(256)S(1)} %select_reduce_fusion.tab, s32[32]{0:T(128)S(1)} %mul.262.order, bf16[384,1024]{1,0:T(8,128)(2,1)S(1)} %get-tuple-element.53.gu, bf16[128,128,128]{2,1,0:T(8,128)(2,1)S(1)} %copy-done.2, bf16[128,128,128]{2,1,0:T(8,128)(2,1)S(1)} %copy-done.4), custom_call_target="tpu_custom_call" | custom-call | flops 1 | bytes 1 | tf_op jit(solution)/shard_map/terms/pallas_call | solution.py:96
  70.0 3.2 %collective-permute-start.21 = (bf16[16,384,128]{2,1,0:T(8,128)(2,1)S(1)}, bf16[16,384,128]{2,1,0:T(8,128)(2,1)}, u32[]{:S(2)}, u32[]{:S(2)}) collective-permute-start(bf16[16,384,128]{2,1,0:T(8,128)(2,1)S(1)} %pad_maximum_fusion.rest_0_), channel_id=1, source_target_pairs={{0,65},{1,0},{32,33},{33,96},{64,1},{65,64},{96,97},{97,32},{2,67}... | collective-permute-start | bytes 4718600 | tf_op jit(solution)/shard_map/ppermute | solution.py:35
  74.9 4.5 %collective-permute-done.9 = bf16[8,384,256]{2,1,0:T(8,128)(2,1)} collective-permute-done((bf16[8,384,256]{2,1,0:T(8,128)(2,1)}, bf16[8,384,256]{2,1,0:T(8,128)(2,1)}, u32[]{:S(2)}, u32[]{:S(2)}) %collective-permute-start.9) | collective-permute-done | bytes 1572896 | tf_op jit(solution)/shard_map/ppermute | solution.py:35
  79.4 4.2 %add_convert_fusion = bf16[8,384,256]{2,1,0:T(8,128)(2,1)} fusion(bf16[8,384,256]{2,1,0:T(8,128)(2,1)} %collective-permute-done.10, bf16[8,384,256]{2,1,0:T(8,128)(2,1)} %collective-permute-done.9, bf16[8,384,256]{2,1,0:T(8,128)(2,1)} %copy-done.5), kind=kLoop, calls=%fused_computation | loop fusion | flops 4718592 | bytes 6291456 | tf_op jit(solution)/shard_map/convert_element_type | solution.py:43
  83.6 17.8 %collective-permute-done.15.rest_2_ = bf16[16,384,128]{2,1,0:T(8,128)(2,1)} collective-permute-done((bf16[16,384,128]{2,1,0:T(8,128)(2,1)S(1)}, bf16[16,384,128]{2,1,0:T(8,128)(2,1)}, u32[]{:S(2)}, u32[]{:S(2)}) %collective-permute-start.15) | collective-permute-done | bytes 1572896 | tf_op jit(solution)/shard_map/ppermute | solution.py:35
  103.3 4.6 %collective-permute-done.21.rest_1_ = bf16[16,384,128]{2,1,0:T(8,128)(2,1)} collective-permute-done((bf16[16,384,128]{2,1,0:T(8,128)(2,1)S(1)}, bf16[16,384,128]{2,1,0:T(8,128)(2,1)}, u32[]{:S(2)}, u32[]{:S(2)}) %collective-permute-start.21) | collective-permute-done | bytes 1572896 | tf_op jit(solution)/shard_map/ppermute | solution.py:35
  112.2 4.1 %collective-permute-start.24 = (bf16[16,384,128]{2,1,0:T(8,128)(2,1)}, bf16[16,384,128]{2,1,0:T(8,128)(2,1)}, u32[]{:S(2)}, u32[]{:S(2)}) collective-permute-start(bf16[16,384,128]{2,1,0:T(8,128)(2,1)} %collective-permute-done.21.rest_1_), channel_id=1, source_target_pairs={{0,32},{32,0},{1,33},{33,1},{2,34},{34,2},{3,35},{35,3},{4,36},{36... | collective-permute-start | bytes 4718600 | tf_op jit(solution)/shard_map/ppermute | solution.py:23
  120.9 10.3 %grads_0_1_2.1 = (bf16[128,128,128]{2,1,0:T(8,128)(2,1)}, bf16[128,128,128]{2,1,0:T(8,128)(2,1)}) custom-call(s32[164]{0:T(256)S(1)} %get-tuple-element.91.lrow, s32[164]{0:T(256)S(1)} %get-tuple-element.90.lslot, s32[656]{0:T(1024)S(1)} %reshape.625.ltile, s32[16]{0:T(128)S(1)} %pad_add_fusion.1.meta, ...), custom_call_target="tpu_custom_call" | custom-call | flops 1 | bytes 1 | tf_op jit(solution)/shard_map/grads_0_1_2/pallas_call | solution.py:164
  133.5 6.5 %grads_3.1 = (bf16[128,128,128]{2,1,0:T(8,128)(2,1)}, bf16[128,128,128]{2,1,0:T(8,128)(2,1)}) custom-call(s32[164]{0:T(256)S(1)} %get-tuple-element.91.lrow, s32[164]{0:T(256)S(1)} %get-tuple-element.90.lslot, s32[656]{0:T(1024)S(1)} %reshape.625.ltile, s32[16]{0:T(128)S(1)} %pad_add_fusion.1.meta, ...), custom_call_target="tpu_custom_call", output_to_operand_aliasing={{0}: (9, {}), {1}: (10, {})} | custom-call | flops 1 | bytes 1 | tf_op jit(solution)/shard_map/grads_3/pallas_call | solution.py:164
  139.9 2.2 %collective-permute-done.19 = bf16[2,384,256]{2,1,0:T(8,128)(2,1)S(1)} collective-permute-done((bf16[2,384,256]{2,1,0:T(8,128)(2,1)S(1)}, bf16[2,384,256]{2,1,0:T(8,128)(2,1)S(1)}, u32[]{:S(2)}, u32[]{:S(2)}) %collective-permute-start.19) | collective-permute-done | bytes 393248 | tf_op jit(solution)/shard_map/ppermute | solution.py:35
  142.3 3.2 %collective-permute-start.29 = (bf16[2,384,256]{2,1,0:T(8,128)(2,1)S(1)}, bf16[2,384,256]{2,1,0:T(8,128)(2,1)S(1)}, u32[]{:S(2)}, u32[]{:S(2)}) collective-permute-start(bf16[2,384,256]{2,1,0:T(8,128)(2,1)S(1)} %get-tuple-element.81), channel_id=1, source_target_pairs={{0,6},{2,0},{4,2},{6,4},{32,34},{34,36},{36,38},{38,32},{1,7},{3,1... | collective-permute-start | bytes 1179656 | tf_op jit(solution)/shard_map/ppermute | solution.py:35
  145.6 5.6 %grads_4.1 = (bf16[128,128,128]{2,1,0:T(8,128)(2,1)}, bf16[128,128,128]{2,1,0:T(8,128)(2,1)}) custom-call(s32[164]{0:T(256)S(1)} %get-tuple-element.91.lrow, s32[164]{0:T(256)S(1)} %get-tuple-element.90.lslot, s32[656]{0:T(1024)S(1)} %reshape.625.ltile, s32[16]{0:T(128)S(1)} %pad_add_fusion.1.meta, ...), custom_call_target="tpu_custom_call", output_to_operand_aliasing={{0}: (9, {}), {1}: (10, {})} | custom-call | flops 1 | bytes 1 | tf_op jit(solution)/shard_map/grads_4/pallas_call | solution.py:164
  151.2 3.8 %collective-permute-done.25 = bf16[2,384,256]{2,1,0:T(8,128)(2,1)S(1)} collective-permute-done((bf16[2,384,256]{2,1,0:T(8,128)(2,1)S(1)}, bf16[2,384,256]{2,1,0:T(8,128)(2,1)S(1)}, u32[]{:S(2)}, u32[]{:S(2)}) %collective-permute-start.25) | collective-permute-done | bytes 393248 | tf_op jit(solution)/shard_map/ppermute | solution.py:35
  155.2 3.9 %grads_5.1 = (bf16[128,128,128]{2,1,0:T(8,128)(2,1)}, bf16[128,128,128]{2,1,0:T(8,128)(2,1)}) custom-call(s32[164]{0:T(256)S(1)} %get-tuple-element.91.lrow, s32[164]{0:T(256)S(1)} %get-tuple-element.90.lslot, s32[656]{0:T(1024)S(1)} %reshape.625.ltile, s32[16]{0:T(128)S(1)} %pad_add_fusion.1.meta, ...), custom_call_target="tpu_custom_call", output_to_operand_aliasing={{0}: (7, {}), {1}: (8, {})} | custom-call | flops 1 | bytes 1 | tf_op jit(solution)/shard_map/grads_5/pallas_call | solution.py:164
  159.1 2.6 %collective-permute-done.30 = bf16[384,256]{1,0:T(8,128)(2,1)S(1)} collective-permute-done((bf16[384,256]{1,0:T(8,128)(2,1)S(1)}, bf16[384,256]{1,0:T(8,128)(2,1)S(1)}, u32[]{:S(2)}, u32[]{:S(2)}) %collective-permute-start.30) | collective-permute-done | bytes 196640 | tf_op jit(solution)/shard_map/ppermute | solution.py:23
  (155 shorter events, 53.1 us)
Async XLA Ops:
  5.8 18.8 %collective-permute-start = (bf16[2,384,128]{2,1,0:T(8,128)(2,1)S(1)}, bf16[2,384,128]{2,1,0:T(8,128)(2,1)}, u32[]{:S(2)}, u32[]{:S(2)}) collective-permute-start(bf16[2,384,128]{2,1,0:T(8,128)(2,1)S(1)} %pad_maximum_fusion.5), channel_id=1, source_target_pairs={{0,8},{8,16},{16,24},{24,0},{32,56},{40,32},{48,40},{56,48},{1,9},... | collective-permute-start | bytes 589832 | tf_op jit(solution)/shard_map/ppermute | solution.py:35
  7.4 18.1 %collective-permute-start.1 = (bf16[2,384,128]{2,1,0:T(8,128)(2,1)S(1)}, bf16[2,384,128]{2,1,0:T(8,128)(2,1)S(1)}, u32[]{:S(2)}, u32[]{:S(2)}) collective-permute-start(bf16[2,384,128]{2,1,0:T(8,128)(2,1)S(1)} %pad_maximum_fusion.5), channel_id=1, source_target_pairs={{0,16},{8,24},{16,0},{24,8},{32,48},{40,56},{48,32},{56,40},{1,17}... | collective-permute-start | bytes 589832 | tf_op jit(solution)/shard_map/ppermute | solution.py:35
  10.2 15.4 %collective-permute-start.2 = (bf16[2,384,128]{2,1,0:T(8,128)(2,1)S(1)}, bf16[2,384,128]{2,1,0:T(8,128)(2,1)S(1)}, u32[]{:S(2)}, u32[]{:S(2)}) collective-permute-start(bf16[2,384,128]{2,1,0:T(8,128)(2,1)S(1)} %pad_maximum_fusion.5), channel_id=1, source_target_pairs={{0,24},{8,0},{16,8},{24,16},{32,40},{40,48},{48,56},{56,32},{1,25}... | collective-permute-start | bytes 589832 | tf_op jit(solution)/shard_map/ppermute | solution.py:35
  11.6 18.7 %collective-permute-start.4 = (bf16[1024,384]{1,0:T(8,128)(2,1)S(1)}, bf16[1024,384]{1,0:T(8,128)(2,1)S(1)}, u32[]{:S(2)}, u32[]{:S(2)}) collective-permute-start(bf16[1024,384]{1,0:T(8,128)(2,1)S(1)} %get-tuple-element.46), channel_id=1, source_target_pairs={{0,64},{64,0},{1,65},{65,1},{2,66},{66,2},{3,67},{67,3},{4,68},{68... | collective-permute-start | bytes 2359304 | tf_op jit(solution)/shard_map/ppermute | solution.py:23
  23.9 24.4 %collective-permute-start.8 = (bf16[8,384,256]{2,1,0:T(8,128)(2,1)S(1)}, bf16[8,384,256]{2,1,0:T(8,128)(2,1)S(1)}, u32[]{:S(2)}, u32[]{:S(2)}) collective-permute-start(bf16[8,384,256]{2,1,0:T(8,128)(2,1)S(1)} %terms.4), channel_id=1, source_target_pairs={{0,8},{8,16},{16,24},{24,0},{32,56},{40,32},{48,40},{56,48},{1,9},... | collective-permute-start | bytes 4718600 | tf_op jit(solution)/shard_map/ppermute | solution.py:35
  25.7 11.1 %collective-permute-start.3 = (bf16[4,384,128]{2,1,0:T(8,128)(2,1)S(1)}, bf16[4,384,128]{2,1,0:T(8,128)(2,1)S(1)}, u32[]{:S(2)}, u32[]{:S(2)}) collective-permute-start(bf16[4,384,128]{2,1,0:T(8,128)(2,1)S(1)} %pad_maximum_fusion.3), channel_id=1, source_target_pairs={{0,2},{2,4},{4,6},{6,0},{32,38},{34,32},{36,34},{38,36},{1,3},{3,5... | collective-permute-start | bytes 1179656 | tf_op jit(solution)/shard_map/ppermute | solution.py:35
  40.3 33.4 %collective-permute-start.10 = (bf16[8,384,256]{2,1,0:T(8,128)(2,1)}, bf16[8,384,256]{2,1,0:T(8,128)(2,1)}, u32[]{:S(2)}, u32[]{:S(2)}) collective-permute-start(bf16[8,384,256]{2,1,0:T(8,128)(2,1)} %terms.5), channel_id=1, source_target_pairs={{0,24},{8,0},{16,8},{24,16},{32,40},{40,48},{48,56},{56,32},{1,25}... | collective-permute-start | bytes 4718600 | tf_op jit(solution)/shard_map/ppermute | solution.py:35
  49.9 29.5 %collective-permute-start.9 = (bf16[8,384,256]{2,1,0:T(8,128)(2,1)}, bf16[8,384,256]{2,1,0:T(8,128)(2,1)}, u32[]{:S(2)}, u32[]{:S(2)}) collective-permute-start(bf16[8,384,256]{2,1,0:T(8,128)(2,1)} %add_convert_fusion.1), channel_id=1, source_target_pairs={{0,8},{8,16},{16,24},{24,0},{32,56},{40,32},{48,40},{56,48},{1,9},... | collective-permute-start | bytes 4718600 | tf_op jit(solution)/shard_map/ppermute | solution.py:35
  51.7 11.1 %collective-permute-start.12 = (bf16[4,384,128]{2,1,0:T(8,128)(2,1)S(1)}, bf16[4,384,128]{2,1,0:T(8,128)(2,1)}, u32[]{:S(2)}, u32[]{:S(2)}) collective-permute-start(bf16[4,384,128]{2,1,0:T(8,128)(2,1)S(1)} %collective-permute-done.7), channel_id=1, source_target_pairs={{0,1},{1,64},{32,97},{33,32},{64,65},{65,0},{96,33},{97,96},{2,3},... | collective-permute-start | bytes 1179656 | tf_op jit(solution)/shard_map/ppermute | solution.py:35
  51.7 17.0 %collective-permute-start.11 = (bf16[4,384,128]{2,1,0:T(8,128)(2,1)}, bf16[4,384,128]{2,1,0:T(8,128)(2,1)S(1)}, u32[]{:S(2)}, u32[]{:S(2)}) collective-permute-start(bf16[4,384,128]{2,1,0:T(8,128)(2,1)} %collective-permute-done.5), channel_id=1, source_target_pairs={{0,2},{2,4},{4,6},{6,0},{32,38},{34,32},{36,34},{38,36},{1,3},{3,5... | collective-permute-start | bytes 1179656 | tf_op jit(solution)/shard_map/ppermute | solution.py:35
  64.1 37.3 %collective-permute-start.15 = (bf16[16,384,128]{2,1,0:T(8,128)(2,1)S(1)}, bf16[16,384,128]{2,1,0:T(8,128)(2,1)}, u32[]{:S(2)}, u32[]{:S(2)}) collective-permute-start(bf16[16,384,128]{2,1,0:T(8,128)(2,1)S(1)} %pad_maximum_fusion.1.rest_0_), channel_id=1, source_target_pairs={{0,2},{2,4},{4,6},{6,0},{32,38},{34,32},{36,34},{38,36},{1,3},{3,5... | collective-permute-start | bytes 4718600 | tf_op jit(solution)/shard_map/ppermute | solution.py:35
  66.1 36.7 %collective-permute-start.16 = (bf16[16,384,128]{2,1,0:T(8,128)(2,1)S(1)}, bf16[16,384,128]{2,1,0:T(8,128)(2,1)}, u32[]{:S(2)}, u32[]{:S(2)}) collective-permute-start(bf16[16,384,128]{2,1,0:T(8,128)(2,1)S(1)} %pad_maximum_fusion.1.rest_0_), channel_id=1, source_target_pairs={{0,6},{2,0},{4,2},{6,4},{32,34},{34,36},{36,38},{38,32},{1,7},{3,1... | collective-permute-start | bytes 4718600 | tf_op jit(solution)/shard_map/ppermute | solution.py:35
  70.0 37.9 %collective-permute-start.21 = (bf16[16,384,128]{2,1,0:T(8,128)(2,1)S(1)}, bf16[16,384,128]{2,1,0:T(8,128)(2,1)}, u32[]{:S(2)}, u32[]{:S(2)}) collective-permute-start(bf16[16,384,128]{2,1,0:T(8,128)(2,1)S(1)} %pad_maximum_fusion.rest_0_), channel_id=1, source_target_pairs={{0,65},{1,0},{32,33},{33,96},{64,1},{65,64},{96,97},{97,32},{2,67}... | collective-permute-start | bytes 4718600 | tf_op jit(solution)/shard_map/ppermute | solution.py:35
  73.8 34.3 %collective-permute-start.20 = (bf16[16,384,128]{2,1,0:T(8,128)(2,1)S(1)}, bf16[16,384,128]{2,1,0:T(8,128)(2,1)}, u32[]{:S(2)}, u32[]{:S(2)}) collective-permute-start(bf16[16,384,128]{2,1,0:T(8,128)(2,1)S(1)} %pad_maximum_fusion.rest_0_), channel_id=1, source_target_pairs={{0,1},{1,64},{32,97},{33,32},{64,65},{65,0},{96,33},{97,96},{2,3},... | collective-permute-start | bytes 4718600 | tf_op jit(solution)/shard_map/ppermute | solution.py:35
  83.6 24.8 %collective-permute-start.14 = (bf16[16,384,128]{2,1,0:T(8,128)(2,1)S(1)}, bf16[16,384,128]{2,1,0:T(8,128)(2,1)S(1)}, u32[]{:S(2)}, u32[]{:S(2)}) collective-permute-start(bf16[16,384,128]{2,1,0:T(8,128)(2,1)S(1)} %pad_maximum_fusion.1.rest_0_), channel_id=1, source_target_pairs={{0,32},{32,0},{1,33},{33,1},{2,34},{34,2},{3,35},{35,3},{4,36},{36... | collective-permute-start | bytes 4718600 | tf_op jit(solution)/shard_map/ppermute | solution.py:23
  108.1 23.2 %collective-permute-start.22 = (bf16[16,384,128]{2,1,0:T(8,128)(2,1)}, bf16[16,384,128]{2,1,0:T(8,128)(2,1)}, u32[]{:S(2)}, u32[]{:S(2)}) collective-permute-start(bf16[16,384,128]{2,1,0:T(8,128)(2,1)} %collective-permute-done.20.rest_0_), channel_id=1, source_target_pairs={{0,1},{1,64},{32,97},{33,32},{64,65},{65,0},{96,33},{97,96},{2,3},... | collective-permute-start | bytes 4718600 | tf_op jit(solution)/shard_map/ppermute | solution.py:35
  109.5 22.4 %collective-permute-start.26 = (bf16[16,384,128]{2,1,0:T(8,128)(2,1)}, bf16[16,384,128]{2,1,0:T(8,128)(2,1)}, u32[]{:S(2)}, u32[]{:S(2)}) collective-permute-start(bf16[16,384,128]{2,1,0:T(8,128)(2,1)} %collective-permute-done.15.rest_2_), channel_id=1, source_target_pairs={{0,2},{2,4},{4,6},{6,0},{32,38},{34,32},{36,34},{38,36},{1,3},{3,5... | collective-permute-start | bytes 4718600 | tf_op jit(solution)/shard_map/ppermute | solution.py:35
  112.2 20.9 %collective-permute-start.24 = (bf16[16,384,128]{2,1,0:T(8,128)(2,1)}, bf16[16,384,128]{2,1,0:T(8,128)(2,1)}, u32[]{:S(2)}, u32[]{:S(2)}) collective-permute-start(bf16[16,384,128]{2,1,0:T(8,128)(2,1)} %collective-permute-done.21.rest_1_), channel_id=1, source_target_pairs={{0,32},{32,0},{1,33},{33,1},{2,34},{34,2},{3,35},{35,3},{4,36},{36... | collective-permute-start | bytes 4718600 | tf_op jit(solution)/shard_map/ppermute | solution.py:23
  116.4 17.1 %collective-permute-start.23 = (bf16[16,384,128]{2,1,0:T(8,128)(2,1)}, bf16[16,384,128]{2,1,0:T(8,128)(2,1)}, u32[]{:S(2)}, u32[]{:S(2)}) collective-permute-start(bf16[16,384,128]{2,1,0:T(8,128)(2,1)} %collective-permute-done.20.rest_0_), channel_id=1, source_target_pairs={{0,32},{32,0},{1,33},{33,1},{2,34},{34,2},{3,35},{35,3},{4,36},{36... | collective-permute-start | bytes 4718600 | tf_op jit(solution)/shard_map/ppermute | solution.py:23
  131.3 14.3 %collective-permute-start.28 = (bf16[16,384,128]{2,1,0:T(8,128)(2,1)}, bf16[16,384,128]{2,1,0:T(8,128)(2,1)S(1)}, u32[]{:S(2)}, u32[]{:S(2)}) collective-permute-start(bf16[16,384,128]{2,1,0:T(8,128)(2,1)} %collective-permute-done.22.rest_1_), channel_id=1, source_target_pairs={{0,32},{32,0},{1,33},{33,1},{2,34},{34,2},{3,35},{35,3},{4,36},{36... | collective-permute-start | bytes 4718600 | tf_op jit(solution)/shard_map/ppermute | solution.py:23
  131.9 13.7 %collective-permute-start.27 = (bf16[16,384,128]{2,1,0:T(8,128)(2,1)S(1)}, bf16[16,384,128]{2,1,0:T(8,128)(2,1)S(1)}, u32[]{:S(2)}, u32[]{:S(2)}) collective-permute-start(bf16[16,384,128]{2,1,0:T(8,128)(2,1)S(1)} %pad_maximum_fusion.rest_0_), channel_id=1, source_target_pairs={{0,32},{32,0},{1,33},{33,1},{2,34},{34,2},{3,35},{35,3},{4,36},{36... | collective-permute-start | bytes 4718600 | tf_op jit(solution)/shard_map/ppermute | solution.py:23
  131.9 23.3 %collective-permute-start.31 = (bf16[16,384,128]{2,1,0:T(8,128)(2,1)}, bf16[16,384,128]{2,1,0:T(8,128)(2,1)S(1)}, u32[]{:S(2)}, u32[]{:S(2)}) collective-permute-start(bf16[16,384,128]{2,1,0:T(8,128)(2,1)} %collective-permute-done.26.rest_0_), channel_id=1, source_target_pairs={{0,32},{32,0},{1,33},{33,1},{2,34},{34,2},{3,35},{35,3},{4,36},{36... | collective-permute-start | bytes 4718600 | tf_op jit(solution)/shard_map/ppermute | solution.py:23
  142.3 12.8 %collective-permute-start.25 = (bf16[2,384,256]{2,1,0:T(8,128)(2,1)S(1)}, bf16[2,384,256]{2,1,0:T(8,128)(2,1)S(1)}, u32[]{:S(2)}, u32[]{:S(2)}) collective-permute-start(bf16[2,384,256]{2,1,0:T(8,128)(2,1)S(1)} %add_convert_fusion.2), channel_id=1, source_target_pairs={{0,2},{2,4},{4,6},{6,0},{32,38},{34,32},{36,34},{38,36},{1,3},{3,5... | collective-permute-start | bytes 1179656 | tf_op jit(solution)/shard_map/ppermute | solution.py:35
  142.3 12.7 %collective-permute-start.29 = (bf16[2,384,256]{2,1,0:T(8,128)(2,1)S(1)}, bf16[2,384,256]{2,1,0:T(8,128)(2,1)S(1)}, u32[]{:S(2)}, u32[]{:S(2)}) collective-permute-start(bf16[2,384,256]{2,1,0:T(8,128)(2,1)S(1)} %get-tuple-element.81), channel_id=1, source_target_pairs={{0,6},{2,0},{4,2},{6,4},{32,34},{34,36},{36,38},{38,32},{1,7},{3,1... | collective-permute-start | bytes 1179656 | tf_op jit(solution)/shard_map/ppermute | solution.py:35
  (36 other events, 204.9 us)

commit v2 on v1

--- a/solution.py
+++ b/solution.py
@@ -56,21 +56,23 @@
     gut[128:, :] = ug.T.astype(BF)
 
 
-def chunk_kernel(k, tab, order, gu, wg, wu, out):
-    @pl.loop(0, 8)
-    def _(j):
-        base = order[k * 8 + j]
-        total = jnp.zeros((TOK, 256), F32)
-        for r in range(4):
-            sides = []
-            for side in range(2):
-                slot = tab[r * 64 + base + side]
-                index = jnp.minimum(slot, SLOTS - 1)
-                block = jnp.concatenate([wg[index], wu[index]], axis=0)
-                sides.append(jnp.where(slot < SLOTS, block, jnp.zeros_like(block)))
-            both = jnp.concatenate(sides, axis=1)
-            total += jnp.dot(gu[:, r * 256 : (r + 1) * 256], both, preferred_element_type=F32)
-        out[j] = total.astype(BF)
+def chunk_kernel(chunks, tab, order, gu, wg, wu, *outs):
+    for k, out in zip(chunks, outs):
+
+        @pl.loop(0, 8)
+        def _(j):
+            base = order[k * 8 + j]
+            total = jnp.zeros((TOK, 256), F32)
+            for r in range(4):
+                sides = []
+                for side in range(2):
+                    slot = tab[r * 64 + base + side]
+                    index = jnp.minimum(slot, SLOTS - 1)
+                    block = jnp.concatenate([wg[index], wu[index]], axis=0)
+                    sides.append(jnp.where(slot < SLOTS, block, jnp.zeros_like(block)))
+                both = jnp.concatenate(sides, axis=1)
+                total += jnp.dot(gu[:, r * 256 : (r + 1) * 256], both, preferred_element_type=F32)
+            out[j] = total.astype(BF)
 
 
 PIECE = jax.ShapeDtypeStruct((8, TOK, 256), BF)
@@ -92,12 +94,12 @@
     )(gate_pre, up_pre, hidden)
 
 
-def terms(k, tab, order, gu, wg, wu):
+def terms(chunks, tab, order, gu, wg, wu):
     return pl.pallas_call(
-        functools.partial(chunk_kernel, k),
-        out_shape=PIECE,
+        functools.partial(chunk_kernel, chunks),
+        out_shape=[PIECE] * len(chunks),
         in_specs=[SM] * 2 + [VM] * 3,
-        out_specs=VM,
+        out_specs=[VM] * len(chunks),
         compiler_params=pltpu.CompilerParams(vmem_limit_bytes=8 * 1024 * 1024),
         cost_estimate=pl.CostEstimate(flops=1, bytes_accessed=1, transcendentals=0),
         name="terms",
@@ -173,7 +175,7 @@
             pltpu.SemaphoreType.DMA,
         ],
         input_output_aliases={first + n: n for n in range(len(held))},
-        compiler_params=pltpu.CompilerParams(vmem_limit_bytes=25 * 1024 * 1024),
+        compiler_params=pltpu.CompilerParams(vmem_limit_bytes=13 * 1024 * 1024),
         cost_estimate=pl.CostEstimate(flops=1, bytes_accessed=1, transcendentals=0),
         name=name,
     )(*lists, gt, *pieces, *held)
@@ -256,21 +258,20 @@
     other = shift(gut, "yh", 1)
     both = after(jnp.stack([activations[:, :128], activations[:, 128:]]), gut)
     near = [both] + [shift(both, "x", k) for k in (1, 2, 3)]
-    t2 = terms(2, tab, order, gu, *blocks)
+    (t2,) = terms((2,), tab, order, gu, *blocks)
     ahead = shift(t2, "x", 1)
     even = after(jnp.stack([v[0] for v in near]), t2)
     odd = after(jnp.stack([v[1] for v in near]), t2, other)
     evens, odds = [even], [odd]
     evens.append(shift(even, "z", 1))
     odds.append(shift(odd, "y", 1))
-    t1 = terms(1, tab, order, after(gu, even, odd), *blocks)
+    (t1,) = terms((1,), tab, order, after(gu, even, odd), *blocks)
     back = shift(t1, "x", -1)
     evens.append(shift(after(evens[1], t1), "z", 1))
     odds.append(shift(after(odds[1], t1), "y", 1))
-    t3 = terms(3, tab, order, after(gu, evens[1], odds[1]), *blocks)
+    t3, t0 = terms((3, 0), tab, order, after(gu, evens[1], odds[1]), *blocks)
     evens.append(shift(after(evens[2], t3), "z", 1))
     odds.append(shift(after(odds[2], t3), "y", 1))
-    t0 = terms(0, tab, order, after(gu, evens[2], odds[2]), *blocks)
     moving = add(after(ahead, evens[2], odds[2]), t3)
     even_0 = after(jnp.concatenate(evens), t0, moving)
     odd_0 = after(jnp.concatenate(odds), t0, moving)
@@ -291,16 +292,13 @@
     odd_2 = shift(after(odd_1, odd_3), "z", 1)
     odd_1c, odd_3c = shift(odd_1, "c", 1), shift(odd_3, "c", 1)
     even_1c, even_3c = (shift(after(v, odd_1c, odd_3c, odd_0c), "c", 1) for v in (even_1, even_3))
-    grads = grads_of(
-        "grads_0_1_2",
-        ((0, (0, 0, 1, 1)), (1, (3, 3, 4, 4)), (2, (2, 2, 5, 5))),
-        116,
-        (odd_0, odd_0c, odd_1, odd_3, odd_1c, odd_3c),
-    )
+    grads = grads_of("grads_0", ((0, (0, 0, 1, 1)),), 40, (odd_0, odd_0c))
+    grads = grads_of("grads_1", ((1, (0, 0, 1, 1)),), 40, (odd_3, odd_1c), grads)
+    grads = grads_of("grads_2", ((2, (0, 0, 1, 1)),), 40, (odd_1, odd_3c), grads)
     even_0c = shift(after(even_0, grads[0]), "c", 1)
     even_2 = after(even_2, grads[0])
-    ahead = shift(after(mine[2], grads[0]), "z", 1)
-    back = shift(after(mine[1], grads[0]), "z", -1)
+    ahead = shift(after(mine[2], odd_3c), "z", 1)
+    back = shift(after(mine[1], odd_3c), "z", -1)
     grads = grads_of("grads_3", ((3, (0, 1, 2, 3)),), 72, (even_1, even_3, even_1c, even_3c), grads, (even_2,))
     even_2c = shift(even_2, "c", 1)
     odd_2c = shift(odd_2, "c", 1)

time: 163 us -> 162 us (level)
  waiting for transfers between devices: 41.4 us -> 49.9 us
  local copies, waits for them, and re-layouts: 22.8 us -> 17 us
  Pallas kernels: 43.2 us -> 40.6 us
  starting transfers between devices: 41.1 us -> 38.8 us
    ppermute x21, waiting for transfers between devices: 36.2 us -> 44.5 us  [shift(): return lax.ppermute(value, AXES[axis], pairs)]
    unnamed x57 -> x51, local copies, waits for them, and re-layouts: 18.5 us -> 13.7 us
    pallas_call x4 -> x6, Pallas kernels: 26.3 us -> 24.3 us  [weight_grads(): pl.pallas_call(functools.partial(kinds_kernel, kinds, len(held)), out_sha...]
    pallas_call x4 -> x3, Pallas kernels: 15.8 us -> 15.1 us  [terms(): pl.pallas_call(functools.partial(chunk_kernel, chunks), out_shape=[PIECE]...]
  transfers between devices with their start and end apart: 32 -> 32, of which waited for: 12 -> 10; matrix products, arithmetic and copies ran while one was open for 10% -> 10% of each run, Pallas kernels for 26% -> 25%
where the time goes in v2:
time: 162 us; the launch traced here: 160 us
  waiting for transfers between devices  49.9 us (31%)
  Pallas kernels  40.6 us (25%)
  starting transfers between devices  38.8 us (24%)
  local copies, waits for them, and re-layouts  17 us (10%)
  other arithmetic  12.2 us (8%)
  between operations  1.83 us (1%)
    ppermute x21, waiting for transfers between devices, shift(): return lax.ppermute(value, AXES[axis], pairs)  44.5 us
    ppermute x21, starting transfers between devices, shift(): return lax.ppermute(value, AXES[axis], pairs)  29.7 us
    pallas_call x6, Pallas kernels, weight_grads(): pl.pallas_call(functools.partial(kinds_kernel, kinds, len(held)), out_sha...  24.3 us
    pallas_call x3, Pallas kernels, terms(): pl.pallas_call(functools.partial(chunk_kernel, chunks), out_shape=[PIECE]...  15.1 us
    unnamed x51, local copies, waits for them, and re-layouts  13.7 us
    ppermute x11, starting transfers between devices, shift(): return lax.ppermute(value, axis, [(0, 1), (1, 0)])  9.09 us
    ppermute x11, waiting for transfers between devices, shift(): return lax.ppermute(value, axis, [(0, 1), (1, 0)])  5.43 us
    convert_element_type x2, other arithmetic, sum_of(): return (a.astype(F32) + b.astype(F32) + c.astype(F32)).astype(BF)  4.23 us
  transfers between devices with their start and end apart: 32, of which 10 were waited for; matrix products, arithmetic and copies ran while one was open for 10% of the time, Pallas kernels for 25%

profile of v2, /device:TPU:0, one launch (start us, length us, event | category | flops | bytes accessed | tf_op | source)
XLA Modules:
  0.0 160.3 jit_solution(15754269792460084976)
XLA Ops:
  7.4 2.7 %collective-permute-start.1 = (bf16[2,384,128]{2,1,0:T(8,128)(2,1)S(1)}, bf16[2,384,128]{2,1,0:T(8,128)(2,1)S(1)}, u32[]{:S(2)}, u32[]{:S(2)}) collective-permute-start(bf16[2,384,128]{2,1,0:T(8,128)(2,1)S(1)} %pad_maximum_fusion.5), channel_id=1, source_target_pairs={{0,16},{8,24},{16,0},{24,8},{32,48},{40,56},{48,32},{56,40},{1,17}... | collective-permute-start | bytes 589832 | tf_op jit(solution)/shard_map/ppermute | solution.py:35
  11.6 3.2 %collective-permute-start.4 = (bf16[1024,384]{1,0:T(8,128)(2,1)S(1)}, bf16[1024,384]{1,0:T(8,128)(2,1)S(1)}, u32[]{:S(2)}, u32[]{:S(2)}) collective-permute-start(bf16[1024,384]{1,0:T(8,128)(2,1)S(1)} %get-tuple-element.51), channel_id=1, source_target_pairs={{0,64},{64,0},{1,65},{65,1},{2,66},{66,2},{3,67},{67,3},{4,68},{68... | collective-permute-start | bytes 2359304 | tf_op jit(solution)/shard_map/ppermute | solution.py:23
  18.1 2.2 %copy-done.2 = bf16[128,128,128]{2,1,0:T(8,128)(2,1)S(1)} copy-done((bf16[128,128,128]{2,1,0:T(8,128)(2,1)S(1)}, bf16[128,128,128]{2,1,0:T(8,128)(2,1)}, u32[]{:S(2)}) %copy-start.2) | copy-done | bytes 4194328
  20.3 3.6 %terms.3 = bf16[8,384,256]{2,1,0:T(8,128)(2,1)S(1)} custom-call(s32[256]{0:T(256)S(1)} %select_reduce_fusion.tab, s32[32]{0:T(128)S(1)} %mul.262.order, bf16[384,1024]{1,0:T(8,128)(2,1)S(1)} %get-tuple-element.55.gu, bf16[128,128,128]{2,1,0:T(8,128)(2,1)S(1)} %copy-done, bf16[128,128,128]{2,1,0:T(8,128)(2,1)S(1)} %copy-done.2), custom_call_target="tpu_custom_call" | custom-call | flops 1 | bytes 1 | tf_op jit(solution)/shard_map/terms/pallas_call | solution.py:98
  26.8 3.5 %collective-permute-done.4 = bf16[1024,384]{1,0:T(8,128)(2,1)S(1)} collective-permute-done((bf16[1024,384]{1,0:T(8,128)(2,1)S(1)}, bf16[1024,384]{1,0:T(8,128)(2,1)S(1)}, u32[]{:S(2)}, u32[]{:S(2)}) %collective-permute-start.4) | collective-permute-done | bytes 786464 | tf_op jit(solution)/shard_map/ppermute | solution.py:23
  32.0 4.8 %terms.5 = bf16[8,384,256]{2,1,0:T(8,128)(2,1)} custom-call(s32[256]{0:T(256)S(1)} %select_reduce_fusion.tab, s32[32]{0:T(128)S(1)} %mul.262.order, bf16[384,1024]{1,0:T(8,128)(2,1)S(1)} %get-tuple-element.55.gu, bf16[128,128,128]{2,1,0:T(8,128)(2,1)S(1)} %copy-done.1, bf16[128,128,128]{2,1,0:T(8,128)(2,1)S(1)} %copy-done.2), custom_call_target="tpu_custom_call" | custom-call | flops 1 | bytes 1 | tf_op jit(solution)/shard_map/terms/pallas_call | solution.py:98
  40.3 2.3 %collective-permute-start.10 = (bf16[8,384,256]{2,1,0:T(8,128)(2,1)}, bf16[8,384,256]{2,1,0:T(8,128)(2,1)}, u32[]{:S(2)}, u32[]{:S(2)}) collective-permute-start(bf16[8,384,256]{2,1,0:T(8,128)(2,1)} %terms.5), channel_id=1, source_target_pairs={{0,24},{8,0},{16,8},{24,16},{32,40},{40,48},{48,56},{56,32},{1,25}... | collective-permute-start | bytes 4718600 | tf_op jit(solution)/shard_map/ppermute | solution.py:35
  42.6 6.7 %terms.4 = (bf16[8,384,256]{2,1,0:T(8,128)(2,1)S(1)}, bf16[8,384,256]{2,1,0:T(8,128)(2,1)S(1)}) custom-call(s32[256]{0:T(256)S(1)} %select_reduce_fusion.tab, s32[32]{0:T(128)S(1)} %mul.262.order, bf16[384,1024]{1,0:T(8,128)(2,1)S(1)} %get-tuple-element.55.gu, bf16[128,128,128]{2,1,0:T(8,128)(2,1)S(1)} %copy-done.1, bf16[128,128,128]{2,1,0:T(8,128)(2,1)S(1)} %copy-done.2), custom_call_target="tpu_custom_call" | custom-call | flops 1 | bytes 1 | tf_op jit(solution)/shard_map/terms/pallas_call | solution.py:98
  55.9 5.4 %collective-permute-done.11 = bf16[4,384,128]{2,1,0:T(8,128)(2,1)} collective-permute-done((bf16[4,384,128]{2,1,0:T(8,128)(2,1)S(1)}, bf16[4,384,128]{2,1,0:T(8,128)(2,1)}, u32[]{:S(2)}, u32[]{:S(2)}) %collective-permute-start.11) | collective-permute-done | bytes 393248 | tf_op jit(solution)/shard_map/ppermute | solution.py:35
  62.6 3.6 %collective-permute-start.12 = (bf16[16,384,128]{2,1,0:T(8,128)(2,1)S(1)}, bf16[16,384,128]{2,1,0:T(8,128)(2,1)}, u32[]{:S(2)}, u32[]{:S(2)}) collective-permute-start(bf16[16,384,128]{2,1,0:T(8,128)(2,1)S(1)} %pad_maximum_fusion.rest_0_), channel_id=1, source_target_pairs={{0,6},{2,0},{4,2},{6,4},{32,34},{34,36},{36,38},{38,32},{1,7},{3,1... | collective-permute-start | bytes 4718600 | tf_op jit(solution)/shard_map/ppermute | solution.py:35
  71.6 7.8 %collective-permute-done.9 = bf16[8,384,256]{2,1,0:T(8,128)(2,1)} collective-permute-done((bf16[8,384,256]{2,1,0:T(8,128)(2,1)}, bf16[8,384,256]{2,1,0:T(8,128)(2,1)}, u32[]{:S(2)}, u32[]{:S(2)}) %collective-permute-start.9) | collective-permute-done | bytes 1572896 | tf_op jit(solution)/shard_map/ppermute | solution.py:35
  79.4 4.2 %add_convert_fusion = bf16[8,384,256]{2,1,0:T(8,128)(2,1)} fusion(bf16[8,384,256]{2,1,0:T(8,128)(2,1)} %collective-permute-done.10, bf16[8,384,256]{2,1,0:T(8,128)(2,1)} %collective-permute-done.9, bf16[8,384,256]{2,1,0:T(8,128)(2,1)} %copy-done.5), kind=kLoop, calls=%fused_computation | loop fusion | flops 4718592 | bytes 6291456 | tf_op jit(solution)/shard_map/convert_element_type | solution.py:43
  83.6 15.0 %collective-permute-done.12.rest_0_ = bf16[16,384,128]{2,1,0:T(8,128)(2,1)} collective-permute-done((bf16[16,384,128]{2,1,0:T(8,128)(2,1)S(1)}, bf16[16,384,128]{2,1,0:T(8,128)(2,1)}, u32[]{:S(2)}, u32[]{:S(2)}) %collective-permute-start.12) | collective-permute-done | bytes 1572896 | tf_op jit(solution)/shard_map/ppermute | solution.py:35
  99.6 5.4 %collective-permute-done.17.rest_1_ = bf16[16,384,128]{2,1,0:T(8,128)(2,1)} collective-permute-done((bf16[16,384,128]{2,1,0:T(8,128)(2,1)S(1)}, bf16[16,384,128]{2,1,0:T(8,128)(2,1)}, u32[]{:S(2)}, u32[]{:S(2)}) %collective-permute-start.17) | collective-permute-done | bytes 1572896 | tf_op jit(solution)/shard_map/ppermute | solution.py:35
  110.1 4.1 %collective-permute-start.24 = (bf16[16,384,128]{2,1,0:T(8,128)(2,1)}, bf16[16,384,128]{2,1,0:T(8,128)(2,1)}, u32[]{:S(2)}, u32[]{:S(2)}) collective-permute-start(bf16[16,384,128]{2,1,0:T(8,128)(2,1)} %collective-permute-done.17.rest_1_), channel_id=1, source_target_pairs={{0,32},{32,0},{1,33},{33,1},{2,34},{34,2},{3,35},{35,3},{4,36},{36... | collective-permute-start | bytes 4718600 | tf_op jit(solution)/shard_map/ppermute | solution.py:23
  118.3 4.9 %grads_0.1 = (bf16[128,128,128]{2,1,0:T(8,128)(2,1)}, bf16[128,128,128]{2,1,0:T(8,128)(2,1)}) custom-call(s32[164]{0:T(256)S(1)} %get-tuple-element.101.lrow, s32[164]{0:T(256)S(1)} %get-tuple-element.100.lslot, s32[656]{0:T(1024)S(1)} %reshape.625.ltile, s32[16]{0:T(128)S(1)} %pad_add_fusion.1.meta, ...), custom_call_target="tpu_custom_call" | custom-call | flops 1 | bytes 1 | tf_op jit(solution)/shard_map/grads_0/pallas_call | solution.py:166
  123.2 3.4 %grads_1.1 = (bf16[128,128,128]{2,1,0:T(8,128)(2,1)}, bf16[128,128,128]{2,1,0:T(8,128)(2,1)}) custom-call(s32[164]{0:T(256)S(1)} %get-tuple-element.101.lrow, s32[164]{0:T(256)S(1)} %get-tuple-element.100.lslot, s32[656]{0:T(1024)S(1)} %reshape.625.ltile, s32[16]{0:T(128)S(1)} %pad_add_fusion.1.meta, ...), custom_call_target="tpu_custom_call", output_to_operand_aliasing={{0}: (7, {}), {1}: (8, {})} | custom-call | flops 1 | bytes 1 | tf_op jit(solution)/shard_map/grads_1/pallas_call | solution.py:166
  126.7 3.4 %grads_2.1 = (bf16[128,128,128]{2,1,0:T(8,128)(2,1)}, bf16[128,128,128]{2,1,0:T(8,128)(2,1)}) custom-call(s32[164]{0:T(256)S(1)} %get-tuple-element.101.lrow, s32[164]{0:T(256)S(1)} %get-tuple-element.100.lslot, s32[656]{0:T(1024)S(1)} %reshape.625.ltile, s32[16]{0:T(128)S(1)} %pad_add_fusion.1.meta, ...), custom_call_target="tpu_custom_call", output_to_operand_aliasing={{0}: (7, {}), {1}: (8, {})} | custom-call | flops 1 | bytes 1 | tf_op jit(solution)/shard_map/grads_2/pallas_call | solution.py:166
  131.4 5.3 %grads_3.1 = (bf16[128,128,128]{2,1,0:T(8,128)(2,1)}, bf16[128,128,128]{2,1,0:T(8,128)(2,1)}) custom-call(s32[164]{0:T(256)S(1)} %get-tuple-element.101.lrow, s32[164]{0:T(256)S(1)} %get-tuple-element.100.lslot, s32[656]{0:T(1024)S(1)} %reshape.625.ltile, s32[16]{0:T(128)S(1)} %pad_add_fusion.1.meta, ...), custom_call_target="tpu_custom_call", output_to_operand_aliasing={{0}: (9, {}), {1}: (10, {})} | custom-call | flops 1 | bytes 1 | tf_op jit(solution)/shard_map/grads_3/pallas_call | solution.py:166
  136.7 3.6 %collective-permute-done.14 = bf16[2,384,256]{2,1,0:T(8,128)(2,1)S(1)} collective-permute-done((bf16[2,384,256]{2,1,0:T(8,128)(2,1)S(1)}, bf16[2,384,256]{2,1,0:T(8,128)(2,1)S(1)}, u32[]{:S(2)}, u32[]{:S(2)}) %collective-permute-start.14) | collective-permute-done | bytes 393248 | tf_op jit(solution)/shard_map/ppermute | solution.py:35
  140.5 3.2 %collective-permute-start.29 = (bf16[2,384,256]{2,1,0:T(8,128)(2,1)S(1)}, bf16[2,384,256]{2,1,0:T(8,128)(2,1)S(1)}, u32[]{:S(2)}, u32[]{:S(2)}) collective-permute-start(bf16[2,384,256]{2,1,0:T(8,128)(2,1)S(1)} %get-tuple-element.91), channel_id=1, source_target_pairs={{0,6},{2,0},{4,2},{6,4},{32,34},{34,36},{36,38},{38,32},{1,7},{3,1... | collective-permute-start | bytes 1179656 | tf_op jit(solution)/shard_map/ppermute | solution.py:35
  143.7 3.3 %grads_4.1 = (bf16[128,128,128]{2,1,0:T(8,128)(2,1)}, bf16[128,128,128]{2,1,0:T(8,128)(2,1)}) custom-call(s32[164]{0:T(256)S(1)} %get-tuple-element.101.lrow, s32[164]{0:T(256)S(1)} %get-tuple-element.100.lslot, s32[656]{0:T(1024)S(1)} %reshape.625.ltile, s32[16]{0:T(128)S(1)} %pad_add_fusion.1.meta, ...), custom_call_target="tpu_custom_call", output_to_operand_aliasing={{0}: (9, {}), {1}: (10, {})} | custom-call | flops 1 | bytes 1 | tf_op jit(solution)/shard_map/grads_4/pallas_call | solution.py:166
  147.1 6.0 %collective-permute-done.25 = bf16[2,384,256]{2,1,0:T(8,128)(2,1)S(1)} collective-permute-done((bf16[2,384,256]{2,1,0:T(8,128)(2,1)S(1)}, bf16[2,384,256]{2,1,0:T(8,128)(2,1)S(1)}, u32[]{:S(2)}, u32[]{:S(2)}) %collective-permute-start.25) | collective-permute-done | bytes 393248 | tf_op jit(solution)/shard_map/ppermute | solution.py:35
  153.8 3.9 %grads_5.1 = (bf16[128,128,128]{2,1,0:T(8,128)(2,1)}, bf16[128,128,128]{2,1,0:T(8,128)(2,1)}) custom-call(s32[164]{0:T(256)S(1)} %get-tuple-element.101.lrow, s32[164]{0:T(256)S(1)} %get-tuple-element.100.lslot, s32[656]{0:T(1024)S(1)} %reshape.625.ltile, s32[16]{0:T(128)S(1)} %pad_add_fusion.1.meta, ...), custom_call_target="tpu_custom_call", output_to_operand_aliasing={{0}: (7, {}), {1}: (8, {})} | custom-call | flops 1 | bytes 1 | tf_op jit(solution)/shard_map/grads_5/pallas_call | solution.py:166
  (150 shorter events, 46.9 us)
Async XLA Ops:
  5.8 18.8 %collective-permute-start = (bf16[2,384,128]{2,1,0:T(8,128)(2,1)S(1)}, bf16[2,384,128]{2,1,0:T(8,128)(2,1)S(1)}, u32[]{:S(2)}, u32[]{:S(2)}) collective-permute-start(bf16[2,384,128]{2,1,0:T(8,128)(2,1)S(1)} %pad_maximum_fusion.5), channel_id=1, source_target_pairs={{0,8},{8,16},{16,24},{24,0},{32,56},{40,32},{48,40},{56,48},{1,9},... | collective-permute-start | bytes 589832 | tf_op jit(solution)/shard_map/ppermute | solution.py:35
  7.4 17.2 %collective-permute-start.1 = (bf16[2,384,128]{2,1,0:T(8,128)(2,1)S(1)}, bf16[2,384,128]{2,1,0:T(8,128)(2,1)S(1)}, u32[]{:S(2)}, u32[]{:S(2)}) collective-permute-start(bf16[2,384,128]{2,1,0:T(8,128)(2,1)S(1)} %pad_maximum_fusion.5), channel_id=1, source_target_pairs={{0,16},{8,24},{16,0},{24,8},{32,48},{40,56},{48,32},{56,40},{1,17}... | collective-permute-start | bytes 589832 | tf_op jit(solution)/shard_map/ppermute | solution.py:35
  10.2 14.5 %collective-permute-start.2 = (bf16[2,384,128]{2,1,0:T(8,128)(2,1)S(1)}, bf16[2,384,128]{2,1,0:T(8,128)(2,1)S(1)}, u32[]{:S(2)}, u32[]{:S(2)}) collective-permute-start(bf16[2,384,128]{2,1,0:T(8,128)(2,1)S(1)} %pad_maximum_fusion.5), channel_id=1, source_target_pairs={{0,24},{8,0},{16,8},{24,16},{32,40},{40,48},{48,56},{56,32},{1,25}... | collective-permute-start | bytes 589832 | tf_op jit(solution)/shard_map/ppermute | solution.py:35
  11.6 18.7 %collective-permute-start.4 = (bf16[1024,384]{1,0:T(8,128)(2,1)S(1)}, bf16[1024,384]{1,0:T(8,128)(2,1)S(1)}, u32[]{:S(2)}, u32[]{:S(2)}) collective-permute-start(bf16[1024,384]{1,0:T(8,128)(2,1)S(1)} %get-tuple-element.51), channel_id=1, source_target_pairs={{0,64},{64,0},{1,65},{65,1},{2,66},{66,2},{3,67},{67,3},{4,68},{68... | collective-permute-start | bytes 2359304 | tf_op jit(solution)/shard_map/ppermute | solution.py:23
  23.9 26.7 %collective-permute-start.6 = (bf16[8,384,256]{2,1,0:T(8,128)(2,1)S(1)}, bf16[8,384,256]{2,1,0:T(8,128)(2,1)S(1)}, u32[]{:S(2)}, u32[]{:S(2)}) collective-permute-start(bf16[8,384,256]{2,1,0:T(8,128)(2,1)S(1)} %terms.3), channel_id=1, source_target_pairs={{0,8},{8,16},{16,24},{24,0},{32,56},{40,32},{48,40},{56,48},{1,9},... | collective-permute-start | bytes 4718600 | tf_op jit(solution)/shard_map/ppermute | solution.py:35
  24.7 12.1 %collective-permute-start.3 = (bf16[4,384,128]{2,1,0:T(8,128)(2,1)S(1)}, bf16[4,384,128]{2,1,0:T(8,128)(2,1)S(1)}, u32[]{:S(2)}, u32[]{:S(2)}) collective-permute-start(bf16[4,384,128]{2,1,0:T(8,128)(2,1)S(1)} %pad_maximum_fusion.3), channel_id=1, source_target_pairs={{0,2},{2,4},{4,6},{6,0},{32,38},{34,32},{36,34},{38,36},{1,3},{3,5... | collective-permute-start | bytes 1179656 | tf_op jit(solution)/shard_map/ppermute | solution.py:35
  36.8 13.8 %collective-permute-start.7 = (bf16[4,384,128]{2,1,0:T(8,128)(2,1)S(1)}, bf16[4,384,128]{2,1,0:T(8,128)(2,1)}, u32[]{:S(2)}, u32[]{:S(2)}) collective-permute-start(bf16[4,384,128]{2,1,0:T(8,128)(2,1)S(1)} %collective-permute-done.3), channel_id=1, source_target_pairs={{0,2},{2,4},{4,6},{6,0},{32,38},{34,32},{36,34},{38,36},{1,3},{3,5... | collective-permute-start | bytes 1179656 | tf_op jit(solution)/shard_map/ppermute | solution.py:35
  40.3 31.0 %collective-permute-start.10 = (bf16[8,384,256]{2,1,0:T(8,128)(2,1)}, bf16[8,384,256]{2,1,0:T(8,128)(2,1)}, u32[]{:S(2)}, u32[]{:S(2)}) collective-permute-start(bf16[8,384,256]{2,1,0:T(8,128)(2,1)} %terms.5), channel_id=1, source_target_pairs={{0,24},{8,0},{16,8},{24,16},{32,40},{40,48},{48,56},{56,32},{1,25}... | collective-permute-start | bytes 4718600 | tf_op jit(solution)/shard_map/ppermute | solution.py:35
  52.2 27.2 %collective-permute-start.9 = (bf16[8,384,256]{2,1,0:T(8,128)(2,1)}, bf16[8,384,256]{2,1,0:T(8,128)(2,1)}, u32[]{:S(2)}, u32[]{:S(2)}) collective-permute-start(bf16[8,384,256]{2,1,0:T(8,128)(2,1)} %add_convert_fusion.1), channel_id=1, source_target_pairs={{0,8},{8,16},{16,24},{24,0},{32,56},{40,32},{48,40},{56,48},{1,9},... | collective-permute-start | bytes 4718600 | tf_op jit(solution)/shard_map/ppermute | solution.py:35
  54.1 13.6 %collective-permute-start.15 = (bf16[4,384,128]{2,1,0:T(8,128)(2,1)}, bf16[4,384,128]{2,1,0:T(8,128)(2,1)S(1)}, u32[]{:S(2)}, u32[]{:S(2)}) collective-permute-start(bf16[4,384,128]{2,1,0:T(8,128)(2,1)} %collective-permute-done.7), channel_id=1, source_target_pairs={{0,2},{2,4},{4,6},{6,0},{32,38},{34,32},{36,34},{38,36},{1,3},{3,5... | collective-permute-start | bytes 1179656 | tf_op jit(solution)/shard_map/ppermute | solution.py:35
  62.6 35.9 %collective-permute-start.12 = (bf16[16,384,128]{2,1,0:T(8,128)(2,1)S(1)}, bf16[16,384,128]{2,1,0:T(8,128)(2,1)}, u32[]{:S(2)}, u32[]{:S(2)}) collective-permute-start(bf16[16,384,128]{2,1,0:T(8,128)(2,1)S(1)} %pad_maximum_fusion.rest_0_), channel_id=1, source_target_pairs={{0,6},{2,0},{4,2},{6,4},{32,34},{34,36},{36,38},{38,32},{1,7},{3,1... | collective-permute-start | bytes 4718600 | tf_op jit(solution)/shard_map/ppermute | solution.py:35
  66.3 32.9 %collective-permute-start.20 = (bf16[16,384,128]{2,1,0:T(8,128)(2,1)S(1)}, bf16[16,384,128]{2,1,0:T(8,128)(2,1)}, u32[]{:S(2)}, u32[]{:S(2)}) collective-permute-start(bf16[16,384,128]{2,1,0:T(8,128)(2,1)S(1)} %pad_maximum_fusion.rest_0_), channel_id=1, source_target_pairs={{0,2},{2,4},{4,6},{6,0},{32,38},{34,32},{36,34},{38,36},{1,3},{3,5... | collective-permute-start | bytes 4718600 | tf_op jit(solution)/shard_map/ppermute | solution.py:35
  68.8 36.1 %collective-permute-start.17 = (bf16[16,384,128]{2,1,0:T(8,128)(2,1)S(1)}, bf16[16,384,128]{2,1,0:T(8,128)(2,1)}, u32[]{:S(2)}, u32[]{:S(2)}) collective-permute-start(bf16[16,384,128]{2,1,0:T(8,128)(2,1)S(1)} %pad_maximum_fusion.1.rest_0_), channel_id=1, source_target_pairs={{0,65},{1,0},{32,33},{33,96},{64,1},{65,64},{96,97},{97,32},{2,67}... | collective-permute-start | bytes 4718600 | tf_op jit(solution)/shard_map/ppermute | solution.py:35
  71.3 33.6 %collective-permute-start.16 = (bf16[16,384,128]{2,1,0:T(8,128)(2,1)S(1)}, bf16[16,384,128]{2,1,0:T(8,128)(2,1)}, u32[]{:S(2)}, u32[]{:S(2)}) collective-permute-start(bf16[16,384,128]{2,1,0:T(8,128)(2,1)S(1)} %pad_maximum_fusion.1.rest_0_), channel_id=1, source_target_pairs={{0,1},{1,64},{32,97},{33,32},{64,65},{65,0},{96,33},{97,96},{2,3},... | collective-permute-start | bytes 4718600 | tf_op jit(solution)/shard_map/ppermute | solution.py:35
  83.5 22.1 %collective-permute-start.22 = (bf16[16,384,128]{2,1,0:T(8,128)(2,1)S(1)}, bf16[16,384,128]{2,1,0:T(8,128)(2,1)S(1)}, u32[]{:S(2)}, u32[]{:S(2)}) collective-permute-start(bf16[16,384,128]{2,1,0:T(8,128)(2,1)S(1)} %pad_maximum_fusion.rest_0_), channel_id=1, source_target_pairs={{0,32},{32,0},{1,33},{33,1},{2,34},{34,2},{3,35},{35,3},{4,36},{36... | collective-permute-start | bytes 4718600 | tf_op jit(solution)/shard_map/ppermute | solution.py:23
  104.9 25.2 %collective-permute-start.18 = (bf16[16,384,128]{2,1,0:T(8,128)(2,1)}, bf16[16,384,128]{2,1,0:T(8,128)(2,1)}, u32[]{:S(2)}, u32[]{:S(2)}) collective-permute-start(bf16[16,384,128]{2,1,0:T(8,128)(2,1)} %collective-permute-done.16.rest_0_), channel_id=1, source_target_pairs={{0,1},{1,64},{32,97},{33,32},{64,65},{65,0},{96,33},{97,96},{2,3},... | collective-permute-start | bytes 4718600 | tf_op jit(solution)/shard_map/ppermute | solution.py:35
  106.8 24.0 %collective-permute-start.26 = (bf16[16,384,128]{2,1,0:T(8,128)(2,1)}, bf16[16,384,128]{2,1,0:T(8,128)(2,1)}, u32[]{:S(2)}, u32[]{:S(2)}) collective-permute-start(bf16[16,384,128]{2,1,0:T(8,128)(2,1)} %collective-permute-done.20.rest_0_), channel_id=1, source_target_pairs={{0,2},{2,4},{4,6},{6,0},{32,38},{34,32},{36,34},{38,36},{1,3},{3,5... | collective-permute-start | bytes 4718600 | tf_op jit(solution)/shard_map/ppermute | solution.py:35
  110.1 21.1 %collective-permute-start.24 = (bf16[16,384,128]{2,1,0:T(8,128)(2,1)}, bf16[16,384,128]{2,1,0:T(8,128)(2,1)}, u32[]{:S(2)}, u32[]{:S(2)}) collective-permute-start(bf16[16,384,128]{2,1,0:T(8,128)(2,1)} %collective-permute-done.17.rest_1_), channel_id=1, source_target_pairs={{0,32},{32,0},{1,33},{33,1},{2,34},{34,2},{3,35},{35,3},{4,36},{36... | collective-permute-start | bytes 4718600 | tf_op jit(solution)/shard_map/ppermute | solution.py:23
  114.4 17.0 %collective-permute-start.23 = (bf16[16,384,128]{2,1,0:T(8,128)(2,1)}, bf16[16,384,128]{2,1,0:T(8,128)(2,1)}, u32[]{:S(2)}, u32[]{:S(2)}) collective-permute-start(bf16[16,384,128]{2,1,0:T(8,128)(2,1)} %collective-permute-done.16.rest_0_), channel_id=1, source_target_pairs={{0,32},{32,0},{1,33},{33,1},{2,34},{34,2},{3,35},{35,3},{4,36},{36... | collective-permute-start | bytes 4718600 | tf_op jit(solution)/shard_map/ppermute | solution.py:23
  130.1 13.6 %collective-permute-start.28 = (bf16[16,384,128]{2,1,0:T(8,128)(2,1)}, bf16[16,384,128]{2,1,0:T(8,128)(2,1)S(1)}, u32[]{:S(2)}, u32[]{:S(2)}) collective-permute-start(bf16[16,384,128]{2,1,0:T(8,128)(2,1)} %collective-permute-done.18.rest_1_), channel_id=1, source_target_pairs={{0,32},{32,0},{1,33},{33,1},{2,34},{34,2},{3,35},{35,3},{4,36},{36... | collective-permute-start | bytes 4718600 | tf_op jit(solution)/shard_map/ppermute | solution.py:23
  130.7 13.1 %collective-permute-start.27 = (bf16[16,384,128]{2,1,0:T(8,128)(2,1)S(1)}, bf16[16,384,128]{2,1,0:T(8,128)(2,1)S(1)}, u32[]{:S(2)}, u32[]{:S(2)}) collective-permute-start(bf16[16,384,128]{2,1,0:T(8,128)(2,1)S(1)} %pad_maximum_fusion.1.rest_0_), channel_id=1, source_target_pairs={{0,32},{32,0},{1,33},{33,1},{2,34},{34,2},{3,35},{35,3},{4,36},{36... | collective-permute-start | bytes 4718600 | tf_op jit(solution)/shard_map/ppermute | solution.py:23
  130.8 23.0 %collective-permute-start.31 = (bf16[16,384,128]{2,1,0:T(8,128)(2,1)}, bf16[16,384,128]{2,1,0:T(8,128)(2,1)S(1)}, u32[]{:S(2)}, u32[]{:S(2)}) collective-permute-start(bf16[16,384,128]{2,1,0:T(8,128)(2,1)} %collective-permute-done.26.rest_0_), channel_id=1, source_target_pairs={{0,32},{32,0},{1,33},{33,1},{2,34},{34,2},{3,35},{35,3},{4,36},{36... | collective-permute-start | bytes 4718600 | tf_op jit(solution)/shard_map/ppermute | solution.py:23
  140.4 12.6 %collective-permute-start.25 = (bf16[2,384,256]{2,1,0:T(8,128)(2,1)S(1)}, bf16[2,384,256]{2,1,0:T(8,128)(2,1)S(1)}, u32[]{:S(2)}, u32[]{:S(2)}) collective-permute-start(bf16[2,384,256]{2,1,0:T(8,128)(2,1)S(1)} %add_convert_fusion.2), channel_id=1, source_target_pairs={{0,2},{2,4},{4,6},{6,0},{32,38},{34,32},{36,34},{38,36},{1,3},{3,5... | collective-permute-start | bytes 1179656 | tf_op jit(solution)/shard_map/ppermute | solution.py:35
  140.5 12.5 %collective-permute-start.29 = (bf16[2,384,256]{2,1,0:T(8,128)(2,1)S(1)}, bf16[2,384,256]{2,1,0:T(8,128)(2,1)S(1)}, u32[]{:S(2)}, u32[]{:S(2)}) collective-permute-start(bf16[2,384,256]{2,1,0:T(8,128)(2,1)S(1)} %get-tuple-element.91), channel_id=1, source_target_pairs={{0,6},{2,0},{4,2},{6,4},{32,34},{34,36},{36,38},{38,32},{1,7},{3,1... | collective-permute-start | bytes 1179656 | tf_op jit(solution)/shard_map/ppermute | solution.py:35
  (33 other events, 219.7 us)

commit v3 on v2

--- a/solution.py
+++ b/solution.py
@@ -116,13 +116,13 @@
         pltpu.make_async_copy(zero, grads.at[0], sem).wait()
 
 
-def same_row_pairs(kind, origin, refs, groups, lrow, lslot, ltile, meta, gt, gate, up, gbuf, ubuf, sem):
+def same_row_pairs(kind, origin, refs, groups, lrow, lslot, ltile, meta, gts, gate, up, gbuf, ubuf, sem):
     @pl.loop(meta[kind], meta[kind + 1])
     def _(step):
         for pair in range(2):
             pos = step * 4 + pair * 2
             rows = pl.ds(pl.multiple_of(lrow[pos] * 256, 256), 256)
-            left = jnp.concatenate([gt[g, rows, :] for g in groups], axis=1)
+            left = jnp.concatenate([gts[n // 2][g, rows, :] for n, g in enumerate(groups)], axis=1)
             sides = []
             for side in range(2):
                 tiles = [ref[ltile[(pos + side) * 4 + n]] for n, ref in enumerate(refs)]
@@ -140,7 +140,7 @@
                 put(ubuf.at[pos - origin], up, lslot[pos], sem)
 
 
-def kinds_kernel(kinds, held, lrow, lslot, ltile, meta, gt, *rest):
+def kinds_kernel(kinds, held, lrow, lslot, ltile, meta, gt, gt_c, *rest):
     pieces, (gate, up, gbuf, ubuf, zero, sem) = rest[: len(rest) - 6 - held], rest[-6:]
     origin = meta[kinds[0][0]] * 4
     if not held:
@@ -155,18 +155,18 @@
     for kind, picks in kinds:
         refs = [pieces[n] for n in picks]
         flip = meta[7]
-        groups = (flip, 1 - flip, 3 - flip, 2 + flip) if kind == 3 else (0, 1, 2, 3)
-        same_row_pairs(kind, origin, refs, groups, lrow, lslot, ltile, meta, gt, gate, up, gbuf, ubuf, sem)
+        groups = (flip, 1 - flip, 1 - flip, flip) if kind == 3 else (0, 1, 0, 1)
+        same_row_pairs(kind, origin, refs, groups, lrow, lslot, ltile, meta, (gt, gt_c), gate, up, gbuf, ubuf, sem)
     finish(2 * (meta[9 + kinds[-1][0] + 1] - meta[9 + kinds[0][0]]), zero, gate, sem)
 
 
-def weight_grads(name, kinds, room, lists, gt, pieces, held=()):
+def weight_grads(name, kinds, room, lists, gts, pieces, held=()):
     grads = jax.ShapeDtypeStruct((SLOTS, 128, 128), BF)
-    first = 5 + len(pieces)
+    first = 6 + len(pieces)
     return pl.pallas_call(
         functools.partial(kinds_kernel, kinds, len(held)),
         out_shape=[grads] * 2,
-        in_specs=[SM] * 4 + [VM] * (1 + len(pieces)) + [ANY] * len(held),
+        in_specs=[SM] * 4 + [VM] * (2 + len(pieces)) + [ANY] * len(held),
         out_specs=[ANY] * 2,
         scratch_shapes=[
             pltpu.VMEM((room, 128, 128), BF),
@@ -178,7 +178,7 @@
         compiler_params=pltpu.CompilerParams(vmem_limit_bytes=13 * 1024 * 1024),
         cost_estimate=pl.CostEstimate(flops=1, bytes_accessed=1, transcendentals=0),
         name=name,
-    )(*lists, gt, *pieces, *held)
+    )(*lists, *gts, *pieces, *held)
 
 
 def block_table(block_rows, block_cols, block_count):
@@ -281,36 +281,37 @@
     rows_late, cols_late, count_late = (after(v, even_0, odd_0) for v in (block_rows, block_cols, block_count))
     lrow, lslot, ltile, meta = slot_lists(rows_late, cols_late, count_late)
     mine = sum_of(t0, ahead, back).reshape(4, 2, TOK, 256)
-    own = after(jnp.stack([gut, other]), mine)
-    gt = jnp.concatenate([own, shift(own, "c", 1)])
-    odd_0c = shift(after(odd_0, mine), "c", 1)
+    own = jnp.stack([gut, other])
+    own_c = shift(own, "c", 1)
+    odd_0c = shift(after(odd_0, mine, own_c), "c", 1)
 
     def grads_of(name, kinds, room, pieces, held=(), wait=()):
-        return weight_grads(name, kinds, room, (lrow, lslot, ltile, after(meta, *wait)), gt, pieces, held)
+        return weight_grads(name, kinds, room, (lrow, lslot, ltile, after(meta, *wait)), (own, own_c), pieces, held)
 
     even_2 = shift(after(even_1, even_3), "y", 1)
     odd_2 = shift(after(odd_1, odd_3), "z", 1)
     odd_1c, odd_3c = shift(odd_1, "c", 1), shift(odd_3, "c", 1)
     even_1c, even_3c = (shift(after(v, odd_1c, odd_3c, odd_0c), "c", 1) for v in (even_1, even_3))
+    ahead = shift(after(mine[2], odd_3c), "z", 1)
+    back = shift(after(mine[1], odd_3c), "z", -1)
+    ahead = add(ahead, mine[3])
     grads = grads_of("grads_0", ((0, (0, 0, 1, 1)),), 40, (odd_0, odd_0c))
     grads = grads_of("grads_1", ((1, (0, 0, 1, 1)),), 40, (odd_3, odd_1c), grads)
-    grads = grads_of("grads_2", ((2, (0, 0, 1, 1)),), 40, (odd_1, odd_3c), grads)
+    grads = grads_of("grads_2", ((2, (0, 0, 1, 1)),), 40, (odd_1, odd_3c), grads, (ahead,))
+    ahead = shift(ahead, "z", 1)
     even_0c = shift(after(even_0, grads[0]), "c", 1)
     even_2 = after(even_2, grads[0])
-    ahead = shift(after(mine[2], odd_3c), "z", 1)
-    back = shift(after(mine[1], odd_3c), "z", -1)
-    grads = grads_of("grads_3", ((3, (0, 1, 2, 3)),), 72, (even_1, even_3, even_1c, even_3c), grads, (even_2,))
+    grads = grads_of("grads_3", ((3, (0, 1, 2, 3)),), 72, (even_1, even_3, even_1c, even_3c), grads, (even_2, back))
     even_2c = shift(even_2, "c", 1)
     odd_2c = shift(odd_2, "c", 1)
-    ahead = add(after(ahead, grads[0]), mine[3])
-    grads = grads_of(
-        "grads_4", ((4, (0, 1, 2, 3)),), 72, (even_0, even_2, even_0c, even_2c), grads, (ahead, odd_2)
-    )
-    ahead = after(shift(ahead, "z", 1), grads[0])
+    ahead = after(ahead, grads[0])
     send = sum_of(mine[0, 1], ahead[1], back[1])
     keep = mine[0, 0].astype(F32) + ahead[0].astype(F32) + back[0].astype(F32)
-    gate_grad, up_grad = grads_of("grads_5", ((5, (0, 0, 1, 1)),), 40, (odd_2, odd_2c), grads, (send,))
-    input_grad = (keep + after(shift(send, "yl", 1), gate_grad).astype(F32)).astype(BF)
+    grads = grads_of(
+        "grads_4", ((4, (0, 1, 2, 3)),), 72, (even_0, even_2, even_0c, even_2c), grads, (send, odd_2)
+    )
+    gate_grad, up_grad = grads_of("grads_5", ((5, (0, 0, 1, 1)),), 40, (odd_2, odd_2c), grads)
+    input_grad = (keep + after(shift(send, "yl", 1), grads[0]).astype(F32)).astype(BF)
     return input_grad, gate_grad, up_grad
 
 

time: 162 us -> 170 us (1.049)
  the two profiles are of different devices: /device:TPU:0 before, /device:TPU:10 now
where the time goes in v3:
time: 170 us; the launch traced here: 169 us
  Pallas kernels  52 us (31%)
  starting transfers between devices  44.3 us (26%)
  waiting for transfers between devices  40.5 us (24%)
  local copies, waits for them, and re-layouts  17.2 us (10%)
  other arithmetic  13.2 us (8%)
  between operations  1.99 us (1%)
    pallas_call x6, Pallas kernels, weight_grads(): pl.pallas_call(functools.partial(kinds_kernel, kinds, len(held)), out_sha...  35.6 us
    ppermute x21, waiting for transfers between devices, shift(): return lax.ppermute(value, AXES[axis], pairs)  34.2 us
    ppermute x21, starting transfers between devices, shift(): return lax.ppermute(value, AXES[axis], pairs)  28.2 us
    ppermute x11, starting transfers between devices, shift(): return lax.ppermute(value, axis, [(0, 1), (1, 0)])  16 us
    pallas_call x3, Pallas kernels, terms(): pl.pallas_call(functools.partial(chunk_kernel, chunks), out_shape=[PIECE]...  15.2 us
    unnamed x52, local copies, waits for them, and re-layouts  13.4 us
    ppermute x11, waiting for transfers between devices, shift(): return lax.ppermute(value, axis, [(0, 1), (1, 0)])  6.26 us
  transfers between devices with their start and end apart: 32, of which 8 were waited for; matrix products, arithmetic and copies ran while one was open for 9% of the time, Pallas kernels for 27%

profile of v3, /device:TPU:10, one launch (start us, length us, event | category | flops | bytes accessed | tf_op | source)
XLA Modules:
  0.0 169.1 jit_solution(14071726750669490986)
XLA Ops:
  10.6 2.3 %collective-permute-start.4 = (bf16[1024,384]{1,0:T(8,128)(2,1)S(1)}, bf16[1024,384]{1,0:T(8,128)(2,1)S(1)}, u32[]{:S(2)}, u32[]{:S(2)}) collective-permute-start(bf16[1024,384]{1,0:T(8,128)(2,1)S(1)} %get-tuple-element.49), channel_id=1, source_target_pairs={{0,64},{64,0},{1,65},{65,1},{2,66},{66,2},{3,67},{67,3},{4,68},{68... | collective-permute-start | bytes 2359304 | tf_op jit(solution)/shard_map/ppermute | solution.py:23
  14.0 2.2 %copy-done = bf16[128,128,128]{2,1,0:T(8,128)(2,1)S(1)} copy-done((bf16[128,128,128]{2,1,0:T(8,128)(2,1)S(1)}, bf16[128,128,128]{2,1,0:T(8,128)(2,1)}, u32[]{:S(2)}) %copy-start) | copy-done | bytes 4194328
  16.2 2.2 %copy-done.2 = bf16[128,128,128]{2,1,0:T(8,128)(2,1)S(1)} copy-done((bf16[128,128,128]{2,1,0:T(8,128)(2,1)S(1)}, bf16[128,128,128]{2,1,0:T(8,128)(2,1)}, u32[]{:S(2)}) %copy-start.2) | copy-done | bytes 4194328
  18.4 3.6 %terms.3 = bf16[8,384,256]{2,1,0:T(8,128)(2,1)S(1)} custom-call(s32[256]{0:T(256)S(1)} %select_reduce_fusion.tab, s32[32]{0:T(128)S(1)} %mul.262.order, bf16[384,1024]{1,0:T(8,128)(2,1)S(1)} %get-tuple-element.53.gu, bf16[128,128,128]{2,1,0:T(8,128)(2,1)S(1)} %copy-done, bf16[128,128,128]{2,1,0:T(8,128)(2,1)S(1)} %copy-done.2), custom_call_target="tpu_custom_call" | custom-call | flops 1 | bytes 1 | tf_op jit(solution)/shard_map/terms/pallas_call | solution.py:98
  24.4 6.2 %collective-permute-done.4 = bf16[1024,384]{1,0:T(8,128)(2,1)S(1)} collective-permute-done((bf16[1024,384]{1,0:T(8,128)(2,1)S(1)}, bf16[1024,384]{1,0:T(8,128)(2,1)S(1)}, u32[]{:S(2)}, u32[]{:S(2)}) %collective-permute-start.4) | collective-permute-done | bytes 786464 | tf_op jit(solution)/shard_map/ppermute | solution.py:23
  32.2 4.8 %terms.5 = bf16[8,384,256]{2,1,0:T(8,128)(2,1)} custom-call(s32[256]{0:T(256)S(1)} %select_reduce_fusion.tab, s32[32]{0:T(128)S(1)} %mul.262.order, bf16[384,1024]{1,0:T(8,128)(2,1)S(1)} %get-tuple-element.53.gu, bf16[128,128,128]{2,1,0:T(8,128)(2,1)S(1)} %copy-done.1, bf16[128,128,128]{2,1,0:T(8,128)(2,1)S(1)} %copy-done.2), custom_call_target="tpu_custom_call" | custom-call | flops 1 | bytes 1 | tf_op jit(solution)/shard_map/terms/pallas_call | solution.py:98
  41.3 6.8 %terms.4 = (bf16[8,384,256]{2,1,0:T(8,128)(2,1)S(1)}, bf16[8,384,256]{2,1,0:T(8,128)(2,1)S(1)}) custom-call(s32[256]{0:T(256)S(1)} %select_reduce_fusion.tab, s32[32]{0:T(128)S(1)} %mul.262.order, bf16[384,1024]{1,0:T(8,128)(2,1)S(1)} %get-tuple-element.53.gu, bf16[128,128,128]{2,1,0:T(8,128)(2,1)S(1)} %copy-done.1, bf16[128,128,128]{2,1,0:T(8,128)(2,1)S(1)} %copy-done.2), custom_call_target="tpu_custom_call" | custom-call | flops 1 | bytes 1 | tf_op jit(solution)/shard_map/terms/pallas_call | solution.py:98
  55.0 4.9 %collective-permute-done.11 = bf16[4,384,128]{2,1,0:T(8,128)(2,1)} collective-permute-done((bf16[4,384,128]{2,1,0:T(8,128)(2,1)}, bf16[4,384,128]{2,1,0:T(8,128)(2,1)}, u32[]{:S(2)}, u32[]{:S(2)}) %collective-permute-start.11) | collective-permute-done | bytes 393248 | tf_op jit(solution)/shard_map/ppermute | solution.py:35
  59.9 2.5 %pad_maximum_fusion.rest_0_ = bf16[16,384,128]{2,1,0:T(8,128)(2,1)} fusion(bf16[4,384,128]{2,1,0:T(8,128)(2,1)} %collective-permute-done.11, bf16[4,384,128]{2,1,0:T(8,128)(2,1)} %collective-permute-done.8, bf16[4,384,128]{2,1,0:T(8,128)(2,1)S(1)} %copy-done.23, bf16[4,384,128]{2,1,0:T(8,128)(2,1)S(1)} %copy-done.19), kind=kLoop, calls=%fused_computation.2 | loop fusion | flops 2359296 | bytes 3145728 | tf_op jit(solution)/shard_map/concatenate | solution.py:277
  62.4 3.8 %collective-permute-start.12 = (bf16[16,384,128]{2,1,0:T(8,128)(2,1)}, bf16[16,384,128]{2,1,0:T(8,128)(2,1)}, u32[]{:S(2)}, u32[]{:S(2)}) collective-permute-start(bf16[16,384,128]{2,1,0:T(8,128)(2,1)} %pad_maximum_fusion.rest_0_), channel_id=1, source_target_pairs={{0,6},{2,0},{4,2},{6,4},{32,34},{34,36},{36,38},{38,32},{1,7},{3,1... | collective-permute-start | bytes 4718600 | tf_op jit(solution)/shard_map/ppermute | solution.py:35
  66.2 2.4 %pad_maximum_fusion.1.rest_0_ = bf16[16,384,128]{2,1,0:T(8,128)(2,1)} fusion(bf16[4,384,128]{2,1,0:T(8,128)(2,1)S(1)} %collective-permute-done.16, bf16[4,384,128]{2,1,0:T(8,128)(2,1)} %collective-permute-done.7, bf16[4,384,128]{2,1,0:T(8,128)(2,1)S(1)} %copy-done.21, bf16[4,384,128]{2,1,0:T(8,128)(2,1)S(1)} %pad_maximum_fusion.3), kind=kLoop, calls=%fused_computation.3 | loop fusion | flops 2359296 | bytes 3145728 | tf_op jit(solution)/shard_map/concatenate | solution.py:276
  70.7 6.1 %collective-permute-done.9 = bf16[8,384,256]{2,1,0:T(8,128)(2,1)} collective-permute-done((bf16[8,384,256]{2,1,0:T(8,128)(2,1)}, bf16[8,384,256]{2,1,0:T(8,128)(2,1)}, u32[]{:S(2)}, u32[]{:S(2)}) %collective-permute-start.9) | collective-permute-done | bytes 1572896 | tf_op jit(solution)/shard_map/ppermute | solution.py:35
  77.0 2.9 %add_convert_fusion = bf16[8,384,256]{2,1,0:T(8,128)(2,1)S(1)} fusion(bf16[8,384,256]{2,1,0:T(8,128)(2,1)} %collective-permute-done.10, bf16[8,384,256]{2,1,0:T(8,128)(2,1)} %collective-permute-done.9, bf16[8,384,256]{2,1,0:T(8,128)(2,1)} %copy-done.6), kind=kLoop, calls=%fused_computation | loop fusion | flops 4718592 | bytes 6291456 | tf_op jit(solution)/shard_map/convert_element_type | solution.py:43
  81.6 16.4 %collective-permute-done.12.rest_0_ = bf16[16,384,128]{2,1,0:T(8,128)(2,1)} collective-permute-done((bf16[16,384,128]{2,1,0:T(8,128)(2,1)}, bf16[16,384,128]{2,1,0:T(8,128)(2,1)}, u32[]{:S(2)}, u32[]{:S(2)}) %collective-permute-start.12) | collective-permute-done | bytes 1572896 | tf_op jit(solution)/shard_map/ppermute | solution.py:35
  99.1 4.1 %collective-permute-done.17.rest_0_ = bf16[16,384,128]{2,1,0:T(8,128)(2,1)} collective-permute-done((bf16[16,384,128]{2,1,0:T(8,128)(2,1)}, bf16[16,384,128]{2,1,0:T(8,128)(2,1)}, u32[]{:S(2)}, u32[]{:S(2)}) %collective-permute-start.17) | collective-permute-done | bytes 1572896 | tf_op jit(solution)/shard_map/ppermute | solution.py:35
  103.4 3.9 %collective-permute-start.28 = (bf16[16,384,128]{2,1,0:T(8,128)(2,1)}, bf16[16,384,128]{2,1,0:T(8,128)(2,1)}, u32[]{:S(2)}, u32[]{:S(2)}) collective-permute-start(bf16[16,384,128]{2,1,0:T(8,128)(2,1)} %collective-permute-done.21.rest_0_), channel_id=1, source_target_pairs={{0,2},{2,4},{4,6},{6,0},{32,38},{34,32},{36,34},{38,36},{1,3},{3,5... | collective-permute-start | bytes 4718600 | tf_op jit(solution)/shard_map/ppermute | solution.py:35
  110.8 5.7 %collective-permute-start.26 = (bf16[16,384,128]{2,1,0:T(8,128)(2,1)}, bf16[16,384,128]{2,1,0:T(8,128)(2,1)}, u32[]{:S(2)}, u32[]{:S(2)}) collective-permute-start(bf16[16,384,128]{2,1,0:T(8,128)(2,1)} %collective-permute-done.18.rest_1_), channel_id=1, source_target_pairs={{0,32},{32,0},{1,33},{33,1},{2,34},{34,2},{3,35},{35,3},{4,36},{36... | collective-permute-start | bytes 4718600 | tf_op jit(solution)/shard_map/ppermute | solution.py:23
  121.1 5.8 %grads_0.1 = (bf16[128,128,128]{2,1,0:T(8,128)(2,1)}, bf16[128,128,128]{2,1,0:T(8,128)(2,1)}) custom-call(s32[164]{0:T(256)S(1)} %get-tuple-element.97.lrow, s32[164]{0:T(256)S(1)} %get-tuple-element.96.lslot, s32[656]{0:T(1024)S(1)} %reshape.625.ltile, s32[16]{0:T(128)S(1)} %pad_add_fusion.1.meta, bf16[2,1024,384]{2,1,0:T(8,128)(2,1)S(1)} %pad_maximum_fusion.2.gt, ...), custom_call_target="tpu_custom_call" | custom-call | flops 1 | bytes 1 | tf_op jit(solution)/shard_map/grads_0/pallas_call | solution.py:166
  126.9 4.6 %grads_1.1 = (bf16[128,128,128]{2,1,0:T(8,128)(2,1)}, bf16[128,128,128]{2,1,0:T(8,128)(2,1)}) custom-call(s32[164]{0:T(256)S(1)} %get-tuple-element.97.lrow, s32[164]{0:T(256)S(1)} %get-tuple-element.96.lslot, s32[656]{0:T(1024)S(1)} %reshape.625.ltile, s32[16]{0:T(128)S(1)} %pad_add_fusion.1.meta, ...), custom_call_target="tpu_custom_call", output_to_operand_aliasing={{0}: (8, {}), {1}: (9, {})} | custom-call | flops 1 | bytes 1 | tf_op jit(solution)/shard_map/grads_1/pallas_call | solution.py:166
  135.5 5.1 %grads_2.1 = (bf16[128,128,128]{2,1,0:T(8,128)(2,1)}, bf16[128,128,128]{2,1,0:T(8,128)(2,1)}) custom-call(s32[164]{0:T(256)S(1)} %get-tuple-element.97.lrow, s32[164]{0:T(256)S(1)} %get-tuple-element.96.lslot, s32[656]{0:T(1024)S(1)} %reshape.625.ltile, s32[16]{0:T(128)S(1)} %pad_add_fusion.1.meta, ...), custom_call_target="tpu_custom_call", output_to_operand_aliasing={{0}: (8, {}), {1}: (9, {})} | custom-call | flops 1 | bytes 1 | tf_op jit(solution)/shard_map/grads_2/pallas_call | solution.py:166
  143.2 7.7 %grads_3.1 = (bf16[128,128,128]{2,1,0:T(8,128)(2,1)}, bf16[128,128,128]{2,1,0:T(8,128)(2,1)}) custom-call(s32[164]{0:T(256)S(1)} %get-tuple-element.97.lrow, s32[164]{0:T(256)S(1)} %get-tuple-element.96.lslot, s32[656]{0:T(1024)S(1)} %reshape.625.ltile, s32[16]{0:T(128)S(1)} %pad_add_fusion.1.meta, ...), custom_call_target="tpu_custom_call", output_to_operand_aliasing={{0}: (10, {}), {1}: (11, {})} | custom-call | flops 1 | bytes 1 | tf_op jit(solution)/shard_map/grads_3/pallas_call | solution.py:166
  152.3 3.5 %collective-permute-start.27 = (bf16[384,256]{1,0:T(8,128)(2,1)S(1)}, bf16[384,256]{1,0:T(8,128)(2,1)S(1)}, u32[]{:S(2)}, u32[]{:S(2)}) collective-permute-start(bf16[384,256]{1,0:T(8,128)(2,1)S(1)} %fusion), channel_id=1, source_target_pairs={{0,1},{1,0},{2,3},{3,2},{4,5},{5,4},{6,7},{7,6},{8,9},{9,8},{10,11... | collective-permute-start | bytes 589832 | tf_op jit(solution)/shard_map/ppermute | solution.py:23
  155.7 7.4 %grads_4.1 = (bf16[128,128,128]{2,1,0:T(8,128)(2,1)}, bf16[128,128,128]{2,1,0:T(8,128)(2,1)}) custom-call(s32[164]{0:T(256)S(1)} %get-tuple-element.97.lrow, s32[164]{0:T(256)S(1)} %get-tuple-element.96.lslot, s32[656]{0:T(1024)S(1)} %reshape.625.ltile, s32[16]{0:T(128)S(1)} %pad_add_fusion.1.meta, ...), custom_call_target="tpu_custom_call", output_to_operand_aliasing={{0}: (10, {}), {1}: (11, {})} | custom-call | flops 1 | bytes 1 | tf_op jit(solution)/shard_map/grads_4/pallas_call | solution.py:166
  164.0 5.0 %grads_5.1 = (bf16[128,128,128]{2,1,0:T(8,128)(2,1)}, bf16[128,128,128]{2,1,0:T(8,128)(2,1)}) custom-call(s32[164]{0:T(256)S(1)} %get-tuple-element.97.lrow, s32[164]{0:T(256)S(1)} %get-tuple-element.96.lslot, s32[656]{0:T(1024)S(1)} %reshape.625.ltile, s32[16]{0:T(128)S(1)} %pad_add_fusion.1.meta, ...), custom_call_target="tpu_custom_call", output_to_operand_aliasing={{0}: (8, {}), {1}: (9, {})} | custom-call | flops 1 | bytes 1 | tf_op jit(solution)/shard_map/grads_5/pallas_call | solution.py:166
  (150 shorter events, 47.4 us)
Async XLA Ops:
  5.8 16.3 %collective-permute-start = (bf16[2,384,128]{2,1,0:T(8,128)(2,1)S(1)}, bf16[2,384,128]{2,1,0:T(8,128)(2,1)S(1)}, u32[]{:S(2)}, u32[]{:S(2)}) collective-permute-start(bf16[2,384,128]{2,1,0:T(8,128)(2,1)S(1)} %pad_maximum_fusion.5), channel_id=1, source_target_pairs={{0,8},{8,16},{16,24},{24,0},{32,56},{40,32},{48,40},{56,48},{1,9},... | collective-permute-start | bytes 589832 | tf_op jit(solution)/shard_map/ppermute | solution.py:35
  7.4 14.8 %collective-permute-start.1 = (bf16[2,384,128]{2,1,0:T(8,128)(2,1)S(1)}, bf16[2,384,128]{2,1,0:T(8,128)(2,1)S(1)}, u32[]{:S(2)}, u32[]{:S(2)}) collective-permute-start(bf16[2,384,128]{2,1,0:T(8,128)(2,1)S(1)} %pad_maximum_fusion.5), channel_id=1, source_target_pairs={{0,16},{8,24},{16,0},{24,8},{32,48},{40,56},{48,32},{56,40},{1,17}... | collective-permute-start | bytes 589832 | tf_op jit(solution)/shard_map/ppermute | solution.py:35
  8.5 13.7 %collective-permute-start.2 = (bf16[2,384,128]{2,1,0:T(8,128)(2,1)S(1)}, bf16[2,384,128]{2,1,0:T(8,128)(2,1)S(1)}, u32[]{:S(2)}, u32[]{:S(2)}) collective-permute-start(bf16[2,384,128]{2,1,0:T(8,128)(2,1)S(1)} %pad_maximum_fusion.5), channel_id=1, source_target_pairs={{0,24},{8,0},{16,8},{24,16},{32,40},{40,48},{48,56},{56,32},{1,25}... | collective-permute-start | bytes 589832 | tf_op jit(solution)/shard_map/ppermute | solution.py:35
  10.6 19.9 %collective-permute-start.4 = (bf16[1024,384]{1,0:T(8,128)(2,1)S(1)}, bf16[1024,384]{1,0:T(8,128)(2,1)S(1)}, u32[]{:S(2)}, u32[]{:S(2)}) collective-permute-start(bf16[1024,384]{1,0:T(8,128)(2,1)S(1)} %get-tuple-element.49), channel_id=1, source_target_pairs={{0,64},{64,0},{1,65},{65,1},{2,66},{66,2},{3,67},{67,3},{4,68},{68... | collective-permute-start | bytes 2359304 | tf_op jit(solution)/shard_map/ppermute | solution.py:23
  22.0 27.2 %collective-permute-start.6 = (bf16[8,384,256]{2,1,0:T(8,128)(2,1)S(1)}, bf16[8,384,256]{2,1,0:T(8,128)(2,1)S(1)}, u32[]{:S(2)}, u32[]{:S(2)}) collective-permute-start(bf16[8,384,256]{2,1,0:T(8,128)(2,1)S(1)} %terms.3), channel_id=1, source_target_pairs={{0,8},{8,16},{16,24},{24,0},{32,56},{40,32},{48,40},{56,48},{1,9},... | collective-permute-start | bytes 4718600 | tf_op jit(solution)/shard_map/ppermute | solution.py:35
  22.3 14.7 %collective-permute-start.3 = (bf16[4,384,128]{2,1,0:T(8,128)(2,1)S(1)}, bf16[4,384,128]{2,1,0:T(8,128)(2,1)S(1)}, u32[]{:S(2)}, u32[]{:S(2)}) collective-permute-start(bf16[4,384,128]{2,1,0:T(8,128)(2,1)S(1)} %pad_maximum_fusion.3), channel_id=1, source_target_pairs={{0,2},{2,4},{4,6},{6,0},{32,38},{34,32},{36,34},{38,36},{1,3},{3,5... | collective-permute-start | bytes 1179656 | tf_op jit(solution)/shard_map/ppermute | solution.py:35
  37.0 12.2 %collective-permute-start.7 = (bf16[4,384,128]{2,1,0:T(8,128)(2,1)S(1)}, bf16[4,384,128]{2,1,0:T(8,128)(2,1)}, u32[]{:S(2)}, u32[]{:S(2)}) collective-permute-start(bf16[4,384,128]{2,1,0:T(8,128)(2,1)S(1)} %collective-permute-done.3), channel_id=1, source_target_pairs={{0,2},{2,4},{4,6},{6,0},{32,38},{34,32},{36,34},{38,36},{1,3},{3,5... | collective-permute-start | bytes 1179656 | tf_op jit(solution)/shard_map/ppermute | solution.py:35
  40.2 28.8 %collective-permute-start.10 = (bf16[8,384,256]{2,1,0:T(8,128)(2,1)}, bf16[8,384,256]{2,1,0:T(8,128)(2,1)}, u32[]{:S(2)}, u32[]{:S(2)}) collective-permute-start(bf16[8,384,256]{2,1,0:T(8,128)(2,1)} %terms.5), channel_id=1, source_target_pairs={{0,24},{8,0},{16,8},{24,16},{32,40},{40,48},{48,56},{56,32},{1,25}... | collective-permute-start | bytes 4718600 | tf_op jit(solution)/shard_map/ppermute | solution.py:35
  50.8 26.0 %collective-permute-start.9 = (bf16[8,384,256]{2,1,0:T(8,128)(2,1)}, bf16[8,384,256]{2,1,0:T(8,128)(2,1)}, u32[]{:S(2)}, u32[]{:S(2)}) collective-permute-start(bf16[8,384,256]{2,1,0:T(8,128)(2,1)} %add_convert_fusion.1), channel_id=1, source_target_pairs={{0,8},{8,16},{16,24},{24,0},{32,56},{40,32},{48,40},{56,48},{1,9},... | collective-permute-start | bytes 4718600 | tf_op jit(solution)/shard_map/ppermute | solution.py:35
  52.8 13.4 %collective-permute-start.16 = (bf16[4,384,128]{2,1,0:T(8,128)(2,1)}, bf16[4,384,128]{2,1,0:T(8,128)(2,1)S(1)}, u32[]{:S(2)}, u32[]{:S(2)}) collective-permute-start(bf16[4,384,128]{2,1,0:T(8,128)(2,1)} %collective-permute-done.7), channel_id=1, source_target_pairs={{0,2},{2,4},{4,6},{6,0},{32,38},{34,32},{36,34},{38,36},{1,3},{3,5... | collective-permute-start | bytes 1179656 | tf_op jit(solution)/shard_map/ppermute | solution.py:35
  54.9 25.0 %collective-permute-start.20 = (bf16[2,1024,384]{2,1,0:T(8,128)(2,1)S(1)}, bf16[2,1024,384]{2,1,0:T(8,128)(2,1)S(1)}, u32[]{:S(2)}, u32[]{:S(2)}) collective-permute-start(bf16[2,1024,384]{2,1,0:T(8,128)(2,1)S(1)} %pad_maximum_fusion.2.gt), channel_id=1, source_target_pairs={{0,32},{32,0},{1,33},{33,1},{2,34},{34,2},{3,35},{35,3},{4,36},{36... | collective-permute-start | bytes 4718600 | tf_op jit(solution)/shard_map/ppermute | solution.py:23
  62.4 35.6 %collective-permute-start.12 = (bf16[16,384,128]{2,1,0:T(8,128)(2,1)}, bf16[16,384,128]{2,1,0:T(8,128)(2,1)}, u32[]{:S(2)}, u32[]{:S(2)}) collective-permute-start(bf16[16,384,128]{2,1,0:T(8,128)(2,1)} %pad_maximum_fusion.rest_0_), channel_id=1, source_target_pairs={{0,6},{2,0},{4,2},{6,4},{32,34},{34,36},{36,38},{38,32},{1,7},{3,1... | collective-permute-start | bytes 4718600 | tf_op jit(solution)/shard_map/ppermute | solution.py:35
  66.2 32.6 %collective-permute-start.21 = (bf16[16,384,128]{2,1,0:T(8,128)(2,1)}, bf16[16,384,128]{2,1,0:T(8,128)(2,1)}, u32[]{:S(2)}, u32[]{:S(2)}) collective-permute-start(bf16[16,384,128]{2,1,0:T(8,128)(2,1)} %pad_maximum_fusion.rest_0_), channel_id=1, source_target_pairs={{0,2},{2,4},{4,6},{6,0},{32,38},{34,32},{36,34},{38,36},{1,3},{3,5... | collective-permute-start | bytes 4718600 | tf_op jit(solution)/shard_map/ppermute | solution.py:35
  69.0 30.0 %collective-permute-start.18 = (bf16[16,384,128]{2,1,0:T(8,128)(2,1)}, bf16[16,384,128]{2,1,0:T(8,128)(2,1)}, u32[]{:S(2)}, u32[]{:S(2)}) collective-permute-start(bf16[16,384,128]{2,1,0:T(8,128)(2,1)} %pad_maximum_fusion.1.rest_0_), channel_id=1, source_target_pairs={{0,65},{1,0},{32,33},{33,96},{64,1},{65,64},{96,97},{97,32},{2,67}... | collective-permute-start | bytes 4718600 | tf_op jit(solution)/shard_map/ppermute | solution.py:35
  76.8 26.3 %collective-permute-start.17 = (bf16[16,384,128]{2,1,0:T(8,128)(2,1)}, bf16[16,384,128]{2,1,0:T(8,128)(2,1)}, u32[]{:S(2)}, u32[]{:S(2)}) collective-permute-start(bf16[16,384,128]{2,1,0:T(8,128)(2,1)} %pad_maximum_fusion.1.rest_0_), channel_id=1, source_target_pairs={{0,1},{1,64},{32,97},{33,32},{64,65},{65,0},{96,33},{97,96},{2,3},... | collective-permute-start | bytes 4718600 | tf_op jit(solution)/shard_map/ppermute | solution.py:35
  79.9 27.4 %collective-permute-start.23 = (bf16[16,384,128]{2,1,0:T(8,128)(2,1)}, bf16[16,384,128]{2,1,0:T(8,128)(2,1)S(1)}, u32[]{:S(2)}, u32[]{:S(2)}) collective-permute-start(bf16[16,384,128]{2,1,0:T(8,128)(2,1)} %pad_maximum_fusion.rest_0_), channel_id=1, source_target_pairs={{0,32},{32,0},{1,33},{33,1},{2,34},{34,2},{3,35},{35,3},{4,36},{36... | collective-permute-start | bytes 4718600 | tf_op jit(solution)/shard_map/ppermute | solution.py:23
  103.1 37.5 %collective-permute-start.19 = (bf16[16,384,128]{2,1,0:T(8,128)(2,1)}, bf16[16,384,128]{2,1,0:T(8,128)(2,1)}, u32[]{:S(2)}, u32[]{:S(2)}) collective-permute-start(bf16[16,384,128]{2,1,0:T(8,128)(2,1)} %collective-permute-done.17.rest_0_), channel_id=1, source_target_pairs={{0,1},{1,64},{32,97},{33,32},{64,65},{65,0},{96,33},{97,96},{2,3},... | collective-permute-start | bytes 4718600 | tf_op jit(solution)/shard_map/ppermute | solution.py:35
  103.4 37.3 %collective-permute-start.28 = (bf16[16,384,128]{2,1,0:T(8,128)(2,1)}, bf16[16,384,128]{2,1,0:T(8,128)(2,1)}, u32[]{:S(2)}, u32[]{:S(2)}) collective-permute-start(bf16[16,384,128]{2,1,0:T(8,128)(2,1)} %collective-permute-done.21.rest_0_), channel_id=1, source_target_pairs={{0,2},{2,4},{4,6},{6,0},{32,38},{34,32},{36,34},{38,36},{1,3},{3,5... | collective-permute-start | bytes 4718600 | tf_op jit(solution)/shard_map/ppermute | solution.py:35
  110.8 32.3 %collective-permute-start.26 = (bf16[16,384,128]{2,1,0:T(8,128)(2,1)}, bf16[16,384,128]{2,1,0:T(8,128)(2,1)}, u32[]{:S(2)}, u32[]{:S(2)}) collective-permute-start(bf16[16,384,128]{2,1,0:T(8,128)(2,1)} %collective-permute-done.18.rest_1_), channel_id=1, source_target_pairs={{0,32},{32,0},{1,33},{33,1},{2,34},{34,2},{3,35},{35,3},{4,36},{36... | collective-permute-start | bytes 4718600 | tf_op jit(solution)/shard_map/ppermute | solution.py:23
  117.4 14.9 %collective-permute-start.14 = (bf16[2,384,256]{2,1,0:T(8,128)(2,1)}, bf16[2,384,256]{2,1,0:T(8,128)(2,1)}, u32[]{:S(2)}, u32[]{:S(2)}) collective-permute-start(bf16[2,384,256]{2,1,0:T(8,128)(2,1)} %get-tuple-element.62), channel_id=1, source_target_pairs={{0,2},{2,4},{4,6},{6,0},{32,38},{34,32},{36,34},{38,36},{1,3},{3,5... | collective-permute-start | bytes 1179656 | tf_op jit(solution)/shard_map/ppermute | solution.py:35
  117.6 25.6 %collective-permute-start.25 = (bf16[16,384,128]{2,1,0:T(8,128)(2,1)}, bf16[16,384,128]{2,1,0:T(8,128)(2,1)}, u32[]{:S(2)}, u32[]{:S(2)}) collective-permute-start(bf16[16,384,128]{2,1,0:T(8,128)(2,1)} %collective-permute-done.17.rest_0_), channel_id=1, source_target_pairs={{0,32},{32,0},{1,33},{33,1},{2,34},{34,2},{3,35},{35,3},{4,36},{36... | collective-permute-start | bytes 4718600 | tf_op jit(solution)/shard_map/ppermute | solution.py:23
  140.6 15.1 %collective-permute-start.30 = (bf16[16,384,128]{2,1,0:T(8,128)(2,1)}, bf16[16,384,128]{2,1,0:T(8,128)(2,1)S(1)}, u32[]{:S(2)}, u32[]{:S(2)}) collective-permute-start(bf16[16,384,128]{2,1,0:T(8,128)(2,1)} %collective-permute-done.19.rest_1_), channel_id=1, source_target_pairs={{0,32},{32,0},{1,33},{33,1},{2,34},{34,2},{3,35},{35,3},{4,36},{36... | collective-permute-start | bytes 4718600 | tf_op jit(solution)/shard_map/ppermute | solution.py:23
  140.7 15.0 %collective-permute-start.29 = (bf16[16,384,128]{2,1,0:T(8,128)(2,1)S(1)}, bf16[16,384,128]{2,1,0:T(8,128)(2,1)S(1)}, u32[]{:S(2)}, u32[]{:S(2)}) collective-permute-start(bf16[16,384,128]{2,1,0:T(8,128)(2,1)S(1)} %copy-done.3), channel_id=1, source_target_pairs={{0,32},{32,0},{1,33},{33,1},{2,34},{34,2},{3,35},{35,3},{4,36},{36... | collective-permute-start | bytes 4718600 | tf_op jit(solution)/shard_map/ppermute | solution.py:23
  141.2 22.7 %collective-permute-start.31 = (bf16[16,384,128]{2,1,0:T(8,128)(2,1)}, bf16[16,384,128]{2,1,0:T(8,128)(2,1)S(1)}, u32[]{:S(2)}, u32[]{:S(2)}) collective-permute-start(bf16[16,384,128]{2,1,0:T(8,128)(2,1)} %collective-permute-done.28.rest_0_), channel_id=1, source_target_pairs={{0,32},{32,0},{1,33},{33,1},{2,34},{34,2},{3,35},{35,3},{4,36},{36... | collective-permute-start | bytes 4718600 | tf_op jit(solution)/shard_map/ppermute | solution.py:23
  (34 other events, 271.8 us)

commit v4 on v2

--- a/solution.py
+++ b/solution.py
@@ -116,13 +116,13 @@
         pltpu.make_async_copy(zero, grads.at[0], sem).wait()
 
 
-def same_row_pairs(kind, origin, refs, groups, lrow, lslot, ltile, meta, gt, gate, up, gbuf, ubuf, sem):
+def same_row_pairs(kind, origin, refs, groups, lrow, lslot, ltile, meta, gts, gate, up, gbuf, ubuf, sem):
     @pl.loop(meta[kind], meta[kind + 1])
     def _(step):
         for pair in range(2):
             pos = step * 4 + pair * 2
             rows = pl.ds(pl.multiple_of(lrow[pos] * 256, 256), 256)
-            left = jnp.concatenate([gt[g, rows, :] for g in groups], axis=1)
+            left = jnp.concatenate([gts[n // 2][g, rows, :] for n, g in enumerate(groups)], axis=1)
             sides = []
             for side in range(2):
                 tiles = [ref[ltile[(pos + side) * 4 + n]] for n, ref in enumerate(refs)]
@@ -140,7 +140,7 @@
                 put(ubuf.at[pos - origin], up, lslot[pos], sem)
 
 
-def kinds_kernel(kinds, held, lrow, lslot, ltile, meta, gt, *rest):
+def kinds_kernel(kinds, held, lrow, lslot, ltile, meta, gt, gt_c, *rest):
     pieces, (gate, up, gbuf, ubuf, zero, sem) = rest[: len(rest) - 6 - held], rest[-6:]
     origin = meta[kinds[0][0]] * 4
     if not held:
@@ -155,18 +155,18 @@
     for kind, picks in kinds:
         refs = [pieces[n] for n in picks]
         flip = meta[7]
-        groups = (flip, 1 - flip, 3 - flip, 2 + flip) if kind == 3 else (0, 1, 2, 3)
-        same_row_pairs(kind, origin, refs, groups, lrow, lslot, ltile, meta, gt, gate, up, gbuf, ubuf, sem)
+        groups = (flip, 1 - flip, 1 - flip, flip) if kind == 3 else (0, 1, 0, 1)
+        same_row_pairs(kind, origin, refs, groups, lrow, lslot, ltile, meta, (gt, gt_c), gate, up, gbuf, ubuf, sem)
     finish(2 * (meta[9 + kinds[-1][0] + 1] - meta[9 + kinds[0][0]]), zero, gate, sem)
 
 
-def weight_grads(name, kinds, room, lists, gt, pieces, held=()):
+def weight_grads(name, kinds, room, lists, gts, pieces, held=()):
     grads = jax.ShapeDtypeStruct((SLOTS, 128, 128), BF)
-    first = 5 + len(pieces)
+    first = 6 + len(pieces)
     return pl.pallas_call(
         functools.partial(kinds_kernel, kinds, len(held)),
         out_shape=[grads] * 2,
-        in_specs=[SM] * 4 + [VM] * (1 + len(pieces)) + [ANY] * len(held),
+        in_specs=[SM] * 4 + [VM] * (2 + len(pieces)) + [ANY] * len(held),
         out_specs=[ANY] * 2,
         scratch_shapes=[
             pltpu.VMEM((room, 128, 128), BF),
@@ -178,7 +178,7 @@
         compiler_params=pltpu.CompilerParams(vmem_limit_bytes=13 * 1024 * 1024),
         cost_estimate=pl.CostEstimate(flops=1, bytes_accessed=1, transcendentals=0),
         name=name,
-    )(*lists, gt, *pieces, *held)
+    )(*lists, *gts, *pieces, *held)
 
 
 def block_table(block_rows, block_cols, block_count):
@@ -282,11 +282,11 @@
     lrow, lslot, ltile, meta = slot_lists(rows_late, cols_late, count_late)
     mine = sum_of(t0, ahead, back).reshape(4, 2, TOK, 256)
     own = after(jnp.stack([gut, other]), mine)
-    gt = jnp.concatenate([own, shift(own, "c", 1)])
+    own_c = shift(own, "c", 1)
     odd_0c = shift(after(odd_0, mine), "c", 1)
 
     def grads_of(name, kinds, room, pieces, held=(), wait=()):
-        return weight_grads(name, kinds, room, (lrow, lslot, ltile, after(meta, *wait)), gt, pieces, held)
+        return weight_grads(name, kinds, room, (lrow, lslot, ltile, after(meta, *wait)), (own, own_c), pieces, held)
 
     even_2 = shift(after(even_1, even_3), "y", 1)
     odd_2 = shift(after(odd_1, odd_3), "z", 1)
@@ -302,7 +302,7 @@
     grads = grads_of("grads_3", ((3, (0, 1, 2, 3)),), 72, (even_1, even_3, even_1c, even_3c), grads, (even_2,))
     even_2c = shift(even_2, "c", 1)
     odd_2c = shift(odd_2, "c", 1)
-    ahead = add(after(ahead, grads[0]), mine[3])
+    ahead = add(after(ahead, grads[0], back), mine[3])
     grads = grads_of(
         "grads_4", ((4, (0, 1, 2, 3)),), 72, (even_0, even_2, even_0c, even_2c), grads, (ahead, odd_2)
     )

time: 162 us -> 198 us (1.22)
  waiting for transfers between devices: 49.9 us -> 88.7 us
  Pallas kernels: 40.6 us -> 48.7 us
  starting transfers between devices: 38.8 us -> 31.2 us
  local copies, waits for them, and re-layouts: 17 us -> 13 us
    ppermute x21, waiting for transfers between devices: 44.5 us -> 83.7 us  [shift(): return lax.ppermute(value, AXES[axis], pairs)]
    pallas_call x6, Pallas kernels: 24.3 us -> 32.4 us  [weight_grads(): pl.pallas_call(functools.partial(kinds_kernel, kinds, len(held)), out_sha...]
    ppermute x21, starting transfers between devices: 29.7 us -> 24.8 us  [shift(): return lax.ppermute(value, AXES[axis], pairs)]
    unnamed x51 -> x36, local copies, waits for them, and re-layouts: 13.7 us -> 10.6 us
    ppermute x11, starting transfers between devices: 9.09 us -> 6.37 us  [shift(): return lax.ppermute(value, axis, [(0, 1), (1, 0)])]
  transfers between devices with their start and end apart: 32 -> 32, of which waited for: 10 -> 11; matrix products, arithmetic and copies ran while one was open for 10% -> 7% of each run, Pallas kernels for 25% -> 24%
where the time goes in v4:
time: 198 us; the launch traced here: 197 us
  waiting for transfers between devices  88.7 us (45%)
  Pallas kernels  48.7 us (25%)
  starting transfers between devices  31.2 us (16%)
  other arithmetic  14 us (7%)
  local copies, waits for them, and re-layouts  13 us (7%)
    ppermute x21, waiting for transfers between devices, shift(): return lax.ppermute(value, AXES[axis], pairs)  83.7 us
    pallas_call x6, Pallas kernels, weight_grads(): pl.pallas_call(functools.partial(kinds_kernel, kinds, len(held)), out_sha...  32.4 us
    ppermute x21, starting transfers between devices, shift(): return lax.ppermute(value, AXES[axis], pairs)  24.8 us
    pallas_call x3, Pallas kernels, terms(): pl.pallas_call(functools.partial(chunk_kernel, chunks), out_shape=[PIECE]...  15.2 us
    unnamed x36, local copies, waits for them, and re-layouts  10.6 us
    ppermute x11, starting transfers between devices, shift(): return lax.ppermute(value, axis, [(0, 1), (1, 0)])  6.37 us
    ppermute x11, waiting for transfers between devices, shift(): return lax.ppermute(value, axis, [(0, 1), (1, 0)])  5 us
  transfers between devices with their start and end apart: 32, of which 11 were waited for; matrix products, arithmetic and copies ran while one was open for 7% of the time, Pallas kernels for 24%

profile of v4, /device:TPU:0, one launch (start us, length us, event | category | flops | bytes accessed | tf_op | source)
XLA Modules:
  0.0 197.4 jit_solution(8889376603840324725)
XLA Ops:
  5.8 2.9 %collective-permute-start.2 = (bf16[2,384,128]{2,1,0:T(8,128)(2,1)S(1)}, bf16[2,384,128]{2,1,0:T(8,128)(2,1)S(1)}, u32[]{:S(2)}, u32[]{:S(2)}) collective-permute-start(bf16[2,384,128]{2,1,0:T(8,128)(2,1)S(1)} %pad_maximum_fusion.5), channel_id=1, source_target_pairs={{0,24},{8,0},{16,8},{24,16},{32,40},{40,48},{48,56},{56,32},{1,25}... | collective-permute-start | bytes 589832 | tf_op jit(solution)/shard_map/ppermute | solution.py:35
  10.4 3.2 %collective-permute-start.4 = (bf16[1024,384]{1,0:T(8,128)(2,1)S(1)}, bf16[1024,384]{1,0:T(8,128)(2,1)S(1)}, u32[]{:S(2)}, u32[]{:S(2)}) collective-permute-start(bf16[1024,384]{1,0:T(8,128)(2,1)S(1)} %get-tuple-element.51), channel_id=1, source_target_pairs={{0,64},{64,0},{1,65},{65,1},{2,66},{66,2},{3,67},{67,3},{4,68},{68... | collective-permute-start | bytes 2359304 | tf_op jit(solution)/shard_map/ppermute | solution.py:23
  14.7 2.2 %copy-done = bf16[128,128,128]{2,1,0:T(8,128)(2,1)S(1)} copy-done((bf16[128,128,128]{2,1,0:T(8,128)(2,1)S(1)}, bf16[128,128,128]{2,1,0:T(8,128)(2,1)}, u32[]{:S(2)}) %copy-start) | copy-done | bytes 4194328
  16.9 2.2 %copy-done.2 = bf16[128,128,128]{2,1,0:T(8,128)(2,1)S(1)} copy-done((bf16[128,128,128]{2,1,0:T(8,128)(2,1)S(1)}, bf16[128,128,128]{2,1,0:T(8,128)(2,1)}, u32[]{:S(2)}) %copy-start.2) | copy-done | bytes 4194328
  19.1 3.6 %terms.3 = bf16[8,384,256]{2,1,0:T(8,128)(2,1)S(1)} custom-call(s32[256]{0:T(256)S(1)} %select_reduce_fusion.tab, s32[32]{0:T(128)S(1)} %mul.262.order, bf16[384,1024]{1,0:T(8,128)(2,1)S(1)} %get-tuple-element.55.gu, bf16[128,128,128]{2,1,0:T(8,128)(2,1)S(1)} %copy-done, bf16[128,128,128]{2,1,0:T(8,128)(2,1)S(1)} %copy-done.2), custom_call_target="tpu_custom_call" | custom-call | flops 1 | bytes 1 | tf_op jit(solution)/shard_map/terms/pallas_call | solution.py:98
  25.7 2.0 %collective-permute-start.3 = (bf16[4,384,128]{2,1,0:T(8,128)(2,1)S(1)}, bf16[4,384,128]{2,1,0:T(8,128)(2,1)S(1)}, u32[]{:S(2)}, u32[]{:S(2)}) collective-permute-start(bf16[4,384,128]{2,1,0:T(8,128)(2,1)S(1)} %pad_maximum_fusion.3), channel_id=1, source_target_pairs={{0,2},{2,4},{4,6},{6,0},{32,38},{34,32},{36,34},{38,36},{1,3},{3,5... | collective-permute-start | bytes 1179656 | tf_op jit(solution)/shard_map/ppermute | solution.py:35
  27.8 3.8 %collective-permute-done.4 = bf16[1024,384]{1,0:T(8,128)(2,1)S(1)} collective-permute-done((bf16[1024,384]{1,0:T(8,128)(2,1)S(1)}, bf16[1024,384]{1,0:T(8,128)(2,1)S(1)}, u32[]{:S(2)}, u32[]{:S(2)}) %collective-permute-start.4) | collective-permute-done | bytes 786464 | tf_op jit(solution)/shard_map/ppermute | solution.py:23
  34.0 4.8 %terms.5 = bf16[8,384,256]{2,1,0:T(8,128)(2,1)} custom-call(s32[256]{0:T(256)S(1)} %select_reduce_fusion.tab, s32[32]{0:T(128)S(1)} %mul.262.order, bf16[384,1024]{1,0:T(8,128)(2,1)S(1)} %get-tuple-element.55.gu, bf16[128,128,128]{2,1,0:T(8,128)(2,1)S(1)} %copy-done.1, bf16[128,128,128]{2,1,0:T(8,128)(2,1)S(1)} %copy-done.2), custom_call_target="tpu_custom_call" | custom-call | flops 1 | bytes 1 | tf_op jit(solution)/shard_map/terms/pallas_call | solution.py:98
  42.6 6.7 %terms.4 = (bf16[8,384,256]{2,1,0:T(8,128)(2,1)S(1)}, bf16[8,384,256]{2,1,0:T(8,128)(2,1)S(1)}) custom-call(s32[256]{0:T(256)S(1)} %select_reduce_fusion.tab, s32[32]{0:T(128)S(1)} %mul.262.order, bf16[384,1024]{1,0:T(8,128)(2,1)S(1)} %get-tuple-element.55.gu, bf16[128,128,128]{2,1,0:T(8,128)(2,1)S(1)} %copy-done.1, bf16[128,128,128]{2,1,0:T(8,128)(2,1)S(1)} %copy-done.2), custom_call_target="tpu_custom_call" | custom-call | flops 1 | bytes 1 | tf_op jit(solution)/shard_map/terms/pallas_call | solution.py:98
  54.0 7.7 %collective-permute-done.11 = bf16[4,384,128]{2,1,0:T(8,128)(2,1)S(1)} collective-permute-done((bf16[4,384,128]{2,1,0:T(8,128)(2,1)S(1)}, bf16[4,384,128]{2,1,0:T(8,128)(2,1)S(1)}, u32[]{:S(2)}, u32[]{:S(2)}) %collective-permute-start.11) | collective-permute-done | bytes 393248 | tf_op jit(solution)/shard_map/ppermute | solution.py:35
  63.1 4.0 %collective-permute-start.12 = (bf16[16,384,128]{2,1,0:T(8,128)(2,1)}, bf16[16,384,128]{2,1,0:T(8,128)(2,1)}, u32[]{:S(2)}, u32[]{:S(2)}) collective-permute-start(bf16[16,384,128]{2,1,0:T(8,128)(2,1)} %pad_maximum_fusion.rest_0_), channel_id=1, source_target_pairs={{0,6},{2,0},{4,2},{6,4},{32,34},{34,36},{36,38},{38,32},{1,7},{3,1... | collective-permute-start | bytes 4718600 | tf_op jit(solution)/shard_map/ppermute | solution.py:35
  68.7 36.6 %collective-permute-done.15 = bf16[4,384,128]{2,1,0:T(8,128)(2,1)} collective-permute-done((bf16[4,384,128]{2,1,0:T(8,128)(2,1)}, bf16[4,384,128]{2,1,0:T(8,128)(2,1)}, u32[]{:S(2)}, u32[]{:S(2)}) %collective-permute-start.15) | collective-permute-done | bytes 393248 | tf_op jit(solution)/shard_map/ppermute | solution.py:35
  105.3 2.5 %pad_maximum_fusion.1.rest_0_ = bf16[16,384,128]{2,1,0:T(8,128)(2,1)} fusion(bf16[4,384,128]{2,1,0:T(8,128)(2,1)} %collective-permute-done.15, bf16[4,384,128]{2,1,0:T(8,128)(2,1)} %collective-permute-done.7, bf16[4,384,128]{2,1,0:T(8,128)(2,1)S(1)} %copy-done.14, bf16[4,384,128]{2,1,0:T(8,128)(2,1)S(1)} %pad_maximum_fusion.3), kind=kLoop, calls=%fused_computation.3 | loop fusion | flops 2359296 | bytes 3145728 | tf_op jit(solution)/shard_map/concatenate | solution.py:276
  108.9 2.3 %collective-permute-start.17 = (bf16[16,384,128]{2,1,0:T(8,128)(2,1)}, bf16[16,384,128]{2,1,0:T(8,128)(2,1)}, u32[]{:S(2)}, u32[]{:S(2)}) collective-permute-start(bf16[16,384,128]{2,1,0:T(8,128)(2,1)} %pad_maximum_fusion.1.rest_0_), channel_id=1, source_target_pairs={{0,65},{1,0},{32,33},{33,96},{64,1},{65,64},{96,97},{97,32},{2,67}... | collective-permute-start | bytes 4718600 | tf_op jit(solution)/shard_map/ppermute | solution.py:35
  111.1 3.7 %add_convert_fusion = bf16[8,384,256]{2,1,0:T(8,128)(2,1)} fusion(bf16[8,384,256]{2,1,0:T(8,128)(2,1)} %collective-permute-done.10, bf16[8,384,256]{2,1,0:T(8,128)(2,1)} %collective-permute-done.9, bf16[8,384,256]{2,1,0:T(8,128)(2,1)S(1)} %get-tuple-element.56), kind=kLoop, calls=%fused_computation | loop fusion | flops 4718592 | bytes 6291456 | tf_op jit(solution)/shard_map/convert_element_type | solution.py:43
  116.9 29.4 %collective-permute-done.16.rest_0_ = bf16[16,384,128]{2,1,0:T(8,128)(2,1)} collective-permute-done((bf16[16,384,128]{2,1,0:T(8,128)(2,1)}, bf16[16,384,128]{2,1,0:T(8,128)(2,1)}, u32[]{:S(2)}, u32[]{:S(2)}) %collective-permute-start.16) | collective-permute-done | bytes 1572896 | tf_op jit(solution)/shard_map/ppermute | solution.py:35
  151.7 6.1 %grads_0.1 = (bf16[128,128,128]{2,1,0:T(8,128)(2,1)}, bf16[128,128,128]{2,1,0:T(8,128)(2,1)}) custom-call(s32[164]{0:T(256)S(1)} %get-tuple-element.101.lrow, s32[164]{0:T(256)S(1)} %get-tuple-element.100.lslot, s32[656]{0:T(1024)S(1)} %reshape.625.ltile, s32[16]{0:T(128)S(1)} %pad_add_fusion.1.meta, bf16[2,1024,384]{2,1,0:T(8,128)(2,1)S(1)} %pad_maximum_fusion.2.gt, ...), custom_call_target="tpu_custom_call" | custom-call | flops 1 | bytes 1 | tf_op jit(solution)/shard_map/grads_0/pallas_call | solution.py:166
  157.8 4.6 %grads_1.1 = (bf16[128,128,128]{2,1,0:T(8,128)(2,1)}, bf16[128,128,128]{2,1,0:T(8,128)(2,1)}) custom-call(s32[164]{0:T(256)S(1)} %get-tuple-element.101.lrow, s32[164]{0:T(256)S(1)} %get-tuple-element.100.lslot, s32[656]{0:T(1024)S(1)} %reshape.625.ltile, s32[16]{0:T(128)S(1)} %pad_add_fusion.1.meta, ...), custom_call_target="tpu_custom_call", output_to_operand_aliasing={{0}: (8, {}), {1}: (9, {})} | custom-call | flops 1 | bytes 1 | tf_op jit(solution)/shard_map/grads_1/pallas_call | solution.py:166
  162.5 4.0 %grads_2.1 = (bf16[128,128,128]{2,1,0:T(8,128)(2,1)}, bf16[128,128,128]{2,1,0:T(8,128)(2,1)}) custom-call(s32[164]{0:T(256)S(1)} %get-tuple-element.101.lrow, s32[164]{0:T(256)S(1)} %get-tuple-element.100.lslot, s32[656]{0:T(1024)S(1)} %reshape.625.ltile, s32[16]{0:T(128)S(1)} %pad_add_fusion.1.meta, ...), custom_call_target="tpu_custom_call", output_to_operand_aliasing={{0}: (8, {}), {1}: (9, {})} | custom-call | flops 1 | bytes 1 | tf_op jit(solution)/shard_map/grads_2/pallas_call | solution.py:166
  171.0 7.1 %grads_3.1 = (bf16[128,128,128]{2,1,0:T(8,128)(2,1)}, bf16[128,128,128]{2,1,0:T(8,128)(2,1)}) custom-call(s32[164]{0:T(256)S(1)} %get-tuple-element.101.lrow, s32[164]{0:T(256)S(1)} %get-tuple-element.100.lslot, s32[656]{0:T(1024)S(1)} %reshape.625.ltile, s32[16]{0:T(128)S(1)} %pad_add_fusion.1.meta, ...), custom_call_target="tpu_custom_call", output_to_operand_aliasing={{0}: (10, {}), {1}: (11, {})} | custom-call | flops 1 | bytes 1 | tf_op jit(solution)/shard_map/grads_3/pallas_call | solution.py:166
  178.1 2.5 %collective-permute-done.25 = bf16[2,384,256]{2,1,0:T(8,128)(2,1)S(1)} collective-permute-done((bf16[2,384,256]{2,1,0:T(8,128)(2,1)S(1)}, bf16[2,384,256]{2,1,0:T(8,128)(2,1)S(1)}, u32[]{:S(2)}, u32[]{:S(2)}) %collective-permute-start.25) | collective-permute-done | bytes 393248 | tf_op jit(solution)/shard_map/ppermute | solution.py:35
  181.9 6.2 %grads_4.1 = (bf16[128,128,128]{2,1,0:T(8,128)(2,1)}, bf16[128,128,128]{2,1,0:T(8,128)(2,1)}) custom-call(s32[164]{0:T(256)S(1)} %get-tuple-element.101.lrow, s32[164]{0:T(256)S(1)} %get-tuple-element.100.lslot, s32[656]{0:T(1024)S(1)} %reshape.625.ltile, s32[16]{0:T(128)S(1)} %pad_add_fusion.1.meta, ...), custom_call_target="tpu_custom_call", output_to_operand_aliasing={{0}: (10, {}), {1}: (11, {})} | custom-call | flops 1 | bytes 1 | tf_op jit(solution)/shard_map/grads_4/pallas_call | solution.py:166
  188.0 2.8 %collective-permute-done.26 = bf16[2,384,256]{2,1,0:T(8,128)(2,1)S(1)} collective-permute-done((bf16[2,384,256]{2,1,0:T(8,128)(2,1)S(1)}, bf16[2,384,256]{2,1,0:T(8,128)(2,1)S(1)}, u32[]{:S(2)}, u32[]{:S(2)}) %collective-permute-start.26) | collective-permute-done | bytes 393248 | tf_op jit(solution)/shard_map/ppermute | solution.py:35
  191.0 4.5 %grads_5.1 = (bf16[128,128,128]{2,1,0:T(8,128)(2,1)}, bf16[128,128,128]{2,1,0:T(8,128)(2,1)}) custom-call(s32[164]{0:T(256)S(1)} %get-tuple-element.101.lrow, s32[164]{0:T(256)S(1)} %get-tuple-element.100.lslot, s32[656]{0:T(1024)S(1)} %reshape.625.ltile, s32[16]{0:T(128)S(1)} %pad_add_fusion.1.meta, ...), custom_call_target="tpu_custom_call", output_to_operand_aliasing={{0}: (8, {}), {1}: (9, {})} | custom-call | flops 1 | bytes 1 | tf_op jit(solution)/shard_map/grads_5/pallas_call | solution.py:166
  (134 shorter events, 40.4 us)
Async XLA Ops:
  5.8 18.8 %collective-permute-start.2 = (bf16[2,384,128]{2,1,0:T(8,128)(2,1)S(1)}, bf16[2,384,128]{2,1,0:T(8,128)(2,1)S(1)}, u32[]{:S(2)}, u32[]{:S(2)}) collective-permute-start(bf16[2,384,128]{2,1,0:T(8,128)(2,1)S(1)} %pad_maximum_fusion.5), channel_id=1, source_target_pairs={{0,24},{8,0},{16,8},{24,16},{32,40},{40,48},{48,56},{56,32},{1,25}... | collective-permute-start | bytes 589832 | tf_op jit(solution)/shard_map/ppermute | solution.py:35
  8.7 15.9 %collective-permute-start.1 = (bf16[2,384,128]{2,1,0:T(8,128)(2,1)S(1)}, bf16[2,384,128]{2,1,0:T(8,128)(2,1)}, u32[]{:S(2)}, u32[]{:S(2)}) collective-permute-start(bf16[2,384,128]{2,1,0:T(8,128)(2,1)S(1)} %pad_maximum_fusion.5), channel_id=1, source_target_pairs={{0,16},{8,24},{16,0},{24,8},{32,48},{40,56},{48,32},{56,40},{1,17}... | collective-permute-start | bytes 589832 | tf_op jit(solution)/shard_map/ppermute | solution.py:35
  9.5 16.1 %collective-permute-start = (bf16[2,384,128]{2,1,0:T(8,128)(2,1)S(1)}, bf16[2,384,128]{2,1,0:T(8,128)(2,1)S(1)}, u32[]{:S(2)}, u32[]{:S(2)}) collective-permute-start(bf16[2,384,128]{2,1,0:T(8,128)(2,1)S(1)} %pad_maximum_fusion.5), channel_id=1, source_target_pairs={{0,8},{8,16},{16,24},{24,0},{32,56},{40,32},{48,40},{56,48},{1,9},... | collective-permute-start | bytes 589832 | tf_op jit(solution)/shard_map/ppermute | solution.py:35
  10.4 21.2 %collective-permute-start.4 = (bf16[1024,384]{1,0:T(8,128)(2,1)S(1)}, bf16[1024,384]{1,0:T(8,128)(2,1)S(1)}, u32[]{:S(2)}, u32[]{:S(2)}) collective-permute-start(bf16[1024,384]{1,0:T(8,128)(2,1)S(1)} %get-tuple-element.51), channel_id=1, source_target_pairs={{0,64},{64,0},{1,65},{65,1},{2,66},{66,2},{3,67},{67,3},{4,68},{68... | collective-permute-start | bytes 2359304 | tf_op jit(solution)/shard_map/ppermute | solution.py:23
  22.7 26.7 %collective-permute-start.6 = (bf16[8,384,256]{2,1,0:T(8,128)(2,1)S(1)}, bf16[8,384,256]{2,1,0:T(8,128)(2,1)S(1)}, u32[]{:S(2)}, u32[]{:S(2)}) collective-permute-start(bf16[8,384,256]{2,1,0:T(8,128)(2,1)S(1)} %terms.3), channel_id=1, source_target_pairs={{0,8},{8,16},{16,24},{24,0},{32,56},{40,32},{48,40},{56,48},{1,9},... | collective-permute-start | bytes 4718600 | tf_op jit(solution)/shard_map/ppermute | solution.py:35
  25.7 13.1 %collective-permute-start.3 = (bf16[4,384,128]{2,1,0:T(8,128)(2,1)S(1)}, bf16[4,384,128]{2,1,0:T(8,128)(2,1)S(1)}, u32[]{:S(2)}, u32[]{:S(2)}) collective-permute-start(bf16[4,384,128]{2,1,0:T(8,128)(2,1)S(1)} %pad_maximum_fusion.3), channel_id=1, source_target_pairs={{0,2},{2,4},{4,6},{6,0},{32,38},{34,32},{36,34},{38,36},{1,3},{3,5... | collective-permute-start | bytes 1179656 | tf_op jit(solution)/shard_map/ppermute | solution.py:35
  42.3 66.5 %collective-permute-start.10 = (bf16[8,384,256]{2,1,0:T(8,128)(2,1)}, bf16[8,384,256]{2,1,0:T(8,128)(2,1)}, u32[]{:S(2)}, u32[]{:S(2)}) collective-permute-start(bf16[8,384,256]{2,1,0:T(8,128)(2,1)} %terms.5), channel_id=1, source_target_pairs={{0,24},{8,0},{16,8},{24,16},{32,40},{40,48},{48,56},{56,32},{1,25}... | collective-permute-start | bytes 4718600 | tf_op jit(solution)/shard_map/ppermute | solution.py:35
  52.0 59.1 %collective-permute-start.9 = (bf16[8,384,256]{2,1,0:T(8,128)(2,1)}, bf16[8,384,256]{2,1,0:T(8,128)(2,1)}, u32[]{:S(2)}, u32[]{:S(2)}) collective-permute-start(bf16[8,384,256]{2,1,0:T(8,128)(2,1)} %add_convert_fusion.1), channel_id=1, source_target_pairs={{0,8},{8,16},{16,24},{24,0},{32,56},{40,32},{48,40},{56,48},{1,9},... | collective-permute-start | bytes 4718600 | tf_op jit(solution)/shard_map/ppermute | solution.py:35
  63.1 52.1 %collective-permute-start.12 = (bf16[16,384,128]{2,1,0:T(8,128)(2,1)}, bf16[16,384,128]{2,1,0:T(8,128)(2,1)}, u32[]{:S(2)}, u32[]{:S(2)}) collective-permute-start(bf16[16,384,128]{2,1,0:T(8,128)(2,1)} %pad_maximum_fusion.rest_0_), channel_id=1, source_target_pairs={{0,6},{2,0},{4,2},{6,4},{32,34},{34,36},{36,38},{38,32},{1,7},{3,1... | collective-permute-start | bytes 4718600 | tf_op jit(solution)/shard_map/ppermute | solution.py:35
  67.1 48.7 %collective-permute-start.20 = (bf16[16,384,128]{2,1,0:T(8,128)(2,1)}, bf16[16,384,128]{2,1,0:T(8,128)(2,1)}, u32[]{:S(2)}, u32[]{:S(2)}) collective-permute-start(bf16[16,384,128]{2,1,0:T(8,128)(2,1)} %pad_maximum_fusion.rest_0_), channel_id=1, source_target_pairs={{0,2},{2,4},{4,6},{6,0},{32,38},{34,32},{36,34},{38,36},{1,3},{3,5... | collective-permute-start | bytes 4718600 | tf_op jit(solution)/shard_map/ppermute | solution.py:35
  67.1 38.3 %collective-permute-start.15 = (bf16[4,384,128]{2,1,0:T(8,128)(2,1)}, bf16[4,384,128]{2,1,0:T(8,128)(2,1)}, u32[]{:S(2)}, u32[]{:S(2)}) collective-permute-start(bf16[4,384,128]{2,1,0:T(8,128)(2,1)} %collective-permute-done.7), channel_id=1, source_target_pairs={{0,2},{2,4},{4,6},{6,0},{32,38},{34,32},{36,34},{38,36},{1,3},{3,5... | collective-permute-start | bytes 1179656 | tf_op jit(solution)/shard_map/ppermute | solution.py:35
  107.8 38.5 %collective-permute-start.16 = (bf16[16,384,128]{2,1,0:T(8,128)(2,1)}, bf16[16,384,128]{2,1,0:T(8,128)(2,1)}, u32[]{:S(2)}, u32[]{:S(2)}) collective-permute-start(bf16[16,384,128]{2,1,0:T(8,128)(2,1)} %pad_maximum_fusion.1.rest_0_), channel_id=1, source_target_pairs={{0,1},{1,64},{32,97},{33,32},{64,65},{65,0},{96,33},{97,96},{2,3},... | collective-permute-start | bytes 4718600 | tf_op jit(solution)/shard_map/ppermute | solution.py:35
  108.9 37.5 %collective-permute-start.17 = (bf16[16,384,128]{2,1,0:T(8,128)(2,1)}, bf16[16,384,128]{2,1,0:T(8,128)(2,1)}, u32[]{:S(2)}, u32[]{:S(2)}) collective-permute-start(bf16[16,384,128]{2,1,0:T(8,128)(2,1)} %pad_maximum_fusion.1.rest_0_), channel_id=1, source_target_pairs={{0,65},{1,0},{32,33},{33,96},{64,1},{65,64},{96,97},{97,32},{2,67}... | collective-permute-start | bytes 4718600 | tf_op jit(solution)/shard_map/ppermute | solution.py:35
  114.8 31.7 %collective-permute-start.22 = (bf16[16,384,128]{2,1,0:T(8,128)(2,1)}, bf16[16,384,128]{2,1,0:T(8,128)(2,1)}, u32[]{:S(2)}, u32[]{:S(2)}) collective-permute-start(bf16[16,384,128]{2,1,0:T(8,128)(2,1)} %pad_maximum_fusion.rest_0_), channel_id=1, source_target_pairs={{0,32},{32,0},{1,33},{33,1},{2,34},{34,2},{3,35},{35,3},{4,36},{36... | collective-permute-start | bytes 4718600 | tf_op jit(solution)/shard_map/ppermute | solution.py:23
  115.2 31.7 %collective-permute-start.13 = (bf16[16,384,128]{2,1,0:T(8,128)(2,1)}, bf16[16,384,128]{2,1,0:T(8,128)(2,1)S(1)}, u32[]{:S(2)}, u32[]{:S(2)}) collective-permute-start(bf16[16,384,128]{2,1,0:T(8,128)(2,1)} %collective-permute-done.12.rest_0_), channel_id=1, source_target_pairs={{0,32},{32,0},{1,33},{33,1},{2,34},{34,2},{3,35},{35,3},{4,36},{36... | collective-permute-start | bytes 4718600 | tf_op jit(solution)/shard_map/ppermute | solution.py:23
  115.7 32.2 %collective-permute-start.21 = (bf16[16,384,128]{2,1,0:T(8,128)(2,1)}, bf16[16,384,128]{2,1,0:T(8,128)(2,1)S(1)}, u32[]{:S(2)}, u32[]{:S(2)}) collective-permute-start(bf16[16,384,128]{2,1,0:T(8,128)(2,1)} %collective-permute-done.20.rest_0_), channel_id=1, source_target_pairs={{0,32},{32,0},{1,33},{33,1},{2,34},{34,2},{3,35},{35,3},{4,36},{36... | collective-permute-start | bytes 4718600 | tf_op jit(solution)/shard_map/ppermute | solution.py:23
  146.3 21.9 %collective-permute-start.18 = (bf16[16,384,128]{2,1,0:T(8,128)(2,1)}, bf16[16,384,128]{2,1,0:T(8,128)(2,1)}, u32[]{:S(2)}, u32[]{:S(2)}) collective-permute-start(bf16[16,384,128]{2,1,0:T(8,128)(2,1)} %collective-permute-done.16.rest_0_), channel_id=1, source_target_pairs={{0,1},{1,64},{32,97},{33,32},{64,65},{65,0},{96,33},{97,96},{2,3},... | collective-permute-start | bytes 4718600 | tf_op jit(solution)/shard_map/ppermute | solution.py:35
  146.5 22.2 %collective-permute-start.27 = (bf16[16,384,128]{2,1,0:T(8,128)(2,1)}, bf16[16,384,128]{2,1,0:T(8,128)(2,1)}, u32[]{:S(2)}, u32[]{:S(2)}) collective-permute-start(bf16[16,384,128]{2,1,0:T(8,128)(2,1)} %collective-permute-done.20.rest_0_), channel_id=1, source_target_pairs={{0,2},{2,4},{4,6},{6,0},{32,38},{34,32},{36,34},{38,36},{1,3},{3,5... | collective-permute-start | bytes 4718600 | tf_op jit(solution)/shard_map/ppermute | solution.py:35
  149.2 19.7 %collective-permute-start.23 = (bf16[16,384,128]{2,1,0:T(8,128)(2,1)}, bf16[16,384,128]{2,1,0:T(8,128)(2,1)}, u32[]{:S(2)}, u32[]{:S(2)}) collective-permute-start(bf16[16,384,128]{2,1,0:T(8,128)(2,1)} %collective-permute-done.16.rest_0_), channel_id=1, source_target_pairs={{0,32},{32,0},{1,33},{33,1},{2,34},{34,2},{3,35},{35,3},{4,36},{36... | collective-permute-start | bytes 4718600 | tf_op jit(solution)/shard_map/ppermute | solution.py:23
  151.1 18.9 %collective-permute-start.24 = (bf16[16,384,128]{2,1,0:T(8,128)(2,1)}, bf16[16,384,128]{2,1,0:T(8,128)(2,1)}, u32[]{:S(2)}, u32[]{:S(2)}) collective-permute-start(bf16[16,384,128]{2,1,0:T(8,128)(2,1)} %collective-permute-done.17.rest_1_), channel_id=1, source_target_pairs={{0,32},{32,0},{1,33},{33,1},{2,34},{34,2},{3,35},{35,3},{4,36},{36... | collective-permute-start | bytes 4718600 | tf_op jit(solution)/shard_map/ppermute | solution.py:23
  168.3 13.6 %collective-permute-start.28 = (bf16[16,384,128]{2,1,0:T(8,128)(2,1)}, bf16[16,384,128]{2,1,0:T(8,128)(2,1)S(1)}, u32[]{:S(2)}, u32[]{:S(2)}) collective-permute-start(bf16[16,384,128]{2,1,0:T(8,128)(2,1)} %pad_maximum_fusion.1.rest_0_), channel_id=1, source_target_pairs={{0,32},{32,0},{1,33},{33,1},{2,34},{34,2},{3,35},{35,3},{4,36},{36... | collective-permute-start | bytes 4718600 | tf_op jit(solution)/shard_map/ppermute | solution.py:23
  168.3 13.6 %collective-permute-start.29 = (bf16[16,384,128]{2,1,0:T(8,128)(2,1)}, bf16[16,384,128]{2,1,0:T(8,128)(2,1)S(1)}, u32[]{:S(2)}, u32[]{:S(2)}) collective-permute-start(bf16[16,384,128]{2,1,0:T(8,128)(2,1)} %collective-permute-done.18.rest_1_), channel_id=1, source_target_pairs={{0,32},{32,0},{1,33},{33,1},{2,34},{34,2},{3,35},{35,3},{4,36},{36... | collective-permute-start | bytes 4718600 | tf_op jit(solution)/shard_map/ppermute | solution.py:23
  168.8 22.2 %collective-permute-start.31 = (bf16[16,384,128]{2,1,0:T(8,128)(2,1)}, bf16[16,384,128]{2,1,0:T(8,128)(2,1)S(1)}, u32[]{:S(2)}, u32[]{:S(2)}) collective-permute-start(bf16[16,384,128]{2,1,0:T(8,128)(2,1)} %collective-permute-done.27.rest_0_), channel_id=1, source_target_pairs={{0,32},{32,0},{1,33},{33,1},{2,34},{34,2},{3,35},{35,3},{4,36},{36... | collective-permute-start | bytes 4718600 | tf_op jit(solution)/shard_map/ppermute | solution.py:23
  169.9 11.7 %collective-permute-start.14 = (bf16[2,384,256]{2,1,0:T(8,128)(2,1)S(1)}, bf16[2,384,256]{2,1,0:T(8,128)(2,1)S(1)}, u32[]{:S(2)}, u32[]{:S(2)}) collective-permute-start(bf16[2,384,256]{2,1,0:T(8,128)(2,1)S(1)} %get-tuple-element.64), channel_id=1, source_target_pairs={{0,2},{2,4},{4,6},{6,0},{32,38},{34,32},{36,34},{38,36},{1,3},{3,5... | collective-permute-start | bytes 1179656 | tf_op jit(solution)/shard_map/ppermute | solution.py:35
  (26 other events, 252.6 us)

commit v5 on v4

--- a/solution.py
+++ b/solution.py
@@ -273,8 +273,7 @@
     evens.append(shift(after(evens[2], t3), "z", 1))
     odds.append(shift(after(odds[2], t3), "y", 1))
     moving = add(after(ahead, evens[2], odds[2]), t3)
-    even_0 = after(jnp.concatenate(evens), t0, moving)
-    odd_0 = after(jnp.concatenate(odds), t0, moving)
+    even_0, odd_0 = lax.optimization_barrier((jnp.concatenate(evens), jnp.concatenate(odds), t0, moving))[:2]
     even_1, even_3 = shift(even_0, "y", 1), shift(even_0, "y", -1)
     odd_1, odd_3 = shift(odd_0, "z", 1), shift(odd_0, "z", -1)
     ahead = shift(moving, "x", 1)

time: 198 us -> 158 us (0.80)
  waiting for transfers between devices: 88.7 us -> 41 us
  starting transfers between devices: 31.2 us -> 38.4 us
  Pallas kernels: 48.7 us -> 52.9 us
    ppermute x21, waiting for transfers between devices: 83.7 us -> 38.3 us  [shift(): return lax.ppermute(value, AXES[axis], pairs)]
    ppermute x21, starting transfers between devices: 24.8 us -> 30.3 us  [shift(): return lax.ppermute(value, AXES[axis], pairs)]
    pallas_call x6, Pallas kernels: 32.4 us -> 36.6 us  [weight_grads(): pl.pallas_call(functools.partial(kinds_kernel, kinds, len(held)), out_sha...]
    ppermute x11, waiting for transfers between devices: 5 us -> 2.65 us  [shift(): return lax.ppermute(value, axis, [(0, 1), (1, 0)])]
    unnamed x36 -> x30, local copies, waits for them, and re-layouts: 10.6 us -> 9.75 us
  transfers between devices with their start and end apart: 32 -> 32, of which waited for: 11 -> 11; matrix products, arithmetic and copies ran while one was open for 7% -> 8% of each run, Pallas kernels for 24% -> 33%
where the time goes in v5:
time: 158 us
  Pallas kernels  52.9 us (33%)
  waiting for transfers between devices  41 us (26%)
  starting transfers between devices  38.4 us (24%)
  local copies, waits for them, and re-layouts  12.2 us (8%)
  other arithmetic  12.2 us (8%)
  between operations  1.77 us (1%)
    ppermute x21, waiting for transfers between devices, shift(): return lax.ppermute(value, AXES[axis], pairs)  38.3 us
    pallas_call x6, Pallas kernels, weight_grads(): pl.pallas_call(functools.partial(kinds_kernel, kinds, len(held)), out_sha...  36.6 us
    ppermute x21, starting transfers between devices, shift(): return lax.ppermute(value, AXES[axis], pairs)  30.3 us
    pallas_call x3, Pallas kernels, terms(): pl.pallas_call(functools.partial(chunk_kernel, chunks), out_shape=[PIECE]...  15.2 us
    unnamed x30, local copies, waits for them, and re-layouts  9.75 us
    ppermute x11, starting transfers between devices, shift(): return lax.ppermute(value, axis, [(0, 1), (1, 0)])  8.12 us
    convert_element_type x2, other arithmetic, sum_of(): return (a.astype(F32) + b.astype(F32) + c.astype(F32)).astype(BF)  3.68 us
  transfers between devices with their start and end apart: 32, of which 11 were waited for; matrix products, arithmetic and copies ran while one was open for 8% of the time, Pallas kernels for 33%

profile of v5, /device:TPU:0, one launch (start us, length us, event | category | flops | bytes accessed | tf_op | source)
XLA Modules:
  0.0 158.4 jit_solution(16240235661604841342)
XLA Ops:
  7.5 2.7 %collective-permute-start.1 = (bf16[2,384,128]{2,1,0:T(8,128)(2,1)S(1)}, bf16[2,384,128]{2,1,0:T(8,128)(2,1)S(1)}, u32[]{:S(2)}, u32[]{:S(2)}) collective-permute-start(bf16[2,384,128]{2,1,0:T(8,128)(2,1)S(1)} %pad_maximum_fusion.5), channel_id=1, source_target_pairs={{0,16},{8,24},{16,0},{24,8},{32,48},{40,56},{48,32},{56,40},{1,17}... | collective-permute-start | bytes 589832 | tf_op jit(solution)/shard_map/ppermute | solution.py:35
  11.6 3.2 %collective-permute-start.4 = (bf16[1024,384]{1,0:T(8,128)(2,1)S(1)}, bf16[1024,384]{1,0:T(8,128)(2,1)S(1)}, u32[]{:S(2)}, u32[]{:S(2)}) collective-permute-start(bf16[1024,384]{1,0:T(8,128)(2,1)S(1)} %get-tuple-element.51), channel_id=1, source_target_pairs={{0,64},{64,0},{1,65},{65,1},{2,66},{66,2},{3,67},{67,3},{4,68},{68... | collective-permute-start | bytes 2359304 | tf_op jit(solution)/shard_map/ppermute | solution.py:23
  18.1 2.2 %copy-done.2 = bf16[128,128,128]{2,1,0:T(8,128)(2,1)S(1)} copy-done((bf16[128,128,128]{2,1,0:T(8,128)(2,1)S(1)}, bf16[128,128,128]{2,1,0:T(8,128)(2,1)}, u32[]{:S(2)}) %copy-start.2) | copy-done | bytes 4194328
  20.3 3.6 %terms.3 = bf16[8,384,256]{2,1,0:T(8,128)(2,1)S(1)} custom-call(s32[256]{0:T(256)S(1)} %select_reduce_fusion.tab, s32[32]{0:T(128)S(1)} %mul.262.order, bf16[384,1024]{1,0:T(8,128)(2,1)S(1)} %get-tuple-element.55.gu, bf16[128,128,128]{2,1,0:T(8,128)(2,1)S(1)} %copy-done, bf16[128,128,128]{2,1,0:T(8,128)(2,1)S(1)} %copy-done.2), custom_call_target="tpu_custom_call" | custom-call | flops 1 | bytes 1 | tf_op jit(solution)/shard_map/terms/pallas_call | solution.py:98
  27.7 2.6 %collective-permute-done.4 = bf16[1024,384]{1,0:T(8,128)(2,1)S(1)} collective-permute-done((bf16[1024,384]{1,0:T(8,128)(2,1)S(1)}, bf16[1024,384]{1,0:T(8,128)(2,1)S(1)}, u32[]{:S(2)}, u32[]{:S(2)}) %collective-permute-start.4) | collective-permute-done | bytes 786464 | tf_op jit(solution)/shard_map/ppermute | solution.py:23
  31.9 4.8 %terms.5 = bf16[8,384,256]{2,1,0:T(8,128)(2,1)} custom-call(s32[256]{0:T(256)S(1)} %select_reduce_fusion.tab, s32[32]{0:T(128)S(1)} %mul.262.order, bf16[384,1024]{1,0:T(8,128)(2,1)S(1)} %get-tuple-element.55.gu, bf16[128,128,128]{2,1,0:T(8,128)(2,1)S(1)} %copy-done.1, bf16[128,128,128]{2,1,0:T(8,128)(2,1)S(1)} %copy-done.2), custom_call_target="tpu_custom_call" | custom-call | flops 1 | bytes 1 | tf_op jit(solution)/shard_map/terms/pallas_call | solution.py:98
  40.2 2.4 %collective-permute-start.10 = (bf16[8,384,256]{2,1,0:T(8,128)(2,1)}, bf16[8,384,256]{2,1,0:T(8,128)(2,1)}, u32[]{:S(2)}, u32[]{:S(2)}) collective-permute-start(bf16[8,384,256]{2,1,0:T(8,128)(2,1)} %terms.5), channel_id=1, source_target_pairs={{0,24},{8,0},{16,8},{24,16},{32,40},{40,48},{48,56},{56,32},{1,25}... | collective-permute-start | bytes 4718600 | tf_op jit(solution)/shard_map/ppermute | solution.py:35
  42.6 6.7 %terms.4 = (bf16[8,384,256]{2,1,0:T(8,128)(2,1)S(1)}, bf16[8,384,256]{2,1,0:T(8,128)(2,1)S(1)}) custom-call(s32[256]{0:T(256)S(1)} %select_reduce_fusion.tab, s32[32]{0:T(128)S(1)} %mul.262.order, bf16[384,1024]{1,0:T(8,128)(2,1)S(1)} %get-tuple-element.55.gu, bf16[128,128,128]{2,1,0:T(8,128)(2,1)S(1)} %copy-done.1, bf16[128,128,128]{2,1,0:T(8,128)(2,1)S(1)} %copy-done.2), custom_call_target="tpu_custom_call" | custom-call | flops 1 | bytes 1 | tf_op jit(solution)/shard_map/terms/pallas_call | solution.py:98
  54.7 3.9 %collective-permute-done.11 = bf16[4,384,128]{2,1,0:T(8,128)(2,1)S(1)} collective-permute-done((bf16[4,384,128]{2,1,0:T(8,128)(2,1)S(1)}, bf16[4,384,128]{2,1,0:T(8,128)(2,1)S(1)}, u32[]{:S(2)}, u32[]{:S(2)}) %collective-permute-start.11) | collective-permute-done | bytes 393248 | tf_op jit(solution)/shard_map/ppermute | solution.py:35
  63.3 2.8 %collective-permute-start.13 = (bf16[16,384,128]{2,1,0:T(8,128)(2,1)}, bf16[16,384,128]{2,1,0:T(8,128)(2,1)}, u32[]{:S(2)}, u32[]{:S(2)}) collective-permute-start(bf16[16,384,128]{2,1,0:T(8,128)(2,1)} %pad_maximum_fusion.1.rest_0_), channel_id=1, source_target_pairs={{0,6},{2,0},{4,2},{6,4},{32,34},{34,36},{36,38},{38,32},{1,7},{3,1... | collective-permute-start | bytes 4718600 | tf_op jit(solution)/shard_map/ppermute | solution.py:35
  68.5 3.1 %collective-permute-start.16 = (bf16[16,384,128]{2,1,0:T(8,128)(2,1)}, bf16[16,384,128]{2,1,0:T(8,128)(2,1)}, u32[]{:S(2)}, u32[]{:S(2)}) collective-permute-start(bf16[16,384,128]{2,1,0:T(8,128)(2,1)} %pad_maximum_fusion.rest_0_), channel_id=1, source_target_pairs={{0,1},{1,64},{32,97},{33,32},{64,65},{65,0},{96,33},{97,96},{2,3},... | collective-permute-start | bytes 4718600 | tf_op jit(solution)/shard_map/ppermute | solution.py:35
  71.6 7.8 %collective-permute-done.9 = bf16[8,384,256]{2,1,0:T(8,128)(2,1)} collective-permute-done((bf16[8,384,256]{2,1,0:T(8,128)(2,1)}, bf16[8,384,256]{2,1,0:T(8,128)(2,1)}, u32[]{:S(2)}, u32[]{:S(2)}) %collective-permute-start.9) | collective-permute-done | bytes 1572896 | tf_op jit(solution)/shard_map/ppermute | solution.py:35
  79.4 3.6 %add_convert_fusion = bf16[8,384,256]{2,1,0:T(8,128)(2,1)} fusion(bf16[8,384,256]{2,1,0:T(8,128)(2,1)} %collective-permute-done.10, bf16[8,384,256]{2,1,0:T(8,128)(2,1)} %collective-permute-done.9, bf16[8,384,256]{2,1,0:T(8,128)(2,1)S(1)} %get-tuple-element.56), kind=kLoop, calls=%fused_computation | loop fusion | flops 4718592 | bytes 6291456 | tf_op jit(solution)/shard_map/convert_element_type | solution.py:43
  83.4 16.6 %collective-permute-done.13.rest_0_ = bf16[16,384,128]{2,1,0:T(8,128)(2,1)} collective-permute-done((bf16[16,384,128]{2,1,0:T(8,128)(2,1)}, bf16[16,384,128]{2,1,0:T(8,128)(2,1)}, u32[]{:S(2)}, u32[]{:S(2)}) %collective-permute-start.13) | collective-permute-done | bytes 1572896 | tf_op jit(solution)/shard_map/ppermute | solution.py:35
  101.2 2.7 %collective-permute-done.17.rest_1_ = bf16[16,384,128]{2,1,0:T(8,128)(2,1)} collective-permute-done((bf16[16,384,128]{2,1,0:T(8,128)(2,1)}, bf16[16,384,128]{2,1,0:T(8,128)(2,1)}, u32[]{:S(2)}, u32[]{:S(2)}) %collective-permute-start.17) | collective-permute-done | bytes 1572896 | tf_op jit(solution)/shard_map/ppermute | solution.py:35
  109.0 3.7 %collective-permute-start.24 = (bf16[16,384,128]{2,1,0:T(8,128)(2,1)}, bf16[16,384,128]{2,1,0:T(8,128)(2,1)}, u32[]{:S(2)}, u32[]{:S(2)}) collective-permute-start(bf16[16,384,128]{2,1,0:T(8,128)(2,1)} %collective-permute-done.17.rest_1_), channel_id=1, source_target_pairs={{0,32},{32,0},{1,33},{33,1},{2,34},{34,2},{3,35},{35,3},{4,36},{36... | collective-permute-start | bytes 4718600 | tf_op jit(solution)/shard_map/ppermute | solution.py:23
  113.2 6.2 %grads_0.1 = (bf16[128,128,128]{2,1,0:T(8,128)(2,1)}, bf16[128,128,128]{2,1,0:T(8,128)(2,1)}) custom-call(s32[164]{0:T(256)S(1)} %get-tuple-element.101.lrow, s32[164]{0:T(256)S(1)} %get-tuple-element.100.lslot, s32[656]{0:T(1024)S(1)} %reshape.625.ltile, s32[16]{0:T(128)S(1)} %pad_add_fusion.1.meta, bf16[2,1024,384]{2,1,0:T(8,128)(2,1)S(1)} %pad_maximum_fusion.2.gt, ...), custom_call_target="tpu_custom_call" | custom-call | flops 1 | bytes 1 | tf_op jit(solution)/shard_map/grads_0/pallas_call | solution.py:166
  119.4 4.0 %grads_1.1 = (bf16[128,128,128]{2,1,0:T(8,128)(2,1)}, bf16[128,128,128]{2,1,0:T(8,128)(2,1)}) custom-call(s32[164]{0:T(256)S(1)} %get-tuple-element.101.lrow, s32[164]{0:T(256)S(1)} %get-tuple-element.100.lslot, s32[656]{0:T(1024)S(1)} %reshape.625.ltile, s32[16]{0:T(128)S(1)} %pad_add_fusion.1.meta, ...), custom_call_target="tpu_custom_call", output_to_operand_aliasing={{0}: (8, {}), {1}: (9, {})} | custom-call | flops 1 | bytes 1 | tf_op jit(solution)/shard_map/grads_1/pallas_call | solution.py:166
  123.5 5.1 %grads_2.1 = (bf16[128,128,128]{2,1,0:T(8,128)(2,1)}, bf16[128,128,128]{2,1,0:T(8,128)(2,1)}) custom-call(s32[164]{0:T(256)S(1)} %get-tuple-element.101.lrow, s32[164]{0:T(256)S(1)} %get-tuple-element.100.lslot, s32[656]{0:T(1024)S(1)} %reshape.625.ltile, s32[16]{0:T(128)S(1)} %pad_add_fusion.1.meta, ...), custom_call_target="tpu_custom_call", output_to_operand_aliasing={{0}: (8, {}), {1}: (9, {})} | custom-call | flops 1 | bytes 1 | tf_op jit(solution)/shard_map/grads_2/pallas_call | solution.py:166
  129.9 3.2 %collective-permute-start.25 = (bf16[2,384,256]{2,1,0:T(8,128)(2,1)S(1)}, bf16[2,384,256]{2,1,0:T(8,128)(2,1)S(1)}, u32[]{:S(2)}, u32[]{:S(2)}) collective-permute-start(bf16[2,384,256]{2,1,0:T(8,128)(2,1)S(1)} %get-tuple-element.84), channel_id=1, source_target_pairs={{0,6},{2,0},{4,2},{6,4},{32,34},{34,36},{36,38},{38,32},{1,7},{3,1... | collective-permute-start | bytes 1179656 | tf_op jit(solution)/shard_map/ppermute | solution.py:35
  133.1 8.9 %grads_3.1 = (bf16[128,128,128]{2,1,0:T(8,128)(2,1)}, bf16[128,128,128]{2,1,0:T(8,128)(2,1)}) custom-call(s32[164]{0:T(256)S(1)} %get-tuple-element.101.lrow, s32[164]{0:T(256)S(1)} %get-tuple-element.100.lslot, s32[656]{0:T(1024)S(1)} %reshape.625.ltile, s32[16]{0:T(128)S(1)} %pad_add_fusion.1.meta, ...), custom_call_target="tpu_custom_call", output_to_operand_aliasing={{0}: (10, {}), {1}: (11, {})} | custom-call | flops 1 | bytes 1 | tf_op jit(solution)/shard_map/grads_3/pallas_call | solution.py:166
  142.8 6.7 %grads_4.1 = (bf16[128,128,128]{2,1,0:T(8,128)(2,1)}, bf16[128,128,128]{2,1,0:T(8,128)(2,1)}) custom-call(s32[164]{0:T(256)S(1)} %get-tuple-element.101.lrow, s32[164]{0:T(256)S(1)} %get-tuple-element.100.lslot, s32[656]{0:T(1024)S(1)} %reshape.625.ltile, s32[16]{0:T(128)S(1)} %pad_add_fusion.1.meta, ...), custom_call_target="tpu_custom_call", output_to_operand_aliasing={{0}: (10, {}), {1}: (11, {})} | custom-call | flops 1 | bytes 1 | tf_op jit(solution)/shard_map/grads_4/pallas_call | solution.py:166
  149.6 2.2 %collective-permute-done.26 = bf16[2,384,256]{2,1,0:T(8,128)(2,1)S(1)} collective-permute-done((bf16[2,384,256]{2,1,0:T(8,128)(2,1)S(1)}, bf16[2,384,256]{2,1,0:T(8,128)(2,1)S(1)}, u32[]{:S(2)}, u32[]{:S(2)}) %collective-permute-start.26) | collective-permute-done | bytes 393248 | tf_op jit(solution)/shard_map/ppermute | solution.py:35
  152.0 5.6 %grads_5.1 = (bf16[128,128,128]{2,1,0:T(8,128)(2,1)}, bf16[128,128,128]{2,1,0:T(8,128)(2,1)}) custom-call(s32[164]{0:T(256)S(1)} %get-tuple-element.101.lrow, s32[164]{0:T(256)S(1)} %get-tuple-element.100.lslot, s32[656]{0:T(1024)S(1)} %reshape.625.ltile, s32[16]{0:T(128)S(1)} %pad_add_fusion.1.meta, ...), custom_call_target="tpu_custom_call", output_to_operand_aliasing={{0}: (8, {}), {1}: (9, {})} | custom-call | flops 1 | bytes 1 | tf_op jit(solution)/shard_map/grads_5/pallas_call | solution.py:166
  (128 shorter events, 42.1 us)
Async XLA Ops:
  5.8 18.8 %collective-permute-start = (bf16[2,384,128]{2,1,0:T(8,128)(2,1)S(1)}, bf16[2,384,128]{2,1,0:T(8,128)(2,1)}, u32[]{:S(2)}, u32[]{:S(2)}) collective-permute-start(bf16[2,384,128]{2,1,0:T(8,128)(2,1)S(1)} %pad_maximum_fusion.5), channel_id=1, source_target_pairs={{0,8},{8,16},{16,24},{24,0},{32,56},{40,32},{48,40},{56,48},{1,9},... | collective-permute-start | bytes 589832 | tf_op jit(solution)/shard_map/ppermute | solution.py:35
  7.5 18.1 %collective-permute-start.1 = (bf16[2,384,128]{2,1,0:T(8,128)(2,1)S(1)}, bf16[2,384,128]{2,1,0:T(8,128)(2,1)S(1)}, u32[]{:S(2)}, u32[]{:S(2)}) collective-permute-start(bf16[2,384,128]{2,1,0:T(8,128)(2,1)S(1)} %pad_maximum_fusion.5), channel_id=1, source_target_pairs={{0,16},{8,24},{16,0},{24,8},{32,48},{40,56},{48,32},{56,40},{1,17}... | collective-permute-start | bytes 589832 | tf_op jit(solution)/shard_map/ppermute | solution.py:35
  10.2 15.4 %collective-permute-start.2 = (bf16[2,384,128]{2,1,0:T(8,128)(2,1)S(1)}, bf16[2,384,128]{2,1,0:T(8,128)(2,1)S(1)}, u32[]{:S(2)}, u32[]{:S(2)}) collective-permute-start(bf16[2,384,128]{2,1,0:T(8,128)(2,1)S(1)} %pad_maximum_fusion.5), channel_id=1, source_target_pairs={{0,24},{8,0},{16,8},{24,16},{32,40},{40,48},{48,56},{56,32},{1,25}... | collective-permute-start | bytes 589832 | tf_op jit(solution)/shard_map/ppermute | solution.py:35
  11.6 18.7 %collective-permute-start.4 = (bf16[1024,384]{1,0:T(8,128)(2,1)S(1)}, bf16[1024,384]{1,0:T(8,128)(2,1)S(1)}, u32[]{:S(2)}, u32[]{:S(2)}) collective-permute-start(bf16[1024,384]{1,0:T(8,128)(2,1)S(1)} %get-tuple-element.51), channel_id=1, source_target_pairs={{0,64},{64,0},{1,65},{65,1},{2,66},{66,2},{3,67},{67,3},{4,68},{68... | collective-permute-start | bytes 2359304 | tf_op jit(solution)/shard_map/ppermute | solution.py:23
  23.9 27.4 %collective-permute-start.6 = (bf16[8,384,256]{2,1,0:T(8,128)(2,1)S(1)}, bf16[8,384,256]{2,1,0:T(8,128)(2,1)S(1)}, u32[]{:S(2)}, u32[]{:S(2)}) collective-permute-start(bf16[8,384,256]{2,1,0:T(8,128)(2,1)S(1)} %terms.3), channel_id=1, source_target_pairs={{0,8},{8,16},{16,24},{24,0},{32,56},{40,32},{48,40},{56,48},{1,9},... | collective-permute-start | bytes 4718600 | tf_op jit(solution)/shard_map/ppermute | solution.py:35
  25.7 11.1 %collective-permute-start.3 = (bf16[4,384,128]{2,1,0:T(8,128)(2,1)S(1)}, bf16[4,384,128]{2,1,0:T(8,128)(2,1)S(1)}, u32[]{:S(2)}, u32[]{:S(2)}) collective-permute-start(bf16[4,384,128]{2,1,0:T(8,128)(2,1)S(1)} %pad_maximum_fusion.3), channel_id=1, source_target_pairs={{0,2},{2,4},{4,6},{6,0},{32,38},{34,32},{36,34},{38,36},{1,3},{3,5... | collective-permute-start | bytes 1179656 | tf_op jit(solution)/shard_map/ppermute | solution.py:35
  36.8 12.6 %collective-permute-start.7 = (bf16[4,384,128]{2,1,0:T(8,128)(2,1)S(1)}, bf16[4,384,128]{2,1,0:T(8,128)(2,1)S(1)}, u32[]{:S(2)}, u32[]{:S(2)}) collective-permute-start(bf16[4,384,128]{2,1,0:T(8,128)(2,1)S(1)} %collective-permute-done.3), channel_id=1, source_target_pairs={{0,2},{2,4},{4,6},{6,0},{32,38},{34,32},{36,34},{38,36},{1,3},{3,5... | collective-permute-start | bytes 1179656 | tf_op jit(solution)/shard_map/ppermute | solution.py:35
  39.3 12.0 %collective-permute-start.8 = (bf16[4,384,128]{2,1,0:T(8,128)(2,1)S(1)}, bf16[4,384,128]{2,1,0:T(8,128)(2,1)S(1)}, u32[]{:S(2)}, u32[]{:S(2)}) collective-permute-start(bf16[4,384,128]{2,1,0:T(8,128)(2,1)S(1)} %collective-permute-done.5), channel_id=1, source_target_pairs={{0,1},{1,64},{32,97},{33,32},{64,65},{65,0},{96,33},{97,96},{2,3},... | collective-permute-start | bytes 1179656 | tf_op jit(solution)/shard_map/ppermute | solution.py:35
  40.2 28.3 %collective-permute-start.10 = (bf16[8,384,256]{2,1,0:T(8,128)(2,1)}, bf16[8,384,256]{2,1,0:T(8,128)(2,1)}, u32[]{:S(2)}, u32[]{:S(2)}) collective-permute-start(bf16[8,384,256]{2,1,0:T(8,128)(2,1)} %terms.5), channel_id=1, source_target_pairs={{0,24},{8,0},{16,8},{24,16},{32,40},{40,48},{48,56},{56,32},{1,25}... | collective-permute-start | bytes 4718600 | tf_op jit(solution)/shard_map/ppermute | solution.py:35
  52.9 26.5 %collective-permute-start.9 = (bf16[8,384,256]{2,1,0:T(8,128)(2,1)}, bf16[8,384,256]{2,1,0:T(8,128)(2,1)}, u32[]{:S(2)}, u32[]{:S(2)}) collective-permute-start(bf16[8,384,256]{2,1,0:T(8,128)(2,1)} %add_convert_fusion.1), channel_id=1, source_target_pairs={{0,8},{8,16},{16,24},{24,0},{32,56},{40,32},{48,40},{56,48},{1,9},... | collective-permute-start | bytes 4718600 | tf_op jit(solution)/shard_map/ppermute | solution.py:35
  63.3 36.6 %collective-permute-start.13 = (bf16[16,384,128]{2,1,0:T(8,128)(2,1)}, bf16[16,384,128]{2,1,0:T(8,128)(2,1)}, u32[]{:S(2)}, u32[]{:S(2)}) collective-permute-start(bf16[16,384,128]{2,1,0:T(8,128)(2,1)} %pad_maximum_fusion.1.rest_0_), channel_id=1, source_target_pairs={{0,6},{2,0},{4,2},{6,4},{32,34},{34,36},{36,38},{38,32},{1,7},{3,1... | collective-permute-start | bytes 4718600 | tf_op jit(solution)/shard_map/ppermute | solution.py:35
  66.2 34.5 %collective-permute-start.20 = (bf16[16,384,128]{2,1,0:T(8,128)(2,1)}, bf16[16,384,128]{2,1,0:T(8,128)(2,1)}, u32[]{:S(2)}, u32[]{:S(2)}) collective-permute-start(bf16[16,384,128]{2,1,0:T(8,128)(2,1)} %pad_maximum_fusion.1.rest_0_), channel_id=1, source_target_pairs={{0,2},{2,4},{4,6},{6,0},{32,38},{34,32},{36,34},{38,36},{1,3},{3,5... | collective-permute-start | bytes 4718600 | tf_op jit(solution)/shard_map/ppermute | solution.py:35
  67.8 36.2 %collective-permute-start.17 = (bf16[16,384,128]{2,1,0:T(8,128)(2,1)}, bf16[16,384,128]{2,1,0:T(8,128)(2,1)}, u32[]{:S(2)}, u32[]{:S(2)}) collective-permute-start(bf16[16,384,128]{2,1,0:T(8,128)(2,1)} %pad_maximum_fusion.rest_0_), channel_id=1, source_target_pairs={{0,65},{1,0},{32,33},{33,96},{64,1},{65,64},{96,97},{97,32},{2,67}... | collective-permute-start | bytes 4718600 | tf_op jit(solution)/shard_map/ppermute | solution.py:35
  68.5 36.5 %collective-permute-start.16 = (bf16[16,384,128]{2,1,0:T(8,128)(2,1)}, bf16[16,384,128]{2,1,0:T(8,128)(2,1)}, u32[]{:S(2)}, u32[]{:S(2)}) collective-permute-start(bf16[16,384,128]{2,1,0:T(8,128)(2,1)} %pad_maximum_fusion.rest_0_), channel_id=1, source_target_pairs={{0,1},{1,64},{32,97},{33,32},{64,65},{65,0},{96,33},{97,96},{2,3},... | collective-permute-start | bytes 4718600 | tf_op jit(solution)/shard_map/ppermute | solution.py:35
  83.0 22.3 %collective-permute-start.22 = (bf16[16,384,128]{2,1,0:T(8,128)(2,1)}, bf16[16,384,128]{2,1,0:T(8,128)(2,1)}, u32[]{:S(2)}, u32[]{:S(2)}) collective-permute-start(bf16[16,384,128]{2,1,0:T(8,128)(2,1)} %pad_maximum_fusion.1.rest_0_), channel_id=1, source_target_pairs={{0,32},{32,0},{1,33},{33,1},{2,34},{34,2},{3,35},{35,3},{4,36},{36... | collective-permute-start | bytes 4718600 | tf_op jit(solution)/shard_map/ppermute | solution.py:23
  105.0 23.6 %collective-permute-start.18 = (bf16[16,384,128]{2,1,0:T(8,128)(2,1)}, bf16[16,384,128]{2,1,0:T(8,128)(2,1)}, u32[]{:S(2)}, u32[]{:S(2)}) collective-permute-start(bf16[16,384,128]{2,1,0:T(8,128)(2,1)} %collective-permute-done.16.rest_0_), channel_id=1, source_target_pairs={{0,1},{1,64},{32,97},{33,32},{64,65},{65,0},{96,33},{97,96},{2,3},... | collective-permute-start | bytes 4718600 | tf_op jit(solution)/shard_map/ppermute | solution.py:35
  105.3 23.9 %collective-permute-start.27 = (bf16[16,384,128]{2,1,0:T(8,128)(2,1)}, bf16[16,384,128]{2,1,0:T(8,128)(2,1)}, u32[]{:S(2)}, u32[]{:S(2)}) collective-permute-start(bf16[16,384,128]{2,1,0:T(8,128)(2,1)} %collective-permute-done.20.rest_0_), channel_id=1, source_target_pairs={{0,2},{2,4},{4,6},{6,0},{32,38},{34,32},{36,34},{38,36},{1,3},{3,5... | collective-permute-start | bytes 4718600 | tf_op jit(solution)/shard_map/ppermute | solution.py:35
  109.0 20.8 %collective-permute-start.24 = (bf16[16,384,128]{2,1,0:T(8,128)(2,1)}, bf16[16,384,128]{2,1,0:T(8,128)(2,1)}, u32[]{:S(2)}, u32[]{:S(2)}) collective-permute-start(bf16[16,384,128]{2,1,0:T(8,128)(2,1)} %collective-permute-done.17.rest_1_), channel_id=1, source_target_pairs={{0,32},{32,0},{1,33},{33,1},{2,34},{34,2},{3,35},{35,3},{4,36},{36... | collective-permute-start | bytes 4718600 | tf_op jit(solution)/shard_map/ppermute | solution.py:23
  112.7 17.1 %collective-permute-start.23 = (bf16[16,384,128]{2,1,0:T(8,128)(2,1)}, bf16[16,384,128]{2,1,0:T(8,128)(2,1)}, u32[]{:S(2)}, u32[]{:S(2)}) collective-permute-start(bf16[16,384,128]{2,1,0:T(8,128)(2,1)} %collective-permute-done.16.rest_0_), channel_id=1, source_target_pairs={{0,32},{32,0},{1,33},{33,1},{2,34},{34,2},{3,35},{35,3},{4,36},{36... | collective-permute-start | bytes 4718600 | tf_op jit(solution)/shard_map/ppermute | solution.py:23
  128.6 14.2 %collective-permute-start.29 = (bf16[16,384,128]{2,1,0:T(8,128)(2,1)}, bf16[16,384,128]{2,1,0:T(8,128)(2,1)S(1)}, u32[]{:S(2)}, u32[]{:S(2)}) collective-permute-start(bf16[16,384,128]{2,1,0:T(8,128)(2,1)} %collective-permute-done.18.rest_1_), channel_id=1, source_target_pairs={{0,32},{32,0},{1,33},{33,1},{2,34},{34,2},{3,35},{35,3},{4,36},{36... | collective-permute-start | bytes 4718600 | tf_op jit(solution)/shard_map/ppermute | solution.py:23
  129.2 13.6 %collective-permute-start.28 = (bf16[16,384,128]{2,1,0:T(8,128)(2,1)}, bf16[16,384,128]{2,1,0:T(8,128)(2,1)S(1)}, u32[]{:S(2)}, u32[]{:S(2)}) collective-permute-start(bf16[16,384,128]{2,1,0:T(8,128)(2,1)} %pad_maximum_fusion.rest_0_), channel_id=1, source_target_pairs={{0,32},{32,0},{1,33},{33,1},{2,34},{34,2},{3,35},{35,3},{4,36},{36... | collective-permute-start | bytes 4718600 | tf_op jit(solution)/shard_map/ppermute | solution.py:23
  129.3 22.7 %collective-permute-start.31 = (bf16[16,384,128]{2,1,0:T(8,128)(2,1)}, bf16[16,384,128]{2,1,0:T(8,128)(2,1)S(1)}, u32[]{:S(2)}, u32[]{:S(2)}) collective-permute-start(bf16[16,384,128]{2,1,0:T(8,128)(2,1)} %collective-permute-done.27.rest_0_), channel_id=1, source_target_pairs={{0,32},{32,0},{1,33},{33,1},{2,34},{34,2},{3,35},{35,3},{4,36},{36... | collective-permute-start | bytes 4718600 | tf_op jit(solution)/shard_map/ppermute | solution.py:23
  129.8 12.9 %collective-permute-start.15 = (bf16[2,384,256]{2,1,0:T(8,128)(2,1)S(1)}, bf16[2,384,256]{2,1,0:T(8,128)(2,1)S(1)}, u32[]{:S(2)}, u32[]{:S(2)}) collective-permute-start(bf16[2,384,256]{2,1,0:T(8,128)(2,1)S(1)} %get-tuple-element.65), channel_id=1, source_target_pairs={{0,2},{2,4},{4,6},{6,0},{32,38},{34,32},{36,34},{38,36},{1,3},{3,5... | collective-permute-start | bytes 1179656 | tf_op jit(solution)/shard_map/ppermute | solution.py:35
  129.9 12.8 %collective-permute-start.25 = (bf16[2,384,256]{2,1,0:T(8,128)(2,1)S(1)}, bf16[2,384,256]{2,1,0:T(8,128)(2,1)S(1)}, u32[]{:S(2)}, u32[]{:S(2)}) collective-permute-start(bf16[2,384,256]{2,1,0:T(8,128)(2,1)S(1)} %get-tuple-element.84), channel_id=1, source_target_pairs={{0,6},{2,0},{4,2},{6,4},{32,34},{34,36},{36,38},{38,32},{1,7},{3,1... | collective-permute-start | bytes 1179656 | tf_op jit(solution)/shard_map/ppermute | solution.py:35
  (23 other events, 157.7 us)

commit v6 on v5

--- a/solution.py
+++ b/solution.py
@@ -272,7 +272,7 @@
     t3, t0 = terms((3, 0), tab, order, after(gu, evens[1], odds[1]), *blocks)
     evens.append(shift(after(evens[2], t3), "z", 1))
     odds.append(shift(after(odds[2], t3), "y", 1))
-    moving = add(after(ahead, evens[2], odds[2]), t3)
+    moving = add(after(ahead, evens[3], odds[3]), t3)
     even_0, odd_0 = lax.optimization_barrier((jnp.concatenate(evens), jnp.concatenate(odds), t0, moving))[:2]
     even_1, even_3 = shift(even_0, "y", 1), shift(even_0, "y", -1)
     odd_1, odd_3 = shift(odd_0, "z", 1), shift(odd_0, "z", -1)

time: 158 us -> 160 us (1.013)
  starting transfers between devices: 38.4 us -> 42.2 us
    ppermute x21, starting transfers between devices: 30.3 us -> 34.8 us  [shift(): return lax.ppermute(value, AXES[axis], pairs)]
    ppermute x21, waiting for transfers between devices: 38.3 us -> 35.1 us  [shift(): return lax.ppermute(value, AXES[axis], pairs)]
    ppermute x11, waiting for transfers between devices: 2.65 us -> 4.83 us  [shift(): return lax.ppermute(value, axis, [(0, 1), (1, 0)])]
  transfers between devices with their start and end apart: 32 -> 32, of which waited for: 11 -> 13; matrix products, arithmetic and copies ran while one was open for 8% -> 8% of each run, Pallas kernels for 33% -> 32%
where the time goes in v6:
time: 160 us; the launch traced here: 161 us
  Pallas kernels  52.4 us (33%)
  starting transfers between devices  42.2 us (26%)
  waiting for transfers between devices  40 us (25%)
  local copies, waits for them, and re-layouts  12.2 us (8%)
  other arithmetic  12.2 us (8%)
  between operations  1.74 us (1%)
    pallas_call x6, Pallas kernels, weight_grads(): pl.pallas_call(functools.partial(kinds_kernel, kinds, len(held)), out_sha...  36 us
    ppermute x21, waiting for transfers between devices, shift(): return lax.ppermute(value, AXES[axis], pairs)  35.1 us
    ppermute x21, starting transfers between devices, shift(): return lax.ppermute(value, AXES[axis], pairs)  34.8 us
    pallas_call x3, Pallas kernels, terms(): pl.pallas_call(functools.partial(chunk_kernel, chunks), out_shape=[PIECE]...  15.2 us
    unnamed x30, local copies, waits for them, and re-layouts  9.75 us
    ppermute x11, starting transfers between devices, shift(): return lax.ppermute(value, axis, [(0, 1), (1, 0)])  7.38 us
    ppermute x11, waiting for transfers between devices, shift(): return lax.ppermute(value, axis, [(0, 1), (1, 0)])  4.83 us
    convert_element_type x2, other arithmetic, sum_of(): return (a.astype(F32) + b.astype(F32) + c.astype(F32)).astype(BF)  3.68 us
  transfers between devices with their start and end apart: 32, of which 13 were waited for; matrix products, arithmetic and copies ran while one was open for 8% of the time, Pallas kernels for 32%

profile of v6, /device:TPU:0, one launch (start us, length us, event | category | flops | bytes accessed | tf_op | source)
XLA Modules:
  0.0 160.6 jit_solution(915907883111362618)
XLA Ops:
  7.5 2.7 %collective-permute-start.1 = (bf16[2,384,128]{2,1,0:T(8,128)(2,1)S(1)}, bf16[2,384,128]{2,1,0:T(8,128)(2,1)S(1)}, u32[]{:S(2)}, u32[]{:S(2)}) collective-permute-start(bf16[2,384,128]{2,1,0:T(8,128)(2,1)S(1)} %pad_maximum_fusion.5), channel_id=1, source_target_pairs={{0,16},{8,24},{16,0},{24,8},{32,48},{40,56},{48,32},{56,40},{1,17}... | collective-permute-start | bytes 589832 | tf_op jit(solution)/shard_map/ppermute | solution.py:35
  11.6 3.2 %collective-permute-start.4 = (bf16[1024,384]{1,0:T(8,128)(2,1)S(1)}, bf16[1024,384]{1,0:T(8,128)(2,1)S(1)}, u32[]{:S(2)}, u32[]{:S(2)}) collective-permute-start(bf16[1024,384]{1,0:T(8,128)(2,1)S(1)} %get-tuple-element.51), channel_id=1, source_target_pairs={{0,64},{64,0},{1,65},{65,1},{2,66},{66,2},{3,67},{67,3},{4,68},{68... | collective-permute-start | bytes 2359304 | tf_op jit(solution)/shard_map/ppermute | solution.py:23
  18.1 2.2 %copy-done.2 = bf16[128,128,128]{2,1,0:T(8,128)(2,1)S(1)} copy-done((bf16[128,128,128]{2,1,0:T(8,128)(2,1)S(1)}, bf16[128,128,128]{2,1,0:T(8,128)(2,1)}, u32[]{:S(2)}) %copy-start.2) | copy-done | bytes 4194328
  20.3 3.6 %terms.3 = bf16[8,384,256]{2,1,0:T(8,128)(2,1)S(1)} custom-call(s32[256]{0:T(256)S(1)} %select_reduce_fusion.tab, s32[32]{0:T(128)S(1)} %mul.262.order, bf16[384,1024]{1,0:T(8,128)(2,1)S(1)} %get-tuple-element.55.gu, bf16[128,128,128]{2,1,0:T(8,128)(2,1)S(1)} %copy-done, bf16[128,128,128]{2,1,0:T(8,128)(2,1)S(1)} %copy-done.2), custom_call_target="tpu_custom_call" | custom-call | flops 1 | bytes 1 | tf_op jit(solution)/shard_map/terms/pallas_call | solution.py:98
  27.7 2.6 %collective-permute-done.4 = bf16[1024,384]{1,0:T(8,128)(2,1)S(1)} collective-permute-done((bf16[1024,384]{1,0:T(8,128)(2,1)S(1)}, bf16[1024,384]{1,0:T(8,128)(2,1)S(1)}, u32[]{:S(2)}, u32[]{:S(2)}) %collective-permute-start.4) | collective-permute-done | bytes 786464 | tf_op jit(solution)/shard_map/ppermute | solution.py:23
  31.9 4.8 %terms.5 = bf16[8,384,256]{2,1,0:T(8,128)(2,1)} custom-call(s32[256]{0:T(256)S(1)} %select_reduce_fusion.tab, s32[32]{0:T(128)S(1)} %mul.262.order, bf16[384,1024]{1,0:T(8,128)(2,1)S(1)} %get-tuple-element.55.gu, bf16[128,128,128]{2,1,0:T(8,128)(2,1)S(1)} %copy-done.1, bf16[128,128,128]{2,1,0:T(8,128)(2,1)S(1)} %copy-done.2), custom_call_target="tpu_custom_call" | custom-call | flops 1 | bytes 1 | tf_op jit(solution)/shard_map/terms/pallas_call | solution.py:98
  40.2 6.7 %terms.4 = (bf16[8,384,256]{2,1,0:T(8,128)(2,1)S(1)}, bf16[8,384,256]{2,1,0:T(8,128)(2,1)S(1)}) custom-call(s32[256]{0:T(256)S(1)} %select_reduce_fusion.tab, s32[32]{0:T(128)S(1)} %mul.262.order, bf16[384,1024]{1,0:T(8,128)(2,1)S(1)} %get-tuple-element.55.gu, bf16[128,128,128]{2,1,0:T(8,128)(2,1)S(1)} %copy-done.1, bf16[128,128,128]{2,1,0:T(8,128)(2,1)S(1)} %copy-done.2), custom_call_target="tpu_custom_call" | custom-call | flops 1 | bytes 1 | tf_op jit(solution)/shard_map/terms/pallas_call | solution.py:98
  52.6 4.0 %collective-permute-done.8 = bf16[4,384,128]{2,1,0:T(8,128)(2,1)S(1)} collective-permute-done((bf16[4,384,128]{2,1,0:T(8,128)(2,1)S(1)}, bf16[4,384,128]{2,1,0:T(8,128)(2,1)S(1)}, u32[]{:S(2)}, u32[]{:S(2)}) %collective-permute-start.8) | collective-permute-done | bytes 393248 | tf_op jit(solution)/shard_map/ppermute | solution.py:35
  64.1 3.4 %collective-permute-start.13 = (bf16[16,384,128]{2,1,0:T(8,128)(2,1)}, bf16[16,384,128]{2,1,0:T(8,128)(2,1)}, u32[]{:S(2)}, u32[]{:S(2)}) collective-permute-start(bf16[16,384,128]{2,1,0:T(8,128)(2,1)} %pad_maximum_fusion.1.rest_0_), channel_id=1, source_target_pairs={{0,6},{2,0},{4,2},{6,4},{32,34},{34,36},{36,38},{38,32},{1,7},{3,1... | collective-permute-start | bytes 4718600 | tf_op jit(solution)/shard_map/ppermute | solution.py:35
  69.2 13.1 %collective-permute-done.12 = bf16[8,384,256]{2,1,0:T(8,128)(2,1)} collective-permute-done((bf16[8,384,256]{2,1,0:T(8,128)(2,1)}, bf16[8,384,256]{2,1,0:T(8,128)(2,1)}, u32[]{:S(2)}, u32[]{:S(2)}) %collective-permute-start.12) | collective-permute-done | bytes 1572896 | tf_op jit(solution)/shard_map/ppermute | solution.py:35
  82.4 2.6 %collective-permute-start.16 = (bf16[16,384,128]{2,1,0:T(8,128)(2,1)}, bf16[16,384,128]{2,1,0:T(8,128)(2,1)}, u32[]{:S(2)}, u32[]{:S(2)}) collective-permute-start(bf16[16,384,128]{2,1,0:T(8,128)(2,1)} %pad_maximum_fusion.rest_0_), channel_id=1, source_target_pairs={{0,1},{1,64},{32,97},{33,32},{64,65},{65,0},{96,33},{97,96},{2,3},... | collective-permute-start | bytes 4718600 | tf_op jit(solution)/shard_map/ppermute | solution.py:35
  85.0 3.1 %collective-permute-done.11 = bf16[8,384,256]{2,1,0:T(8,128)(2,1)} collective-permute-done((bf16[8,384,256]{2,1,0:T(8,128)(2,1)}, bf16[8,384,256]{2,1,0:T(8,128)(2,1)}, u32[]{:S(2)}, u32[]{:S(2)}) %collective-permute-start.11) | collective-permute-done | bytes 1572896 | tf_op jit(solution)/shard_map/ppermute | solution.py:35
  88.0 3.6 %add_convert_fusion = bf16[8,384,256]{2,1,0:T(8,128)(2,1)} fusion(bf16[8,384,256]{2,1,0:T(8,128)(2,1)} %collective-permute-done.12, bf16[8,384,256]{2,1,0:T(8,128)(2,1)} %collective-permute-done.11, bf16[8,384,256]{2,1,0:T(8,128)(2,1)S(1)} %get-tuple-element.56), kind=kLoop, calls=%fused_computation | loop fusion | flops 4718592 | bytes 6291456 | tf_op jit(solution)/shard_map/convert_element_type | solution.py:43
  92.7 8.7 %collective-permute-done.13.rest_0_ = bf16[16,384,128]{2,1,0:T(8,128)(2,1)} collective-permute-done((bf16[16,384,128]{2,1,0:T(8,128)(2,1)}, bf16[16,384,128]{2,1,0:T(8,128)(2,1)}, u32[]{:S(2)}, u32[]{:S(2)}) %collective-permute-start.13) | collective-permute-done | bytes 1572896 | tf_op jit(solution)/shard_map/ppermute | solution.py:35
  103.2 3.2 %collective-permute-done.16.rest_0_ = bf16[16,384,128]{2,1,0:T(8,128)(2,1)} collective-permute-done((bf16[16,384,128]{2,1,0:T(8,128)(2,1)}, bf16[16,384,128]{2,1,0:T(8,128)(2,1)}, u32[]{:S(2)}, u32[]{:S(2)}) %collective-permute-start.16) | collective-permute-done | bytes 1572896 | tf_op jit(solution)/shard_map/ppermute | solution.py:35
  106.8 2.9 %collective-permute-start.27 = (bf16[16,384,128]{2,1,0:T(8,128)(2,1)}, bf16[16,384,128]{2,1,0:T(8,128)(2,1)}, u32[]{:S(2)}, u32[]{:S(2)}) collective-permute-start(bf16[16,384,128]{2,1,0:T(8,128)(2,1)} %collective-permute-done.20.rest_0_), channel_id=1, source_target_pairs={{0,2},{2,4},{4,6},{6,0},{32,38},{34,32},{36,34},{38,36},{1,3},{3,5... | collective-permute-start | bytes 4718600 | tf_op jit(solution)/shard_map/ppermute | solution.py:35
  113.9 5.1 %grads_0.1 = (bf16[128,128,128]{2,1,0:T(8,128)(2,1)}, bf16[128,128,128]{2,1,0:T(8,128)(2,1)}) custom-call(s32[164]{0:T(256)S(1)} %get-tuple-element.101.lrow, s32[164]{0:T(256)S(1)} %get-tuple-element.100.lslot, s32[656]{0:T(1024)S(1)} %reshape.625.ltile, s32[16]{0:T(128)S(1)} %pad_add_fusion.1.meta, bf16[2,1024,384]{2,1,0:T(8,128)(2,1)S(1)} %pad_maximum_fusion.2.gt, ...), custom_call_target="tpu_custom_call" | custom-call | flops 1 | bytes 1 | tf_op jit(solution)/shard_map/grads_0/pallas_call | solution.py:166
  119.0 4.6 %grads_1.1 = (bf16[128,128,128]{2,1,0:T(8,128)(2,1)}, bf16[128,128,128]{2,1,0:T(8,128)(2,1)}) custom-call(s32[164]{0:T(256)S(1)} %get-tuple-element.101.lrow, s32[164]{0:T(256)S(1)} %get-tuple-element.100.lslot, s32[656]{0:T(1024)S(1)} %reshape.625.ltile, s32[16]{0:T(128)S(1)} %pad_add_fusion.1.meta, ...), custom_call_target="tpu_custom_call", output_to_operand_aliasing={{0}: (8, {}), {1}: (9, {})} | custom-call | flops 1 | bytes 1 | tf_op jit(solution)/shard_map/grads_1/pallas_call | solution.py:166
  123.6 4.6 %grads_2.1 = (bf16[128,128,128]{2,1,0:T(8,128)(2,1)}, bf16[128,128,128]{2,1,0:T(8,128)(2,1)}) custom-call(s32[164]{0:T(256)S(1)} %get-tuple-element.101.lrow, s32[164]{0:T(256)S(1)} %get-tuple-element.100.lslot, s32[656]{0:T(1024)S(1)} %reshape.625.ltile, s32[16]{0:T(128)S(1)} %pad_add_fusion.1.meta, ...), custom_call_target="tpu_custom_call", output_to_operand_aliasing={{0}: (8, {}), {1}: (9, {})} | custom-call | flops 1 | bytes 1 | tf_op jit(solution)/shard_map/grads_2/pallas_call | solution.py:166
  129.4 2.2 %collective-permute-start.15 = (bf16[2,384,256]{2,1,0:T(8,128)(2,1)S(1)}, bf16[2,384,256]{2,1,0:T(8,128)(2,1)S(1)}, u32[]{:S(2)}, u32[]{:S(2)}) collective-permute-start(bf16[2,384,256]{2,1,0:T(8,128)(2,1)S(1)} %get-tuple-element.65), channel_id=1, source_target_pairs={{0,2},{2,4},{4,6},{6,0},{32,38},{34,32},{36,34},{38,36},{1,3},{3,5... | collective-permute-start | bytes 1179656 | tf_op jit(solution)/shard_map/ppermute | solution.py:35
  132.7 8.9 %grads_3.1 = (bf16[128,128,128]{2,1,0:T(8,128)(2,1)}, bf16[128,128,128]{2,1,0:T(8,128)(2,1)}) custom-call(s32[164]{0:T(256)S(1)} %get-tuple-element.101.lrow, s32[164]{0:T(256)S(1)} %get-tuple-element.100.lslot, s32[656]{0:T(1024)S(1)} %reshape.625.ltile, s32[16]{0:T(128)S(1)} %pad_add_fusion.1.meta, ...), custom_call_target="tpu_custom_call", output_to_operand_aliasing={{0}: (10, {}), {1}: (11, {})} | custom-call | flops 1 | bytes 1 | tf_op jit(solution)/shard_map/grads_3/pallas_call | solution.py:166
  141.8 2.2 %collective-permute-start.26 = (bf16[2,384,256]{2,1,0:T(8,128)(2,1)S(1)}, bf16[2,384,256]{2,1,0:T(8,128)(2,1)S(1)}, u32[]{:S(2)}, u32[]{:S(2)}) collective-permute-start(bf16[2,384,256]{2,1,0:T(8,128)(2,1)S(1)} %add_convert_fusion.2), channel_id=1, source_target_pairs={{0,2},{2,4},{4,6},{6,0},{32,38},{34,32},{36,34},{38,36},{1,3},{3,5... | collective-permute-start | bytes 1179656 | tf_op jit(solution)/shard_map/ppermute | solution.py:35
  144.0 7.9 %grads_4.1 = (bf16[128,128,128]{2,1,0:T(8,128)(2,1)}, bf16[128,128,128]{2,1,0:T(8,128)(2,1)}) custom-call(s32[164]{0:T(256)S(1)} %get-tuple-element.101.lrow, s32[164]{0:T(256)S(1)} %get-tuple-element.100.lslot, s32[656]{0:T(1024)S(1)} %reshape.625.ltile, s32[16]{0:T(128)S(1)} %pad_add_fusion.1.meta, ...), custom_call_target="tpu_custom_call", output_to_operand_aliasing={{0}: (10, {}), {1}: (11, {})} | custom-call | flops 1 | bytes 1 | tf_op jit(solution)/shard_map/grads_4/pallas_call | solution.py:166
  152.6 5.0 %grads_5.1 = (bf16[128,128,128]{2,1,0:T(8,128)(2,1)}, bf16[128,128,128]{2,1,0:T(8,128)(2,1)}) custom-call(s32[164]{0:T(256)S(1)} %get-tuple-element.101.lrow, s32[164]{0:T(256)S(1)} %get-tuple-element.100.lslot, s32[656]{0:T(1024)S(1)} %reshape.625.ltile, s32[16]{0:T(128)S(1)} %pad_add_fusion.1.meta, ...), custom_call_target="tpu_custom_call", output_to_operand_aliasing={{0}: (8, {}), {1}: (9, {})} | custom-call | flops 1 | bytes 1 | tf_op jit(solution)/shard_map/grads_5/pallas_call | solution.py:166
  (128 shorter events, 47.9 us)
Async XLA Ops:
  5.8 18.8 %collective-permute-start = (bf16[2,384,128]{2,1,0:T(8,128)(2,1)S(1)}, bf16[2,384,128]{2,1,0:T(8,128)(2,1)}, u32[]{:S(2)}, u32[]{:S(2)}) collective-permute-start(bf16[2,384,128]{2,1,0:T(8,128)(2,1)S(1)} %pad_maximum_fusion.5), channel_id=1, source_target_pairs={{0,8},{8,16},{16,24},{24,0},{32,56},{40,32},{48,40},{56,48},{1,9},... | collective-permute-start | bytes 589832 | tf_op jit(solution)/shard_map/ppermute | solution.py:35
  7.5 18.1 %collective-permute-start.1 = (bf16[2,384,128]{2,1,0:T(8,128)(2,1)S(1)}, bf16[2,384,128]{2,1,0:T(8,128)(2,1)S(1)}, u32[]{:S(2)}, u32[]{:S(2)}) collective-permute-start(bf16[2,384,128]{2,1,0:T(8,128)(2,1)S(1)} %pad_maximum_fusion.5), channel_id=1, source_target_pairs={{0,16},{8,24},{16,0},{24,8},{32,48},{40,56},{48,32},{56,40},{1,17}... | collective-permute-start | bytes 589832 | tf_op jit(solution)/shard_map/ppermute | solution.py:35
  10.2 15.4 %collective-permute-start.2 = (bf16[2,384,128]{2,1,0:T(8,128)(2,1)S(1)}, bf16[2,384,128]{2,1,0:T(8,128)(2,1)S(1)}, u32[]{:S(2)}, u32[]{:S(2)}) collective-permute-start(bf16[2,384,128]{2,1,0:T(8,128)(2,1)S(1)} %pad_maximum_fusion.5), channel_id=1, source_target_pairs={{0,24},{8,0},{16,8},{24,16},{32,40},{40,48},{48,56},{56,32},{1,25}... | collective-permute-start | bytes 589832 | tf_op jit(solution)/shard_map/ppermute | solution.py:35
  11.6 18.7 %collective-permute-start.4 = (bf16[1024,384]{1,0:T(8,128)(2,1)S(1)}, bf16[1024,384]{1,0:T(8,128)(2,1)S(1)}, u32[]{:S(2)}, u32[]{:S(2)}) collective-permute-start(bf16[1024,384]{1,0:T(8,128)(2,1)S(1)} %get-tuple-element.51), channel_id=1, source_target_pairs={{0,64},{64,0},{1,65},{65,1},{2,66},{66,2},{3,67},{67,3},{4,68},{68... | collective-permute-start | bytes 2359304 | tf_op jit(solution)/shard_map/ppermute | solution.py:23
  23.9 32.6 %collective-permute-start.6 = (bf16[8,384,256]{2,1,0:T(8,128)(2,1)S(1)}, bf16[8,384,256]{2,1,0:T(8,128)(2,1)S(1)}, u32[]{:S(2)}, u32[]{:S(2)}) collective-permute-start(bf16[8,384,256]{2,1,0:T(8,128)(2,1)S(1)} %terms.3), channel_id=1, source_target_pairs={{0,8},{8,16},{16,24},{24,0},{32,56},{40,32},{48,40},{56,48},{1,9},... | collective-permute-start | bytes 4718600 | tf_op jit(solution)/shard_map/ppermute | solution.py:35
  25.7 11.1 %collective-permute-start.3 = (bf16[4,384,128]{2,1,0:T(8,128)(2,1)S(1)}, bf16[4,384,128]{2,1,0:T(8,128)(2,1)S(1)}, u32[]{:S(2)}, u32[]{:S(2)}) collective-permute-start(bf16[4,384,128]{2,1,0:T(8,128)(2,1)S(1)} %pad_maximum_fusion.3), channel_id=1, source_target_pairs={{0,2},{2,4},{4,6},{6,0},{32,38},{34,32},{36,34},{38,36},{1,3},{3,5... | collective-permute-start | bytes 1179656 | tf_op jit(solution)/shard_map/ppermute | solution.py:35
  36.7 10.2 %collective-permute-start.7 = (bf16[4,384,128]{2,1,0:T(8,128)(2,1)S(1)}, bf16[4,384,128]{2,1,0:T(8,128)(2,1)S(1)}, u32[]{:S(2)}, u32[]{:S(2)}) collective-permute-start(bf16[4,384,128]{2,1,0:T(8,128)(2,1)S(1)} %collective-permute-done.3), channel_id=1, source_target_pairs={{0,2},{2,4},{4,6},{6,0},{32,38},{34,32},{36,34},{38,36},{1,3},{3,5... | collective-permute-start | bytes 1179656 | tf_op jit(solution)/shard_map/ppermute | solution.py:35
  51.1 31.3 %collective-permute-start.12 = (bf16[8,384,256]{2,1,0:T(8,128)(2,1)}, bf16[8,384,256]{2,1,0:T(8,128)(2,1)}, u32[]{:S(2)}, u32[]{:S(2)}) collective-permute-start(bf16[8,384,256]{2,1,0:T(8,128)(2,1)} %terms.5), channel_id=1, source_target_pairs={{0,24},{8,0},{16,8},{24,16},{32,40},{40,48},{48,56},{56,32},{1,25}... | collective-permute-start | bytes 4718600 | tf_op jit(solution)/shard_map/ppermute | solution.py:35
  59.5 28.5 %collective-permute-start.11 = (bf16[8,384,256]{2,1,0:T(8,128)(2,1)}, bf16[8,384,256]{2,1,0:T(8,128)(2,1)}, u32[]{:S(2)}, u32[]{:S(2)}) collective-permute-start(bf16[8,384,256]{2,1,0:T(8,128)(2,1)} %add_convert_fusion.1), channel_id=1, source_target_pairs={{0,8},{8,16},{16,24},{24,0},{32,56},{40,32},{48,40},{56,48},{1,9},... | collective-permute-start | bytes 4718600 | tf_op jit(solution)/shard_map/ppermute | solution.py:35
  64.1 37.3 %collective-permute-start.13 = (bf16[16,384,128]{2,1,0:T(8,128)(2,1)}, bf16[16,384,128]{2,1,0:T(8,128)(2,1)}, u32[]{:S(2)}, u32[]{:S(2)}) collective-permute-start(bf16[16,384,128]{2,1,0:T(8,128)(2,1)} %pad_maximum_fusion.1.rest_0_), channel_id=1, source_target_pairs={{0,6},{2,0},{4,2},{6,4},{32,34},{34,36},{36,38},{38,32},{1,7},{3,1... | collective-permute-start | bytes 4718600 | tf_op jit(solution)/shard_map/ppermute | solution.py:35
  67.6 34.6 %collective-permute-start.20 = (bf16[16,384,128]{2,1,0:T(8,128)(2,1)}, bf16[16,384,128]{2,1,0:T(8,128)(2,1)}, u32[]{:S(2)}, u32[]{:S(2)}) collective-permute-start(bf16[16,384,128]{2,1,0:T(8,128)(2,1)} %pad_maximum_fusion.1.rest_0_), channel_id=1, source_target_pairs={{0,2},{2,4},{4,6},{6,0},{32,38},{34,32},{36,34},{38,36},{1,3},{3,5... | collective-permute-start | bytes 4718600 | tf_op jit(solution)/shard_map/ppermute | solution.py:35
  69.1 33.5 %collective-permute-start.17 = (bf16[16,384,128]{2,1,0:T(8,128)(2,1)}, bf16[16,384,128]{2,1,0:T(8,128)(2,1)}, u32[]{:S(2)}, u32[]{:S(2)}) collective-permute-start(bf16[16,384,128]{2,1,0:T(8,128)(2,1)} %pad_maximum_fusion.rest_0_), channel_id=1, source_target_pairs={{0,65},{1,0},{32,33},{33,96},{64,1},{65,64},{96,97},{97,32},{2,67}... | collective-permute-start | bytes 4718600 | tf_op jit(solution)/shard_map/ppermute | solution.py:35
  82.4 24.1 %collective-permute-start.16 = (bf16[16,384,128]{2,1,0:T(8,128)(2,1)}, bf16[16,384,128]{2,1,0:T(8,128)(2,1)}, u32[]{:S(2)}, u32[]{:S(2)}) collective-permute-start(bf16[16,384,128]{2,1,0:T(8,128)(2,1)} %pad_maximum_fusion.rest_0_), channel_id=1, source_target_pairs={{0,1},{1,64},{32,97},{33,32},{64,65},{65,0},{96,33},{97,96},{2,3},... | collective-permute-start | bytes 4718600 | tf_op jit(solution)/shard_map/ppermute | solution.py:35
  91.6 15.1 %collective-permute-start.22 = (bf16[16,384,128]{2,1,0:T(8,128)(2,1)}, bf16[16,384,128]{2,1,0:T(8,128)(2,1)}, u32[]{:S(2)}, u32[]{:S(2)}) collective-permute-start(bf16[16,384,128]{2,1,0:T(8,128)(2,1)} %pad_maximum_fusion.1.rest_0_), channel_id=1, source_target_pairs={{0,32},{32,0},{1,33},{33,1},{2,34},{34,2},{3,35},{35,3},{4,36},{36... | collective-permute-start | bytes 4718600 | tf_op jit(solution)/shard_map/ppermute | solution.py:23
  102.7 11.2 %collective-permute-start.19 = (bf16[2,1024,384]{2,1,0:T(8,128)(2,1)S(1)}, bf16[2,1024,384]{2,1,0:T(8,128)(2,1)S(1)}, u32[]{:S(2)}, u32[]{:S(2)}) collective-permute-start(bf16[2,1024,384]{2,1,0:T(8,128)(2,1)S(1)} %pad_maximum_fusion.2.gt), channel_id=1, source_target_pairs={{0,32},{32,0},{1,33},{33,1},{2,34},{34,2},{3,35},{35,3},{4,36},{36... | collective-permute-start | bytes 4718600 | tf_op jit(solution)/shard_map/ppermute | solution.py:23
  106.4 21.9 %collective-permute-start.18 = (bf16[16,384,128]{2,1,0:T(8,128)(2,1)}, bf16[16,384,128]{2,1,0:T(8,128)(2,1)}, u32[]{:S(2)}, u32[]{:S(2)}) collective-permute-start(bf16[16,384,128]{2,1,0:T(8,128)(2,1)} %collective-permute-done.16.rest_0_), channel_id=1, source_target_pairs={{0,1},{1,64},{32,97},{33,32},{64,65},{65,0},{96,33},{97,96},{2,3},... | collective-permute-start | bytes 4718600 | tf_op jit(solution)/shard_map/ppermute | solution.py:35
  106.8 22.2 %collective-permute-start.27 = (bf16[16,384,128]{2,1,0:T(8,128)(2,1)}, bf16[16,384,128]{2,1,0:T(8,128)(2,1)}, u32[]{:S(2)}, u32[]{:S(2)}) collective-permute-start(bf16[16,384,128]{2,1,0:T(8,128)(2,1)} %collective-permute-done.20.rest_0_), channel_id=1, source_target_pairs={{0,2},{2,4},{4,6},{6,0},{32,38},{34,32},{36,34},{38,36},{1,3},{3,5... | collective-permute-start | bytes 4718600 | tf_op jit(solution)/shard_map/ppermute | solution.py:35
  112.1 17.3 %collective-permute-start.24 = (bf16[16,384,128]{2,1,0:T(8,128)(2,1)}, bf16[16,384,128]{2,1,0:T(8,128)(2,1)}, u32[]{:S(2)}, u32[]{:S(2)}) collective-permute-start(bf16[16,384,128]{2,1,0:T(8,128)(2,1)} %collective-permute-done.17.rest_1_), channel_id=1, source_target_pairs={{0,32},{32,0},{1,33},{33,1},{2,34},{34,2},{3,35},{35,3},{4,36},{36... | collective-permute-start | bytes 4718600 | tf_op jit(solution)/shard_map/ppermute | solution.py:23
  113.5 18.1 %collective-permute-start.23 = (bf16[16,384,128]{2,1,0:T(8,128)(2,1)}, bf16[16,384,128]{2,1,0:T(8,128)(2,1)}, u32[]{:S(2)}, u32[]{:S(2)}) collective-permute-start(bf16[16,384,128]{2,1,0:T(8,128)(2,1)} %collective-permute-done.16.rest_0_), channel_id=1, source_target_pairs={{0,32},{32,0},{1,33},{33,1},{2,34},{34,2},{3,35},{35,3},{4,36},{36... | collective-permute-start | bytes 4718600 | tf_op jit(solution)/shard_map/ppermute | solution.py:23
  128.4 15.6 %collective-permute-start.29 = (bf16[16,384,128]{2,1,0:T(8,128)(2,1)}, bf16[16,384,128]{2,1,0:T(8,128)(2,1)S(1)}, u32[]{:S(2)}, u32[]{:S(2)}) collective-permute-start(bf16[16,384,128]{2,1,0:T(8,128)(2,1)} %collective-permute-done.18.rest_1_), channel_id=1, source_target_pairs={{0,32},{32,0},{1,33},{33,1},{2,34},{34,2},{3,35},{35,3},{4,36},{36... | collective-permute-start | bytes 4718600 | tf_op jit(solution)/shard_map/ppermute | solution.py:23
  128.8 15.2 %collective-permute-start.28 = (bf16[16,384,128]{2,1,0:T(8,128)(2,1)}, bf16[16,384,128]{2,1,0:T(8,128)(2,1)S(1)}, u32[]{:S(2)}, u32[]{:S(2)}) collective-permute-start(bf16[16,384,128]{2,1,0:T(8,128)(2,1)} %pad_maximum_fusion.rest_0_), channel_id=1, source_target_pairs={{0,32},{32,0},{1,33},{33,1},{2,34},{34,2},{3,35},{35,3},{4,36},{36... | collective-permute-start | bytes 4718600 | tf_op jit(solution)/shard_map/ppermute | solution.py:23
  128.9 23.7 %collective-permute-start.31 = (bf16[16,384,128]{2,1,0:T(8,128)(2,1)}, bf16[16,384,128]{2,1,0:T(8,128)(2,1)S(1)}, u32[]{:S(2)}, u32[]{:S(2)}) collective-permute-start(bf16[16,384,128]{2,1,0:T(8,128)(2,1)} %collective-permute-done.27.rest_0_), channel_id=1, source_target_pairs={{0,32},{32,0},{1,33},{33,1},{2,34},{34,2},{3,35},{35,3},{4,36},{36... | collective-permute-start | bytes 4718600 | tf_op jit(solution)/shard_map/ppermute | solution.py:23
  129.4 12.3 %collective-permute-start.15 = (bf16[2,384,256]{2,1,0:T(8,128)(2,1)S(1)}, bf16[2,384,256]{2,1,0:T(8,128)(2,1)S(1)}, u32[]{:S(2)}, u32[]{:S(2)}) collective-permute-start(bf16[2,384,256]{2,1,0:T(8,128)(2,1)S(1)} %get-tuple-element.65), channel_id=1, source_target_pairs={{0,2},{2,4},{4,6},{6,0},{32,38},{34,32},{36,34},{38,36},{1,3},{3,5... | collective-permute-start | bytes 1179656 | tf_op jit(solution)/shard_map/ppermute | solution.py:35
  131.6 10.1 %collective-permute-start.25 = (bf16[2,384,256]{2,1,0:T(8,128)(2,1)S(1)}, bf16[2,384,256]{2,1,0:T(8,128)(2,1)S(1)}, u32[]{:S(2)}, u32[]{:S(2)}) collective-permute-start(bf16[2,384,256]{2,1,0:T(8,128)(2,1)S(1)} %get-tuple-element.84), channel_id=1, source_target_pairs={{0,6},{2,0},{4,2},{6,4},{32,34},{34,36},{36,38},{38,32},{1,7},{3,1... | collective-permute-start | bytes 1179656 | tf_op jit(solution)/shard_map/ppermute | solution.py:35
  (23 other events, 163.6 us)
